TPU v7x, 32 devices: a whole 2x2x4 slice. The times are simulated.
32 devices in a mesh: grp: 2 (over y), ctx: 8 (over z, x), head: 1, sub: 2 (over core).
Axes of the slice: x: 2, y: 2, z: 4, core: 2. Of those that a mesh axis runs over, the one named last changes fastest.
Arguments:
- queries: bfloat16 [32, 384, 2048], P(('grp', 'ctx', 'sub'), None, 'head'), parts along dimension 0, may hold values from -6 to 6
- keys: bfloat16 [32, 384, 2048], P(('grp', 'ctx', 'sub'), None, 'head'), parts along dimension 0, may hold values from -6 to 6
- values: bfloat16 [32, 384, 2048], P(('grp', 'ctx', 'sub'), None, 'head'), parts along dimension 0, may hold values from -6 to 6
- grad_out: bfloat16 [32, 384, 2048], P(('grp', 'ctx', 'sub'), None, 'head'), parts along dimension 0, may hold values from -6 to 6
- window_tiles: int32 [32, 6], P(('grp', 'ctx', 'sub')), parts along dimension 0, may hold values from 0 to 15, as said below
- window_count: int32 [32], P(('grp', 'ctx', 'sub')), parts along dimension 0, may hold values from 1 to 6
Outputs:
- attended: bfloat16 [32, 384, 2048], P(('grp', 'ctx', 'sub'), None, 'head'), parts along dimension 0
- grad_queries: bfloat16 [32, 384, 2048], P(('grp', 'ctx', 'sub'), None, 'head'), parts along dimension 0
- grad_keys: bfloat16 [32, 384, 2048], P(('grp', 'ctx', 'sub'), None, 'head'), parts along dimension 0
- grad_values: bfloat16 [32, 384, 2048], P(('grp', 'ctx', 'sub'), None, 'head'), parts along dimension 0
There are 2 independent parts, one for each index of `grp`. A program takes and returns all parts, laid end to end along the dimension named above; each array names one. Nothing has to cross between parts.
Inputs may be any that keep to these rules, and one draw needn't show every extreme that they name: `window_tiles`: tile i lies in tile column i // 16, time slab (i // 2) % 8 and tile row i % 2. The first window_count[i] entries of row i are distinct tiles whose column, slab and row each differ from tile i's by at most 1, tile i among them; the other entries equal i. Tile j is a live entry of tile i's list exactly when tile i is a live entry of tile j's list.
All inputs are finite; a program needn't handle non-finite values.
Results may differ from a plain program's by a relative error of at most 0.022.
Values may be sent and summed in bfloat16 or wider, within the bound.
No kernel may reach another device: no remote copies, remote signals or barrier semaphores. Data moves between devices by JAX's collectives and lax.ppermute only.
A program may use at most 256 MiB of HBM per device.

v0:
```python
import functools
import math

import jax
import jax.numpy as jnp
from jax import lax
from jax.experimental import pallas as pl
from jax.experimental.pallas import tpu as pltpu
from jax.sharding import PartitionSpec as P

HD = 128
FLAG_ROWS = 16
BLOCKS = 4
RING = ("ctx", "sub")
F32 = jnp.float32
BF16 = jnp.bfloat16
SCALE = 1.0 / math.sqrt(HD)
FACTOR = SCALE * math.log2(math.e)
ANY = pl.BlockSpec(memory_space=pl.ANY)
SMEM = pl.BlockSpec(memory_space=pltpu.SMEM)
PARAMS = pltpu.CompilerParams(vmem_limit_bytes=36 * 1024 * 1024)
LIGHT = pltpu.CompilerParams(vmem_limit_bytes=20 * 1024 * 1024)


def struct(shape, dtype):
    return jax.ShapeDtypeStruct(shape, dtype)


def hbm(values):
    return [pltpu.with_memory_space_constraint(value, pltpu.HBM) for value in values]


def moved(nbytes):
    return pl.CostEstimate(flops=0, bytes_accessed=nbytes, transcendentals=0)


def pack_kernel(jobs, step, first, places_ref, flags_ref, *refs):
    sources, outs = refs[:4], refs[-len(jobs) :]
    lane = lax.broadcasted_iota(jnp.int32, (FLAG_ROWS, HD), 1)
    flags = jnp.zeros((FLAG_ROWS, HD), F32)
    for w in range(flags_ref.shape[0]):
        flags = jnp.where(lane == w, flags_ref[w].astype(F32), flags)
    flags = flags.astype(BF16)
    team = places_ref.shape[0]
    for out, (d, heads, kinds, flagged) in zip(outs, jobs):
        for m, c in enumerate(heads):
            lanes = pl.ds(pl.multiple_of(((c - first) * team + places_ref[d]) * HD, HD), HD)
            for at, n in enumerate(kinds):
                out[m, 0, pl.ds(at * step, step)] = sources[n][0, :, lanes]
            if flagged:
                out[m, 0, pl.ds(len(kinds) * step, FLAG_ROWS)] = flags


def pack(jobs, heads, places, flags, sources, spare, kept=jax.ShapeDtypeStruct):
    _, tile, lane_width = sources[0].shape
    step = tile // BLOCKS
    team = places.shape[0]
    first = heads[0]
    count = len(heads)
    wide = count * team * HD if first % count == 0 else lane_width
    block = first // count if first % count == 0 else 0
    start = first if first % count == 0 else 0
    shapes = [
        (len(held), BLOCKS, len(kinds) * step + (FLAG_ROWS if flagged else 0), HD)
        for _, held, kinds, flagged in jobs
    ]
    return pl.pallas_call(
        functools.partial(pack_kernel, jobs, step, start),
        grid=(BLOCKS,),
        out_shape=[kept(shape, BF16) for shape in shapes],
        in_specs=[SMEM, SMEM]
        + [pl.BlockSpec((1, step, wide), lambda i: (0, i, block))] * 4
        + [ANY] * len(spare),
        out_specs=[
            pl.BlockSpec((shape[0], 1, shape[2], HD), lambda i: (0, i, 0, 0)) for shape in shapes
        ],
        cost_estimate=moved(sum(4 * HD * math.prod(shape[:3]) for shape in shapes)),
        compiler_params=LIGHT,
        name="pack",
    )(places, flags, *hbm(sources), *spare)


def relay_kernel(step, rows, near, far, grads, outs):
    for out, pieces, grad in zip(outs, (near, far), grads):
        for e, (piece, at) in enumerate(pieces):
            out[0, :, pl.ds(2 * step * e, 2 * step)] = piece[at, :, pl.ds(0, 2 * step)]
        if grad is not None:
            for e in range(rows):
                for n in range(2):
                    for g in range(BLOCKS):
                        at = pl.ds((2 * rows + 2 * e + n) * step, step)
                        out[0, g, at] = grad[e, n, pl.ds(g * step, step)]


def relay(step, held, near, far, grads, spare, flagged=False, kept=jax.ShapeDtypeStruct):
    rows = len(near)
    kinds = 2 if far else 1
    high = (4 if grads else 2) * rows * step
    flag_sources = [*near, *far] if flagged else []

    def kernel(*refs):
        refs = list(refs)
        near_refs = [(refs.pop(0), 0) for _ in range(rows)]
        far_refs = [(refs.pop(0), 0) for _ in far]
        grad_refs = [refs.pop(0) for _ in grads] or [None] * kinds
        flag_refs = [refs.pop(0) for _ in flag_sources]
        outs = refs[len(spare) :]
        relay_kernel(step, rows, near_refs, far_refs, grad_refs, outs[:kinds])
        for d, ref in enumerate(flag_refs):
            outs[kinds][d] = ref[0, 0]

    def whole(shape):
        return pl.BlockSpec(shape, lambda i: (0,) * len(shape))

    shape = (1, BLOCKS, high, HD)
    return pl.pallas_call(
        kernel,
        grid=(1,),
        out_shape=[kept(shape, BF16)] * kinds
        + ([struct((len(flag_sources), FLAG_ROWS, HD), BF16)] if flagged else []),
        in_specs=[
            pl.BlockSpec((1, BLOCKS, 2 * step, HD), lambda i, at=at: (at, 0, 0, 0))
            for at in [held] * rows + [0] * len(far)
        ]
        + [whole(value.shape) for value in grads]
        + [
            pl.BlockSpec(
                (1, 1, FLAG_ROWS, HD),
                lambda i, at=value.shape[2] // FLAG_ROWS - 1: (0, 0, at, 0),
            )
            for value in flag_sources
        ]
        + [ANY] * len(spare),
        out_specs=[whole(shape)] * kinds
        + ([whole((len(flag_sources), FLAG_ROWS, HD))] if flagged else []),
        cost_estimate=moved(kinds * 4 * BLOCKS * high * HD),
        compiler_params=LIGHT,
        name="relay",
    )(*near, *far, *grads, *flag_sources, *spare)


def nt(a, b):
    return lax.dot_general(a, b, (((1,), (1,)), ((), ())), preferred_element_type=F32)


def nn(a, b):
    return jnp.dot(a, b, preferred_element_type=F32)


def attend_kernel(plan, rows, tile, table_ref, *refs):
    loads, slabs_here, n_in, spare = plan
    inputs = refs[:n_in]
    rest = refs[n_in + spare :]
    done, local, grads_one, grads_two = rest[:4]
    qbuf, gbuf, kbuf, vbuf, kt, vt, dk_t, dv_t, s_buf, p_buf, ds_buf, ot = rest[4:]
    targets = {"k": kbuf, "v": vbuf, "q": qbuf, "g": gbuf}
    step = tile // BLOCKS
    for n, at, kind, slab, e in loads:
        for g in range(BLOCKS):
            targets[kind][slab, pl.ds(e * tile + g * step, step)] = inputs[n][
                0, g, pl.ds(at * step, step)
            ]
    width = rows * tile
    team = slabs_here * rows
    places = kbuf.shape[0]

    def prepare(n, carry):
        kt[n] = kbuf[n].T
        vt[n] = vbuf[n].T
        dk_t[n] = jnp.zeros((HD, width), F32)
        dv_t[n] = jnp.zeros((HD, width), F32)
        return carry

    lax.fori_loop(0, places, prepare, 0)
    lane = lax.broadcasted_iota(jnp.int32, (1, width), 1)

    queries = [qbuf[a] for a in range(slabs_here)]
    grads_in = [gbuf[a] for a in range(slabs_here)]
    late = {}

    def spot(a, b):
        return table_ref[a * rows, 3 * rows + b]

    def by_query(a, b, e, seen, unseen):
        keep = jnp.zeros((1, width), jnp.int32)
        for f in range(rows):
            inside = (lane >= f * tile) & (lane < (f + 1) * tile)
            keep = jnp.where(inside, table_ref[a * rows + f, b * rows + e], keep)
        return jnp.where(keep > 0, seen, unseen)

    def scores(a, b, top):
        for e in range(rows):
            at = pl.ds(e * tile, tile)
            s = nt(kbuf[spot(a, b), at], queries[a])
            s_buf[a, b, at] = s
            best = jnp.max(s, axis=0, keepdims=True)
            top = jnp.maximum(top, by_query(a, b, e, best, -jnp.inf))
        return top

    def expo(a, b, top, total):
        for e in range(rows):
            at = pl.ds(e * tile, tile)
            p = jnp.exp2((s_buf[a, b, at] - by_query(a, b, e, top, jnp.inf)) * FACTOR)
            total = total + jnp.sum(p, axis=0, keepdims=True)
            p_buf[a, b, at] = p.astype(BF16)
        ot[a] += nn(vt[spot(a, b)], p_buf[a, b])
        return total

    def between(a, total):
        inv = 1.0 / total
        low_t = (ot[a] * inv).astype(BF16)
        grad_t = grads_in[a].T.astype(F32)
        offset = jnp.sum(grad_t * low_t.astype(F32), axis=0, keepdims=True)
        grad_over = (grad_t * inv).astype(BF16)
        query_over = (queries[a].T.astype(F32) * (inv * SCALE)).astype(BF16)
        out = low_t.T
        for f in range(rows):
            done[a * rows + f, 0] = out[f * tile : (f + 1) * tile]
        ot[a] = jnp.zeros((HD, width), F32)
        late[a] = (inv, offset, grad_over, query_over)

    def backward(a, b):
        _, offset, grad_over, query_over = late[a]
        place = spot(a, b)
        for e in range(rows):
            at = pl.ds(e * tile, tile)
            dp = nt(vbuf[place, at], grads_in[a])
            ds_buf[at] = p_buf[a, b, at] * (dp - offset).astype(BF16)
        dv_t[place] += nt(grad_over, p_buf[a, b])
        dk_t[place] += nt(query_over, ds_buf[...])
        ot[a] += nn(kt[place], ds_buf[...])

    def after(a):
        dq = (ot[a] * (late[a][0] * SCALE)).astype(BF16).T
        for f in range(rows):
            done[a * rows + f, 1] = dq[f * tile : (f + 1) * tile]

    tops = [jnp.full((1, width), -jnp.inf, F32) for _ in range(slabs_here)]
    totals = [jnp.zeros((1, width), F32) for _ in range(slabs_here)]
    for a in range(slabs_here):
        ot[a] = jnp.zeros((HD, width), F32)
    for turn in range(slabs_here + 2):
        here = [a for a in range(slabs_here) if 0 <= turn - a <= 2]

        def blocks(b, carry, turn=turn, here=here):
            tops, totals = list(carry[0]), list(carry[1])
            for a in here:
                if turn - a == 0:
                    tops[a] = scores(a, b, tops[a])
                elif turn - a == 1:
                    totals[a] = expo(a, b, tops[a], totals[a])
                else:
                    backward(a, b)
            return tuple(tops), tuple(totals)

        tops, totals = lax.fori_loop(0, 3, blocks, (tuple(tops), tuple(totals)))
        for a in here:
            if turn - a == 1:
                between(a, totals[a])
            elif turn - a == 2:
                after(a)

    for n, sums in enumerate((dk_t, dv_t)):
        for d in range(team):
            local[d, n] = sums[d // rows, :, pl.ds(d % rows * tile, tile)].T
        for m, grads in enumerate((grads_one, grads_two)):
            for e in range(rows):
                terms = sums[slabs_here + m, :, pl.ds(e * tile, tile)]
                grads[e, n] = terms.astype(BF16).T


def attend(rows, tile, slabs_here, table, loads, inputs, spare):
    places = slabs_here + 2
    team = slabs_here * rows
    width = rows * tile
    scores = 3 * slabs_here * width * width

    def head_spec(value, c):
        shape = (1,) + value.shape[1:]
        return pl.BlockSpec(shape, lambda i: (c, 0, 0, 0), pipeline_mode=pl.Buffered(1))

    def whole(shape):
        return pl.BlockSpec(shape, lambda i: (0,) * len(shape), pipeline_mode=pl.Buffered(1))

    shapes = [
        struct((team, 2, tile, HD), BF16),
        struct((team, 2, tile, HD), F32),
        struct((rows, 2, tile, HD), BF16),
        struct((rows, 2, tile, HD), BF16),
    ]
    plan = (loads, slabs_here, len(inputs), len(spare))
    return pl.pallas_call(
        functools.partial(attend_kernel, plan, rows, tile),
        grid=(1,),
        out_shape=shapes,
        in_specs=[SMEM] + [head_spec(value, c) for value, c in inputs] + [ANY] * len(spare),
        out_specs=[whole(shape.shape) for shape in shapes],
        scratch_shapes=[
            pltpu.VMEM((slabs_here, width, HD), BF16),
            pltpu.VMEM((slabs_here, width, HD), BF16),
            pltpu.VMEM((places, width, HD), BF16),
            pltpu.VMEM((places, width, HD), BF16),
            pltpu.VMEM((places, HD, width), BF16),
            pltpu.VMEM((places, HD, width), BF16),
            pltpu.VMEM((places, HD, width), F32),
            pltpu.VMEM((places, HD, width), F32),
            pltpu.VMEM((slabs_here, 3, width, width), F32),
            pltpu.VMEM((slabs_here, 3, width, width), BF16),
            pltpu.VMEM((width, width), BF16),
            pltpu.VMEM((slabs_here, HD, width), F32),
        ],
        cost_estimate=pl.CostEstimate(
            flops=12 * scores * HD, bytes_accessed=8 * 1024 * 1024, transcendentals=scores
        ),
        compiler_params=PARAMS,
        name="attend",
    )(table, *[value for value, _ in inputs], *spare)


def finish(rows, extras, done, local, grads, spare):
    team, _, tile, _ = done.shape
    step = tile // BLOCKS

    def kernel(done, local, *refs):
        terms, outs = refs[: len(grads)], refs[-team:]
        for d in range(team):
            out = outs[d].at[0]
            for n in range(2):
                out[n] = done[d, n]
                for g in range(BLOCKS):
                    at = pl.ds(g * step, step)
                    total = local[d, n, at]
                    for term, (_, packed), slab in zip(terms, grads, extras):
                        if d // rows != slab:
                            continue
                        if packed:
                            row = pl.ds((2 * (d % rows) + n) * step, step)
                            total = total + term[0, g, row].astype(F32)
                        else:
                            total = total + term[d % rows, n, at].astype(F32)
                    out[2 + n, at] = total.astype(BF16)

    def whole(shape):
        return pl.BlockSpec(shape, lambda i: (0,) * len(shape))

    def grad_spec(value, packed):
        if not packed:
            return whole(value.shape)
        return pl.BlockSpec((1, BLOCKS, 2 * rows * step, HD), lambda i: (0, 0, 1, 0))

    piece = (1, 4, tile, HD)
    return pl.pallas_call(
        kernel,
        grid=(1,),
        out_shape=[struct(piece, BF16)] * team,
        in_specs=[whole(done.shape), whole(local.shape)]
        + [grad_spec(*grad) for grad in grads]
        + [ANY] * len(spare),
        out_specs=[whole(piece)] * team,
        cost_estimate=moved(team * 24 * tile * HD),
        compiler_params=LIGHT,
        name="finish",
    )(done, local, *[value for value, _ in grads], *spare)


def unpack(c, places, pieces, outs, shape):
    tile = shape[1]
    step = tile // BLOCKS
    team = len(pieces)
    held = [] if outs is None else list(outs)

    def kernel(places_ref, *refs):
        for d in range(team):
            lanes = pl.ds(pl.multiple_of(places_ref[d] * HD, HD), HD)
            for n in range(4):
                refs[n - 4][0, :, lanes] = refs[d][0, n]

    return pl.pallas_call(
        kernel,
        grid=(BLOCKS,),
        out_shape=[struct(shape, BF16)] * 4,
        in_specs=[SMEM]
        + [pl.BlockSpec((1, 4, step, HD), lambda i: (0, 0, i, 0))] * team
        + [ANY] * len(held),
        out_specs=[pl.BlockSpec((1, step, team * HD), lambda i: (0, i, c))] * 4,
        input_output_aliases={1 + team + n: n for n in range(len(held))},
        cost_estimate=moved(16 * tile * team * HD),
        compiler_params=LIGHT,
        name="unpack",
    )(places, *pieces, *held)


def body(queries, keys, values, grad_out, window_tiles, window_count):
    rows_here, tile, lane_width = queries.shape
    wmax = window_tiles.shape[1]
    heads = lane_width // HD
    rows = lax.axis_size("sub")
    slabs = lax.axis_size("ctx")
    span = 2 if heads % (2 * rows) == 0 and slabs % 2 == 0 else 1
    team = span * rows
    per = heads // team
    size = slabs * rows
    slab = lax.axis_index("ctx")
    row = lax.axis_index("sub")
    odd = slab % span
    me = odd * rows + row

    def swap(value, d):
        if d == 0:
            return value
        return lax.ppermute(value, RING, [(i, i - i % team + (i % team ^ d)) for i in range(size)])

    def shift(value, way, flip=0):
        pairs = []
        for i in range(size):
            place = i % team // rows
            forward = (place == span - 1) if way == 0 else (place == 0)
            if span == 1:
                forward = way == 0
            j = i + team if forward else i - team
            if 0 <= j < size:
                pairs.append((i, j ^ flip))
        return lax.ppermute(value, RING, pairs)

    places = (window_tiles[0] // rows - slab + 1) * rows + window_tiles[0] % rows
    listed = jnp.arange(wmax) < window_count[0]
    flags = jnp.any(
        (places[None, :] == jnp.arange(3 * rows)[:, None]) & listed[None, :], axis=1
    ).astype(jnp.int32)

    members = jnp.arange(team, dtype=jnp.int32) ^ me
    sources = (keys, values, queries, grad_out)
    kinds = (0, 1, 2, 3)
    every = tuple(range(per))
    far = tuple(range(rows, team))
    step = tile // BLOCKS

    jobs = [(d, (0,), kinds, True) for d in (*far, 1, 0)]
    packed = pack(jobs, (0,), members, flags, sources, [])
    count = len(far)
    mates = {0: (packed[-1], swap(packed[-2], 1), 0)}
    sent = {(0, d): packed[n] for n, d in enumerate(far)}
    rest = every[1:]
    if rest:
        jobs = [(d, (c,), kinds, False) for c in rest for d in far]
        jobs += [(1, rest, kinds, False), (0, rest, kinds, False)]
        packed = pack(jobs, rest, members, flags, sources, [mates[0][1]], pltpu.HBM)
        sent.update(
            {(c, d): packed[m * count + n] for m, c in enumerate(rest) for n, d in enumerate(far)}
        )
        beside = swap(packed[-2], 1)
        mates.update({c: (packed[-1], beside, m) for m, c in enumerate(rest)})

    arrived = {key: swap(value, key[1]) for key, value in sent.items()}
    halos = {}
    ready = {}
    worked = {}
    home = {}

    def pass_on(c, spare):
        pieces = [arrived[c, d] for d in far]
        if c == 0:
            pieces = hbm(pieces)
        kept = pltpu.HBM if c < 2 else jax.ShapeDtypeStruct
        grads = [worked[c - 2][3], worked[c - 2][2]] if c >= 2 else []
        outs = relay(step, mates[c][2], mates[c][:2], pieces, grads, spare, c == 0, kept)
        ready[c] = outs[0]
        halos[c] = (shift(outs[0], 0), shift(outs[span - 1], 1))
        return outs[-1]

    def finished(c, spare):
        done, local, grads_one, grads_two = worked[c]
        if c + 2 < per:
            grads = [(halos[c + 2][1], True), (halos[c + 2][0], True)]
        else:
            grads = [(shift(grads_one, 1), False), (shift(grads_two, 0), False)]
        pieces = finish(rows, extras, done, local, grads, spare)
        home[c] = [swap(piece, d) for d, piece in enumerate(pieces)]
        return pieces[0]

    all_flags = pass_on(0, hbm([packed[0]]))
    if per > 1:
        pass_on(1, hbm([ready[0]]))
    table = all_flags[:, 0, : 3 * rows].astype(jnp.int32)
    table = table.reshape(team, 3, rows)
    table = jnp.where(row == 0, table, table[:, :, ::-1])
    if span == 2:
        turned = table[:, ::-1]
        table = jnp.concatenate(
            [
                jnp.where(odd == 0, table[:rows], turned[:rows]),
                jnp.where(odd == 0, turned[rows:], table[rows:]),
            ]
        )
    if span == 1:
        windows = ((1, 0, 2),)
        extras = (0, 0)
    else:
        windows = ((3, 0, 1), (2, 1, 0))
        extras = (0, 1)
    spots = jnp.repeat(jnp.asarray(windows, jnp.int32), rows, axis=0)
    table = jnp.concatenate([table.reshape(team, 3 * rows), spots], axis=1)

    for c in every:
        inputs = []
        loads = []

        def add(value, held, wanted, slab_at, tiles):
            for at, (e, kind) in enumerate((e, kind) for e in tiles for kind in wanted):
                loads.append((len(inputs), at, kind, slab_at, e))
            inputs.append((value, held))

        for e in range(rows):
            add(mates[c][e], mates[c][2], "kvqg", 0, [e])
        for n in range(len(far)):
            piece = arrived[c, far[n]]
            add(hbm([piece])[0] if c == 0 else piece, 0, "kvqg", 1, [n])
        for n in range(2):
            add(halos[c][n], 0, "kv", span + n, range(rows))
        spare = [ready[c + 1]] if c < per - 1 else []
        if c == 0:
            spare = hbm(spare)
        if c >= 2:
            spare.append(finished(c - 2, [worked[c - 1][0]]))
        if c >= 3:
            spare += home[c - 3][1:]
        worked[c] = attend(rows, tile, span, table, tuple(loads), inputs, spare)
        if c + 2 < per:
            pass_on(c + 2, [])
    for c in every[-2:]:
        early = [k for k in (c - 2, c - 1) if k in home and (k == c - 2 or c == per - 1)]
        gone = [home[k][d] for k in early for d in (range(1, team) if k == c - 2 else far[:1])]
        finished(c, [worked[per - 1][0]] + gone)
    outs = None
    for c in every:
        outs = unpack(c, members, home[c], outs, queries.shape)
    attended, grad_queries, grad_keys, grad_values = outs
    return (attended, grad_queries, grad_keys, grad_values)


def solution(mesh):
    spec = P(("grp", "ctx", "sub"), None, "head")
    return jax.shard_map(
        body,
        mesh=mesh,
        in_specs=(spec, spec, spec, spec, P(("grp", "ctx", "sub"), None), P(("grp", "ctx", "sub"))),
        out_specs=(spec, spec, spec, spec),
        check_vma=False,
    )
```

profile of v0, /device:TPU:0, one launch (start us, length us, event | category | flops | bytes accessed | tf_op | source)
XLA Modules:
  0.0 185.9 jit_solution(14843234329647722868)
XLA Ops:
  1.3 0.7 fusion.3
  2.0 0.1 fusion.1
  2.1 2.5 %pack.2 = (bf16[1,4,400,128]{3,2,1,0:T(8,128)(2,1)S(1)}, bf16[1,4,400,128]{3,2,1,0:T(8,128)(2,1)S(1)}, bf16[1,4,400,128]{3,2,1,0:T(8,128)(2,1)S(1)}, bf16[1,4,400,128]{3,2,1,0:T(8,128)(2,1)S(1)}) custom-call(s32[4]{0:T(128)S(1)} %iota_xor_fusion.places_ref, s32[6]{0:T(128)S(1)} %convert_element_type.10.flags_ref, bf16[1,384,2048]{2,1,0:T(8,128)(2,1)} %refs_0_.3, ...), custom_call_target="tpu_custom_call" | custom-call | bytes 3276800 | tf_op jit(solution)/shard_map/pack/pallas_call | solution.py:67
  4.7 0.5 collective-permute-start
  5.2 2.6 %collective-permute-start.1 = (bf16[1,4,400,128]{3,2,1,0:T(8,128)(2,1)S(1)}, bf16[1,4,400,128]{3,2,1,0:T(8,128)(2,1)}, u32[]{:S(2)}, u32[]{:S(2)}) collective-permute-start(bf16[1,4,400,128]{3,2,1,0:T(8,128)(2,1)S(1)} %get-tuple-element.71), channel_id=1, source_target_pairs={{0,2},{1,3},{2,0},{3,1},{4,6},{5,7},{6,4},{7,5},{8,10},{9,11},{10,... | collective-permute-start | bytes 1228808 | tf_op jit(solution)/shard_map/ppermute | solution.py:411
  7.8 5.6 %pack.3 = (bf16[1,4,384,128]{3,2,1,0:T(8,128)(2,1)}, bf16[1,4,384,128]{3,2,1,0:T(8,128)(2,1)}, bf16[1,4,384,128]{3,2,1,0:T(8,128)(2,1)}, bf16[1,4,384,128]{3,2,1...) custom-call(s32[4]{0:T(128)S(1)} %iota_xor_fusion.places_ref, ...), custom_call_target="tpu_custom_call" | custom-call | bytes 9437184 | tf_op jit(solution)/shard_map/pack/pallas_call | solution.py:67
  13.5 0.2 collective-permute-start.3
  13.7 1.7 collective-permute-start.7
  15.4 0.3 collective-permute-start.6
  15.7 2.5 %collective-permute-done.1.refs_2_.refs_6_ = bf16[1,4,400,128]{3,2,1,0:T(8,128)(2,1)} collective-permute-done((bf16[1,4,400,128]{3,2,1,0:T(8,128)(2,1)S(1)}, bf16[1,4,400,128]{3,2,1,0:T(8,128)(2,1)}, u32[]{:S(2)}, u32[]{:S(2)}) %collective-permute-start.1) | collective-permute-done | bytes 409632 | tf_op jit(solution)/shard_map/ppermute | solution.py:411
  18.2 8.3 %collective-permute-done.2.refs_3_.refs_7_ = bf16[1,4,400,128]{3,2,1,0:T(8,128)(2,1)} collective-permute-done((bf16[1,4,400,128]{3,2,1,0:T(8,128)(2,1)S(1)}, bf16[1,4,400,128]{3,2,1,0:T(8,128)(2,1)}, u32[]{:S(2)}, u32[]{:S(2)}) %collective-permute-start.2) | collective-permute-done | bytes 409632 | tf_op jit(solution)/shard_map/ppermute | solution.py:411
  26.4 2.1 %relay.4 = (bf16[1,4,384,128]{3,2,1,0:T(8,128)(2,1)}, bf16[1,4,384,128]{3,2,1,0:T(8,128)(2,1)}, bf16[4,16,128]{2,1,0:T(8,128)(2,1)S(1)}) custom-call(bf16[1,4,400,128]{3,2,1,0:T(8,128)(2,1)S(1)} %get-tuple-element.69.refs_0_.refs_4_, bf16[1,4,400,128]{3,2,1,0:T(8,128)(2,1)S(1)} %collective-permute-done.refs_4_.refs_1_.refs_5_, ...), custom_call_target="tpu_custom_call" | custom-call | bytes 1572864 | tf_op jit(solution)/shard_map/relay/pallas_call | solution.py:116
  28.5 0.1 copy.29
  28.7 4.3 %collective-permute-start.13 = (bf16[1,4,384,128]{3,2,1,0:T(8,128)(2,1)}, bf16[1,4,384,128]{3,2,1,0:T(8,128)(2,1)}, u32[]{:S(2)}, u32[]{:S(2)}) collective-permute-start(bf16[1,4,384,128]{3,2,1,0:T(8,128)(2,1)} %get-tuple-element.85), channel_id=1, source_target_pairs={{0,4},{1,5},{4,8},{5,9},{6,2},{7,3},{8,12},{9,13},{10,6},{11,7},{1... | collective-permute-start | bytes 1179656 | tf_op jit(solution)/shard_map/ppermute | solution.py:423
  33.0 1.3 collective-permute-start.12
  34.4 0.1 pad_add_fusion
  34.5 0.1 copy.30
  34.6 0.2 collective-permute-done.7.refs_3_
  34.9 2.3 %collective-permute-start.10 = (bf16[1,4,384,128]{3,2,1,0:T(8,128)(2,1)}, bf16[1,4,384,128]{3,2,1,0:T(8,128)(2,1)S(1)}, u32[]{:S(2)}, u32[]{:S(2)}) collective-permute-start(bf16[1,4,384,128]{3,2,1,0:T(8,128)(2,1)} %get-tuple-element.83), channel_id=1, source_target_pairs={{0,2},{1,3},{2,0},{3,1},{4,6},{5,7},{6,4},{7,5},{8,10},{9,11},{10,... | collective-permute-start | bytes 1179656 | tf_op jit(solution)/shard_map/ppermute | solution.py:411
  37.2 6.6 %collective-permute-done.6.refs_2_ = bf16[1,4,384,128]{3,2,1,0:T(8,128)(2,1)} collective-permute-done((bf16[1,4,384,128]{3,2,1,0:T(8,128)(2,1)}, bf16[1,4,384,128]{3,2,1,0:T(8,128)(2,1)}, u32[]{:S(2)}, u32[]{:S(2)}) %collective-permute-start.6) | collective-permute-done | bytes 393248 | tf_op jit(solution)/shard_map/ppermute | solution.py:411
  43.8 0.8 collective-permute-start.11
  44.6 2.0 %relay.5 = (bf16[1,4,384,128]{3,2,1,0:T(8,128)(2,1)}, bf16[1,4,384,128]{3,2,1,0:T(8,128)(2,1)}) custom-call(bf16[3,4,384,128]{3,2,1,0:T(8,128)(2,1)S(1)} %copy-done, bf16[3,4,384,128]{3,2,1,0:T(8,128)(2,1)S(1)} %collective-permute-done.3.refs_1_, bf16[1,4,384,128]{3,2,1,0:T(8,128)(2,1)} %collective-permute-done.6.refs_2_, ...), custom_call_target="tpu_custom_call" | custom-call | bytes 1572864 | tf_op jit(solution)/shard_map/relay/pallas_call | solution.py:116
  46.5 3.5 %collective-permute-start.9 = (bf16[1,4,384,128]{3,2,1,0:T(8,128)(2,1)}, bf16[1,4,384,128]{3,2,1,0:T(8,128)(2,1)S(1)}, u32[]{:S(2)}, u32[]{:S(2)}) collective-permute-start(bf16[1,4,384,128]{3,2,1,0:T(8,128)(2,1)} %get-tuple-element.82), channel_id=1, source_target_pairs={{0,4},{1,5},{4,8},{5,9},{6,2},{7,3},{8,12},{9,13},{10,6},{11,7},{1... | collective-permute-start | bytes 1179656 | tf_op jit(solution)/shard_map/ppermute | solution.py:423
  50.0 1.3 collective-permute-start.8
  51.3 16.7 %attend.4 = (bf16[4,2,384,128]{3,2,1,0:T(8,128)(2,1)S(1)}, f32[4,2,384,128]{3,2,1,0:T(8,128)S(1)}, bf16[2,2,384,128]{3,2,1,0:T(8,128)(2,1)S(1)}, bf16[2,2,384,128]{3,2,1,0:T(8,128)(2,1)S(1)}) custom-call(s32[4,9]{1,0:T(4,128)S(1)} %pad_add_fusion.1.table_ref, bf16[1,4,400,128]{3,2,1,0:T(8,128)(2,1)S(1)} %get-tuple-element.69.refs_0_.refs_4_, ...), custom_call_target="tpu_custom_call" | custom-call | flops 5435817984 | bytes 8388608 | tf_op jit(solution)/shard_map/attend/pallas_call | solution.py:292
  68.1 0.2 relay.6
  68.3 4.7 %collective-permute-start.17 = (bf16[1,4,768,128]{3,2,1,0:T(8,128)(2,1)S(1)}, bf16[1,4,768,128]{3,2,1,0:T(8,128)(2,1)S(1)}, u32[]{:S(2)}, u32[]{:S(2)}) collective-permute-start(bf16[1,4,768,128]{3,2,1,0:T(8,128)(2,1)S(1)} %get-tuple-element.95), channel_id=1, source_target_pairs={{0,4},{1,5},{4,8},{5,9},{6,2},{7,3},{8,12},{9,13},{10,6},{11,7},{1... | collective-permute-start | bytes 2359304 | tf_op jit(solution)/shard_map/ppermute | solution.py:423
  73.0 1.5 collective-permute-start.16
  74.5 2.3 %collective-permute-start.4 = (bf16[1,4,384,128]{3,2,1,0:T(8,128)(2,1)S(1)}, bf16[1,4,384,128]{3,2,1,0:T(8,128)(2,1)S(1)}, u32[]{:S(2)}, u32[]{:S(2)}) collective-permute-start(bf16[1,4,384,128]{3,2,1,0:T(8,128)(2,1)S(1)} %copy-done.3), channel_id=1, source_target_pairs={{0,2},{1,3},{2,0},{3,1},{4,6},{5,7},{6,4},{7,5},{8,10},{9,11},{10,... | collective-permute-start | bytes 1179656 | tf_op jit(solution)/shard_map/ppermute | solution.py:411
  76.8 16.5 %attend.5 = (bf16[4,2,384,128]{3,2,1,0:T(8,128)(2,1)S(1)}, f32[4,2,384,128]{3,2,1,0:T(8,128)S(1)}, bf16[2,2,384,128]{3,2,1,0:T(8,128)(2,1)S(1)}, bf16[2,2,384,128]{3,2,1,0:T(8,128)(2,1)S(1)}) custom-call(s32[4,9]{1,0:T(4,128)S(1)} %pad_add_fusion.1.table_ref, bf16[3,4,384,128]{3,2,1,0:T(8,128)(2,1)S(1)} %copy-done, ...), custom_call_target="tpu_custom_call" | custom-call | flops 5435817984 | bytes 8388608 | tf_op jit(solution)/shard_map/attend/pallas_call | solution.py:292
  93.3 0.4 collective-permute-done.5.refs_3_
  93.8 0.2 relay.7
  93.9 4.3 %collective-permute-start.15 = (bf16[1,4,768,128]{3,2,1,0:T(8,128)(2,1)S(1)}, bf16[1,4,768,128]{3,2,1,0:T(8,128)(2,1)S(1)}, u32[]{:S(2)}, u32[]{:S(2)}) collective-permute-start(bf16[1,4,768,128]{3,2,1,0:T(8,128)(2,1)S(1)} %get-tuple-element.92), channel_id=1, source_target_pairs={{0,4},{1,5},{4,8},{5,9},{6,2},{7,3},{8,12},{9,13},{10,6},{11,7},{1... | collective-permute-start | bytes 2359304 | tf_op jit(solution)/shard_map/ppermute | solution.py:423
  98.2 1.3 collective-permute-start.14
  99.5 0.3 finish.4
  99.8 0.4 collective-permute-start.18
  100.1 1.2 collective-permute-start.19
  101.3 0.4 collective-permute-start.20
  101.7 15.9 %attend.6 = (bf16[4,2,384,128]{3,2,1,0:T(8,128)(2,1)S(1)}, f32[4,2,384,128]{3,2,1,0:T(8,128)S(1)}, bf16[2,2,384,128]{3,2,1,0:T(8,128)(2,1)S(1)}, bf16[2,2,384,128]{3,2,1,0:T(8,128)(2,1)S(1)}) custom-call(s32[4,9]{1,0:T(4,128)S(1)} %pad_add_fusion.1.table_ref, bf16[3,4,384,128]{3,2,1,0:T(8,128)(2,1)S(1)} %copy-done, ...), custom_call_target="tpu_custom_call" | custom-call | flops 5435817984 | bytes 8388608 | tf_op jit(solution)/shard_map/attend/pallas_call | solution.py:292
  117.6 4.6 %collective-permute-start.26 = (bf16[2,2,384,128]{3,2,1,0:T(8,128)(2,1)S(1)}, bf16[2,2,384,128]{3,2,1,0:T(8,128)(2,1)S(1)}, u32[]{:S(2)}, u32[]{:S(2)}) collective-permute-start(bf16[2,2,384,128]{3,2,1,0:T(8,128)(2,1)S(1)} %get-tuple-element.112), channel_id=1, source_target_pairs={{0,4},{1,5},{4,8},{5,9},{6,2},{7,3},{8,12},{9,13},{10,6},{11,7},{1... | collective-permute-start | bytes 1179656 | tf_op jit(solution)/shard_map/ppermute | solution.py:423
  122.2 1.5 collective-permute-start.27
  123.7 0.3 finish.5
  124.0 0.1 collective-permute-start.23
  124.1 1.1 collective-permute-start.24
  125.3 0.7 collective-permute-start.25
  125.9 15.9 %attend.7 = (bf16[4,2,384,128]{3,2,1,0:T(8,128)(2,1)S(1)}, f32[4,2,384,128]{3,2,1,0:T(8,128)S(1)}, bf16[2,2,384,128]{3,2,1,0:T(8,128)(2,1)S(1)}, bf16[2,2,384,128]{3,2,1,0:T(8,128)(2,1)S(1)}) custom-call(s32[4,9]{1,0:T(4,128)S(1)} %pad_add_fusion.1.table_ref, bf16[3,4,384,128]{3,2,1,0:T(8,128)(2,1)S(1)} %copy-done, ...), custom_call_target="tpu_custom_call" | custom-call | flops 5435817984 | bytes 8388608 | tf_op jit(solution)/shard_map/attend/pallas_call | solution.py:292
  141.9 4.6 %collective-permute-start.21 = (bf16[2,2,384,128]{3,2,1,0:T(8,128)(2,1)S(1)}, bf16[2,2,384,128]{3,2,1,0:T(8,128)(2,1)S(1)}, u32[]{:S(2)}, u32[]{:S(2)}) collective-permute-start(bf16[2,2,384,128]{3,2,1,0:T(8,128)(2,1)S(1)} %get-tuple-element.106), channel_id=1, source_target_pairs={{0,4},{1,5},{4,8},{5,9},{6,2},{7,3},{8,12},{9,13},{10,6},{11,7},{1... | collective-permute-start | bytes 1179656 | tf_op jit(solution)/shard_map/ppermute | solution.py:423
  146.5 1.3 collective-permute-start.22
  147.8 0.2 finish.6
  147.9 1.1 collective-permute-start.28
  149.0 1.1 collective-permute-start.33
  150.2 5.1 %collective-permute-done.21.refs_0_ = bf16[2,2,384,128]{3,2,1,0:T(8,128)(2,1)S(1)} collective-permute-done((bf16[2,2,384,128]{3,2,1,0:T(8,128)(2,1)S(1)}, bf16[2,2,384,128]{3,2,1,0:T(8,128)(2,1)S(1)}, u32[]{:S(2)}, u32[]{:S(2)}) %collective-permute-start.21) | collective-permute-done | bytes 393248 | tf_op jit(solution)/shard_map/ppermute | solution.py:423
  155.3 4.1 %collective-permute-done.22.refs_1_ = bf16[2,2,384,128]{3,2,1,0:T(8,128)(2,1)S(1)} collective-permute-done((bf16[2,2,384,128]{3,2,1,0:T(8,128)(2,1)S(1)}, bf16[2,2,384,128]{3,2,1,0:T(8,128)(2,1)S(1)}, u32[]{:S(2)}, u32[]{:S(2)}) %collective-permute-start.22) | collective-permute-done | bytes 393248 | tf_op jit(solution)/shard_map/ppermute | solution.py:423
  159.4 0.5 collective-permute-done.28.refs_6_.refs_2_
  160.0 0.2 finish.7
  160.2 1.1 collective-permute-start.30
  161.3 0.8 collective-permute-start.31
  162.1 2.4 %unpack.4 = (bf16[1,384,2048]{2,1,0:T(8,128)(2,1)}, bf16[1,384,2048]{2,1,0:T(8,128)(2,1)}, bf16[1,384,2048]{2,1,0:T(8,128)(2,1)}, bf16[1,384,2048]{2,1,0:T(8,128)(2,1)}) custom-call(s32[4]{0:T(128)S(1)} %iota_xor_fusion.places_ref, bf16[1,4,384,128]{3,2,1,0:T(8,128)(2,1)S(1)} %get-tuple-element.98.refs_7_.refs_0_, ...), custom_call_target="tpu_custom_call" | custom-call | bytes 3145728 | tf_op jit(solution)/shard_map/unpack/pallas_call | solution.py:378
  164.5 2.4 %unpack.5 = (bf16[1,384,2048]{2,1,0:T(8,128)(2,1)}, bf16[1,384,2048]{2,1,0:T(8,128)(2,1)}, bf16[1,384,2048]{2,1,0:T(8,128)(2,1)}, bf16[1,384,2048]{2,1,0:T(8,128)(2,1)}) custom-call(s32[4]{0:T(128)S(1)} %iota_xor_fusion.places_ref, ...), custom_call_target="tpu_custom_call", output_to_operand_aliasing={{0}: (5, {}), {1}: (6, {}), {2}: (7, {}), {3}: (8, {})} | custom-call | bytes 3145728 | tf_op jit(solution)/shard_map/unpack/pallas_call | solution.py:378
  166.9 0.1 collective-permute-done.33.refs_3_
  167.0 2.4 %unpack.6 = (bf16[1,384,2048]{2,1,0:T(8,128)(2,1)}, bf16[1,384,2048]{2,1,0:T(8,128)(2,1)}, bf16[1,384,2048]{2,1,0:T(8,128)(2,1)}, bf16[1,384,2048]{2,1,0:T(8,128)(2,1)}) custom-call(s32[4]{0:T(128)S(1)} %iota_xor_fusion.places_ref, ...), custom_call_target="tpu_custom_call", output_to_operand_aliasing={{0}: (5, {}), {1}: (6, {}), {2}: (7, {}), {3}: (8, {})} | custom-call | bytes 3145728 | tf_op jit(solution)/shard_map/unpack/pallas_call | solution.py:378
  169.4 7.5 %collective-permute-done.30.refs_2_ = bf16[1,4,384,128]{3,2,1,0:T(8,128)(2,1)S(1)} collective-permute-done((bf16[1,4,384,128]{3,2,1,0:T(8,128)(2,1)S(1)}, bf16[1,4,384,128]{3,2,1,0:T(8,128)(2,1)S(1)}, u32[]{:S(2)}, u32[]{:S(2)}) %collective-permute-start.30) | collective-permute-done | bytes 393248 | tf_op jit(solution)/shard_map/ppermute | solution.py:411
  176.8 6.6 %collective-permute-done.31.refs_3_ = bf16[1,4,384,128]{3,2,1,0:T(8,128)(2,1)S(1)} collective-permute-done((bf16[1,4,384,128]{3,2,1,0:T(8,128)(2,1)S(1)}, bf16[1,4,384,128]{3,2,1,0:T(8,128)(2,1)S(1)}, u32[]{:S(2)}, u32[]{:S(2)}) %collective-permute-start.31) | collective-permute-done | bytes 393248 | tf_op jit(solution)/shard_map/ppermute | solution.py:411
  183.5 2.4 %unpack.7 = (bf16[1,384,2048]{2,1,0:T(8,128)(2,1)}, bf16[1,384,2048]{2,1,0:T(8,128)(2,1)}, bf16[1,384,2048]{2,1,0:T(8,128)(2,1)}, bf16[1,384,2048]{2,1,0:T(8,128)(2,1)}) custom-call(s32[4]{0:T(128)S(1)} %iota_xor_fusion.places_ref, ...), custom_call_target="tpu_custom_call", output_to_operand_aliasing={{0}: (5, {}), {1}: (6, {}), {2}: (7, {}), {3}: (8, {})} | custom-call | bytes 3145728 | tf_op jit(solution)/shard_map/unpack/pallas_call | solution.py:378
  (47 shorter events, 0.5 us)
Async XLA Ops:
  4.7 3.2 %collective-permute-start = (bf16[1,4,400,128]{3,2,1,0:T(8,128)(2,1)S(1)}, bf16[1,4,400,128]{3,2,1,0:T(8,128)(2,1)S(1)}, u32[]{:S(2)}, u32[]{:S(2)}) collective-permute-start(bf16[1,4,400,128]{3,2,1,0:T(8,128)(2,1)S(1)} %get-tuple-element.70), channel_id=1, source_target_pairs={{0,1},{1,0},{2,3},{3,2},{4,5},{5,4},{6,7},{7,6},{8,9},{9,8},{10,11... | collective-permute-start | bytes 1228808 | tf_op jit(solution)/shard_map/ppermute | solution.py:411
  5.2 13.0 %collective-permute-start.1 = (bf16[1,4,400,128]{3,2,1,0:T(8,128)(2,1)S(1)}, bf16[1,4,400,128]{3,2,1,0:T(8,128)(2,1)}, u32[]{:S(2)}, u32[]{:S(2)}) collective-permute-start(bf16[1,4,400,128]{3,2,1,0:T(8,128)(2,1)S(1)} %get-tuple-element.71), channel_id=1, source_target_pairs={{0,2},{1,3},{2,0},{3,1},{4,6},{5,7},{6,4},{7,5},{8,10},{9,11},{10,... | collective-permute-start | bytes 1228808 | tf_op jit(solution)/shard_map/ppermute | solution.py:411
  7.7 18.7 %collective-permute-start.2 = (bf16[1,4,400,128]{3,2,1,0:T(8,128)(2,1)S(1)}, bf16[1,4,400,128]{3,2,1,0:T(8,128)(2,1)}, u32[]{:S(2)}, u32[]{:S(2)}) collective-permute-start(bf16[1,4,400,128]{3,2,1,0:T(8,128)(2,1)S(1)} %get-tuple-element.72), channel_id=1, source_target_pairs={{0,3},{1,2},{2,1},{3,0},{4,7},{5,6},{6,5},{7,4},{8,11},{9,10},{10,... | collective-permute-start | bytes 1228808 | tf_op jit(solution)/shard_map/ppermute | solution.py:411
  13.5 31.1 %collective-permute-start.3 = (bf16[3,4,384,128]{3,2,1,0:T(8,128)(2,1)}, bf16[3,4,384,128]{3,2,1,0:T(8,128)(2,1)S(1)}, u32[]{:S(2)}, u32[]{:S(2)}) collective-permute-start(bf16[3,4,384,128]{3,2,1,0:T(8,128)(2,1)} %get-tuple-element.76), channel_id=1, source_target_pairs={{0,1},{1,0},{2,3},{3,2},{4,5},{5,4},{6,7},{7,6},{8,9},{9,8},{10,11... | collective-permute-start | bytes 3538952 | tf_op jit(solution)/shard_map/ppermute | solution.py:411
  13.7 21.2 %collective-permute-start.7 = (bf16[1,4,384,128]{3,2,1,0:T(8,128)(2,1)}, bf16[1,4,384,128]{3,2,1,0:T(8,128)(2,1)}, u32[]{:S(2)}, u32[]{:S(2)}) collective-permute-start(bf16[1,4,384,128]{3,2,1,0:T(8,128)(2,1)} %get-tuple-element.79), channel_id=1, source_target_pairs={{0,3},{1,2},{2,1},{3,0},{4,7},{5,6},{6,5},{7,4},{8,11},{9,10},{10,... | collective-permute-start | bytes 1179656 | tf_op jit(solution)/shard_map/ppermute | solution.py:411
  15.4 28.4 %collective-permute-start.6 = (bf16[1,4,384,128]{3,2,1,0:T(8,128)(2,1)}, bf16[1,4,384,128]{3,2,1,0:T(8,128)(2,1)}, u32[]{:S(2)}, u32[]{:S(2)}) collective-permute-start(bf16[1,4,384,128]{3,2,1,0:T(8,128)(2,1)} %get-tuple-element.73.refs_8_), channel_id=1, source_target_pairs={{0,2},{1,3},{2,0},{3,1},{4,6},{5,7},{6,4},{7,5},{8,10},{9,11},{10,... | collective-permute-start | bytes 1179656 | tf_op jit(solution)/shard_map/ppermute | solution.py:411
  26.4 8.1 %copy-start.1 = (s32[2,3]{1,0:T(2,128)S(1)}, s32[2,3]{1,0:T(2,128)}, u32[]{:S(2)}) copy-start(s32[2,3]{1,0:T(2,128)} %constant.47.clone) | copy-start | bytes 76
  26.4 18.1 %copy-start = (bf16[3,4,384,128]{3,2,1,0:T(8,128)(2,1)S(1)}, bf16[3,4,384,128]{3,2,1,0:T(8,128)(2,1)}, u32[]{:S(2)}) copy-start(bf16[3,4,384,128]{3,2,1,0:T(8,128)(2,1)} %get-tuple-element.75.refs_0_) | copy-start | bytes 3538948
  28.7 21.4 %collective-permute-start.13 = (bf16[1,4,384,128]{3,2,1,0:T(8,128)(2,1)}, bf16[1,4,384,128]{3,2,1,0:T(8,128)(2,1)}, u32[]{:S(2)}, u32[]{:S(2)}) collective-permute-start(bf16[1,4,384,128]{3,2,1,0:T(8,128)(2,1)} %get-tuple-element.85), channel_id=1, source_target_pairs={{0,4},{1,5},{4,8},{5,9},{6,2},{7,3},{8,12},{9,13},{10,6},{11,7},{1... | collective-permute-start | bytes 1179656 | tf_op jit(solution)/shard_map/ppermute | solution.py:423
  33.0 18.3 %collective-permute-start.12 = (bf16[1,4,384,128]{3,2,1,0:T(8,128)(2,1)}, bf16[1,4,384,128]{3,2,1,0:T(8,128)(2,1)}, u32[]{:S(2)}, u32[]{:S(2)}) collective-permute-start(bf16[1,4,384,128]{3,2,1,0:T(8,128)(2,1)} %get-tuple-element.80.refs_4_), channel_id=1, source_target_pairs={{2,6},{3,7},{4,0},{5,1},{6,10},{7,11},{8,4},{9,5},{10,14},{11,15},... | collective-permute-start | bytes 1179656 | tf_op jit(solution)/shard_map/ppermute | solution.py:423
  34.9 33.2 %collective-permute-start.10 = (bf16[1,4,384,128]{3,2,1,0:T(8,128)(2,1)}, bf16[1,4,384,128]{3,2,1,0:T(8,128)(2,1)S(1)}, u32[]{:S(2)}, u32[]{:S(2)}) collective-permute-start(bf16[1,4,384,128]{3,2,1,0:T(8,128)(2,1)} %get-tuple-element.83), channel_id=1, source_target_pairs={{0,2},{1,3},{2,0},{3,1},{4,6},{5,7},{6,4},{7,5},{8,10},{9,11},{10,... | collective-permute-start | bytes 1179656 | tf_op jit(solution)/shard_map/ppermute | solution.py:411
  43.8 24.3 %collective-permute-start.11 = (bf16[1,4,384,128]{3,2,1,0:T(8,128)(2,1)}, bf16[1,4,384,128]{3,2,1,0:T(8,128)(2,1)S(1)}, u32[]{:S(2)}, u32[]{:S(2)}) collective-permute-start(bf16[1,4,384,128]{3,2,1,0:T(8,128)(2,1)} %get-tuple-element.84), channel_id=1, source_target_pairs={{0,3},{1,2},{2,1},{3,0},{4,7},{5,6},{6,5},{7,4},{8,11},{9,10},{10,... | collective-permute-start | bytes 1179656 | tf_op jit(solution)/shard_map/ppermute | solution.py:411
  46.5 30.3 %collective-permute-start.9 = (bf16[1,4,384,128]{3,2,1,0:T(8,128)(2,1)}, bf16[1,4,384,128]{3,2,1,0:T(8,128)(2,1)S(1)}, u32[]{:S(2)}, u32[]{:S(2)}) collective-permute-start(bf16[1,4,384,128]{3,2,1,0:T(8,128)(2,1)} %get-tuple-element.82), channel_id=1, source_target_pairs={{0,4},{1,5},{4,8},{5,9},{6,2},{7,3},{8,12},{9,13},{10,6},{11,7},{1... | collective-permute-start | bytes 1179656 | tf_op jit(solution)/shard_map/ppermute | solution.py:423
  50.0 26.8 %collective-permute-start.8 = (bf16[1,4,384,128]{3,2,1,0:T(8,128)(2,1)}, bf16[1,4,384,128]{3,2,1,0:T(8,128)(2,1)S(1)}, u32[]{:S(2)}, u32[]{:S(2)}) collective-permute-start(bf16[1,4,384,128]{3,2,1,0:T(8,128)(2,1)} %get-tuple-element.81.refs_6_), channel_id=1, source_target_pairs={{2,6},{3,7},{4,0},{5,1},{6,10},{7,11},{8,4},{9,5},{10,14},{11,15},... | collective-permute-start | bytes 1179656 | tf_op jit(solution)/shard_map/ppermute | solution.py:423
  68.1 6.4 %copy-start.3 = (bf16[1,4,384,128]{3,2,1,0:T(8,128)(2,1)S(1)}, bf16[1,4,384,128]{3,2,1,0:T(8,128)(2,1)}, u32[]{:S(2)}) copy-start(bf16[1,4,384,128]{3,2,1,0:T(8,128)(2,1)} %get-tuple-element.77) | copy-start | bytes 1179652
  68.1 8.7 %copy-start.2 = (bf16[1,4,384,128]{3,2,1,0:T(8,128)(2,1)S(1)}, bf16[1,4,384,128]{3,2,1,0:T(8,128)(2,1)}, u32[]{:S(2)}) copy-start(bf16[1,4,384,128]{3,2,1,0:T(8,128)(2,1)} %get-tuple-element.78) | copy-start | bytes 1179652
  68.3 31.2 %collective-permute-start.17 = (bf16[1,4,768,128]{3,2,1,0:T(8,128)(2,1)S(1)}, bf16[1,4,768,128]{3,2,1,0:T(8,128)(2,1)S(1)}, u32[]{:S(2)}, u32[]{:S(2)}) collective-permute-start(bf16[1,4,768,128]{3,2,1,0:T(8,128)(2,1)S(1)} %get-tuple-element.95), channel_id=1, source_target_pairs={{0,4},{1,5},{4,8},{5,9},{6,2},{7,3},{8,12},{9,13},{10,6},{11,7},{1... | collective-permute-start | bytes 2359304 | tf_op jit(solution)/shard_map/ppermute | solution.py:423
  73.0 26.5 %collective-permute-start.16 = (bf16[1,4,768,128]{3,2,1,0:T(8,128)(2,1)S(1)}, bf16[1,4,768,128]{3,2,1,0:T(8,128)(2,1)S(1)}, u32[]{:S(2)}, u32[]{:S(2)}) collective-permute-start(bf16[1,4,768,128]{3,2,1,0:T(8,128)(2,1)S(1)} %get-tuple-element.88.refs_6_), channel_id=1, source_target_pairs={{2,6},{3,7},{4,0},{5,1},{6,10},{7,11},{8,4},{9,5},{10,14},{11,15},... | collective-permute-start | bytes 2359304 | tf_op jit(solution)/shard_map/ppermute | solution.py:423
  74.5 18.8 %collective-permute-start.4 = (bf16[1,4,384,128]{3,2,1,0:T(8,128)(2,1)S(1)}, bf16[1,4,384,128]{3,2,1,0:T(8,128)(2,1)S(1)}, u32[]{:S(2)}, u32[]{:S(2)}) collective-permute-start(bf16[1,4,384,128]{3,2,1,0:T(8,128)(2,1)S(1)} %copy-done.3), channel_id=1, source_target_pairs={{0,2},{1,3},{2,0},{3,1},{4,6},{5,7},{6,4},{7,5},{8,10},{9,11},{10,... | collective-permute-start | bytes 1179656 | tf_op jit(solution)/shard_map/ppermute | solution.py:411
  76.8 16.9 %collective-permute-start.5 = (bf16[1,4,384,128]{3,2,1,0:T(8,128)(2,1)S(1)}, bf16[1,4,384,128]{3,2,1,0:T(8,128)(2,1)S(1)}, u32[]{:S(2)}, u32[]{:S(2)}) collective-permute-start(bf16[1,4,384,128]{3,2,1,0:T(8,128)(2,1)S(1)} %copy-done.2), channel_id=1, source_target_pairs={{0,3},{1,2},{2,1},{3,0},{4,7},{5,6},{6,5},{7,4},{8,11},{9,10},{10,... | collective-permute-start | bytes 1179656 | tf_op jit(solution)/shard_map/ppermute | solution.py:411
  93.9 23.7 %collective-permute-start.15 = (bf16[1,4,768,128]{3,2,1,0:T(8,128)(2,1)S(1)}, bf16[1,4,768,128]{3,2,1,0:T(8,128)(2,1)S(1)}, u32[]{:S(2)}, u32[]{:S(2)}) collective-permute-start(bf16[1,4,768,128]{3,2,1,0:T(8,128)(2,1)S(1)} %get-tuple-element.92), channel_id=1, source_target_pairs={{0,4},{1,5},{4,8},{5,9},{6,2},{7,3},{8,12},{9,13},{10,6},{11,7},{1... | collective-permute-start | bytes 2359304 | tf_op jit(solution)/shard_map/ppermute | solution.py:423
  98.2 24.0 %collective-permute-start.14 = (bf16[1,4,768,128]{3,2,1,0:T(8,128)(2,1)S(1)}, bf16[1,4,768,128]{3,2,1,0:T(8,128)(2,1)S(1)}, u32[]{:S(2)}, u32[]{:S(2)}) collective-permute-start(bf16[1,4,768,128]{3,2,1,0:T(8,128)(2,1)S(1)} %get-tuple-element.91.refs_6_), channel_id=1, source_target_pairs={{2,6},{3,7},{4,0},{5,1},{6,10},{7,11},{8,4},{9,5},{10,14},{11,15},... | collective-permute-start | bytes 2359304 | tf_op jit(solution)/shard_map/ppermute | solution.py:423
  99.8 24.2 %collective-permute-start.18 = (bf16[1,4,384,128]{3,2,1,0:T(8,128)(2,1)S(1)}, bf16[1,4,384,128]{3,2,1,0:T(8,128)(2,1)S(1)}, u32[]{:S(2)}, u32[]{:S(2)}) collective-permute-start(bf16[1,4,384,128]{3,2,1,0:T(8,128)(2,1)S(1)} %get-tuple-element.101), channel_id=1, source_target_pairs={{0,1},{1,0},{2,3},{3,2},{4,5},{5,4},{6,7},{7,6},{8,9},{9,8},{10,11... | collective-permute-start | bytes 1179656 | tf_op jit(solution)/shard_map/ppermute | solution.py:411
  100.1 24.0 %collective-permute-start.19 = (bf16[1,4,384,128]{3,2,1,0:T(8,128)(2,1)S(1)}, bf16[1,4,384,128]{3,2,1,0:T(8,128)(2,1)S(1)}, u32[]{:S(2)}, u32[]{:S(2)}) collective-permute-start(bf16[1,4,384,128]{3,2,1,0:T(8,128)(2,1)S(1)} %get-tuple-element.102), channel_id=1, source_target_pairs={{0,2},{1,3},{2,0},{3,1},{4,6},{5,7},{6,4},{7,5},{8,10},{9,11},{10,... | collective-permute-start | bytes 1179656 | tf_op jit(solution)/shard_map/ppermute | solution.py:411
  101.3 24.0 %collective-permute-start.20 = (bf16[1,4,384,128]{3,2,1,0:T(8,128)(2,1)S(1)}, bf16[1,4,384,128]{3,2,1,0:T(8,128)(2,1)S(1)}, u32[]{:S(2)}, u32[]{:S(2)}) collective-permute-start(bf16[1,4,384,128]{3,2,1,0:T(8,128)(2,1)S(1)} %get-tuple-element.103), channel_id=1, source_target_pairs={{0,3},{1,2},{2,1},{3,0},{4,7},{5,6},{6,5},{7,4},{8,11},{9,10},{10,... | collective-permute-start | bytes 1179656 | tf_op jit(solution)/shard_map/ppermute | solution.py:411
  117.6 24.3 %collective-permute-start.26 = (bf16[2,2,384,128]{3,2,1,0:T(8,128)(2,1)S(1)}, bf16[2,2,384,128]{3,2,1,0:T(8,128)(2,1)S(1)}, u32[]{:S(2)}, u32[]{:S(2)}) collective-permute-start(bf16[2,2,384,128]{3,2,1,0:T(8,128)(2,1)S(1)} %get-tuple-element.112), channel_id=1, source_target_pairs={{0,4},{1,5},{4,8},{5,9},{6,2},{7,3},{8,12},{9,13},{10,6},{11,7},{1... | collective-permute-start | bytes 1179656 | tf_op jit(solution)/shard_map/ppermute | solution.py:423
  122.2 24.2 %collective-permute-start.27 = (bf16[2,2,384,128]{3,2,1,0:T(8,128)(2,1)S(1)}, bf16[2,2,384,128]{3,2,1,0:T(8,128)(2,1)S(1)}, u32[]{:S(2)}, u32[]{:S(2)}) collective-permute-start(bf16[2,2,384,128]{3,2,1,0:T(8,128)(2,1)S(1)} %get-tuple-element.113), channel_id=1, source_target_pairs={{2,6},{3,7},{4,0},{5,1},{6,10},{7,11},{8,4},{9,5},{10,14},{11,15},... | collective-permute-start | bytes 1179656 | tf_op jit(solution)/shard_map/ppermute | solution.py:423
  124.0 23.9 %collective-permute-start.23 = (bf16[1,4,384,128]{3,2,1,0:T(8,128)(2,1)S(1)}, bf16[1,4,384,128]{3,2,1,0:T(8,128)(2,1)S(1)}, u32[]{:S(2)}, u32[]{:S(2)}) collective-permute-start(bf16[1,4,384,128]{3,2,1,0:T(8,128)(2,1)S(1)} %get-tuple-element.108), channel_id=1, source_target_pairs={{0,1},{1,0},{2,3},{3,2},{4,5},{5,4},{6,7},{7,6},{8,9},{9,8},{10,11... | collective-permute-start | bytes 1179656 | tf_op jit(solution)/shard_map/ppermute | solution.py:411
  124.1 24.9 %collective-permute-start.24 = (bf16[1,4,384,128]{3,2,1,0:T(8,128)(2,1)S(1)}, bf16[1,4,384,128]{3,2,1,0:T(8,128)(2,1)S(1)}, u32[]{:S(2)}, u32[]{:S(2)}) collective-permute-start(bf16[1,4,384,128]{3,2,1,0:T(8,128)(2,1)S(1)} %get-tuple-element.109), channel_id=1, source_target_pairs={{0,2},{1,3},{2,0},{3,1},{4,6},{5,7},{6,4},{7,5},{8,10},{9,11},{10,... | collective-permute-start | bytes 1179656 | tf_op jit(solution)/shard_map/ppermute | solution.py:411
  125.3 23.8 %collective-permute-start.25 = (bf16[1,4,384,128]{3,2,1,0:T(8,128)(2,1)S(1)}, bf16[1,4,384,128]{3,2,1,0:T(8,128)(2,1)S(1)}, u32[]{:S(2)}, u32[]{:S(2)}) collective-permute-start(bf16[1,4,384,128]{3,2,1,0:T(8,128)(2,1)S(1)} %get-tuple-element.110), channel_id=1, source_target_pairs={{0,3},{1,2},{2,1},{3,0},{4,7},{5,6},{6,5},{7,4},{8,11},{9,10},{10,... | collective-permute-start | bytes 1179656 | tf_op jit(solution)/shard_map/ppermute | solution.py:411
  141.9 13.4 %collective-permute-start.21 = (bf16[2,2,384,128]{3,2,1,0:T(8,128)(2,1)S(1)}, bf16[2,2,384,128]{3,2,1,0:T(8,128)(2,1)S(1)}, u32[]{:S(2)}, u32[]{:S(2)}) collective-permute-start(bf16[2,2,384,128]{3,2,1,0:T(8,128)(2,1)S(1)} %get-tuple-element.106), channel_id=1, source_target_pairs={{0,4},{1,5},{4,8},{5,9},{6,2},{7,3},{8,12},{9,13},{10,6},{11,7},{1... | collective-permute-start | bytes 1179656 | tf_op jit(solution)/shard_map/ppermute | solution.py:423
  146.5 13.0 %collective-permute-start.22 = (bf16[2,2,384,128]{3,2,1,0:T(8,128)(2,1)S(1)}, bf16[2,2,384,128]{3,2,1,0:T(8,128)(2,1)S(1)}, u32[]{:S(2)}, u32[]{:S(2)}) collective-permute-start(bf16[2,2,384,128]{3,2,1,0:T(8,128)(2,1)S(1)} %get-tuple-element.107), channel_id=1, source_target_pairs={{2,6},{3,7},{4,0},{5,1},{6,10},{7,11},{8,4},{9,5},{10,14},{11,15},... | collective-permute-start | bytes 1179656 | tf_op jit(solution)/shard_map/ppermute | solution.py:423
  147.9 12.0 %collective-permute-start.28 = (bf16[1,4,384,128]{3,2,1,0:T(8,128)(2,1)S(1)}, bf16[1,4,384,128]{3,2,1,0:T(8,128)(2,1)S(1)}, u32[]{:S(2)}, u32[]{:S(2)}) collective-permute-start(bf16[1,4,384,128]{3,2,1,0:T(8,128)(2,1)S(1)} %get-tuple-element.114), channel_id=1, source_target_pairs={{0,2},{1,3},{2,0},{3,1},{4,6},{5,7},{6,4},{7,5},{8,10},{9,11},{10,... | collective-permute-start | bytes 1179656 | tf_op jit(solution)/shard_map/ppermute | solution.py:411
  149.0 17.8 %collective-permute-start.32 = (bf16[1,4,384,128]{3,2,1,0:T(8,128)(2,1)S(1)}, bf16[1,4,384,128]{3,2,1,0:T(8,128)(2,1)S(1)}, u32[]{:S(2)}, u32[]{:S(2)}) collective-permute-start(bf16[1,4,384,128]{3,2,1,0:T(8,128)(2,1)S(1)} %get-tuple-element.120), channel_id=1, source_target_pairs={{0,1},{1,0},{2,3},{3,2},{4,5},{5,4},{6,7},{7,6},{8,9},{9,8},{10,11... | collective-permute-start | bytes 1179656 | tf_op jit(solution)/shard_map/ppermute | solution.py:411
  149.0 17.9 %collective-permute-start.33 = (bf16[1,4,384,128]{3,2,1,0:T(8,128)(2,1)S(1)}, bf16[1,4,384,128]{3,2,1,0:T(8,128)(2,1)S(1)}, u32[]{:S(2)}, u32[]{:S(2)}) collective-permute-start(bf16[1,4,384,128]{3,2,1,0:T(8,128)(2,1)S(1)} %get-tuple-element.121), channel_id=1, source_target_pairs={{0,3},{1,2},{2,1},{3,0},{4,7},{5,6},{6,5},{7,4},{8,11},{9,10},{10,... | collective-permute-start | bytes 1179656 | tf_op jit(solution)/shard_map/ppermute | solution.py:411
  160.1 9.2 %collective-permute-start.29 = (bf16[1,4,384,128]{3,2,1,0:T(8,128)(2,1)S(1)}, bf16[1,4,384,128]{3,2,1,0:T(8,128)(2,1)S(1)}, u32[]{:S(2)}, u32[]{:S(2)}) collective-permute-start(bf16[1,4,384,128]{3,2,1,0:T(8,128)(2,1)S(1)} %get-tuple-element.116), channel_id=1, source_target_pairs={{0,1},{1,0},{2,3},{3,2},{4,5},{5,4},{6,7},{7,6},{8,9},{9,8},{10,11... | collective-permute-start | bytes 1179656 | tf_op jit(solution)/shard_map/ppermute | solution.py:411
  160.2 16.6 %collective-permute-start.30 = (bf16[1,4,384,128]{3,2,1,0:T(8,128)(2,1)S(1)}, bf16[1,4,384,128]{3,2,1,0:T(8,128)(2,1)S(1)}, u32[]{:S(2)}, u32[]{:S(2)}) collective-permute-start(bf16[1,4,384,128]{3,2,1,0:T(8,128)(2,1)S(1)} %get-tuple-element.117), channel_id=1, source_target_pairs={{0,2},{1,3},{2,0},{3,1},{4,6},{5,7},{6,4},{7,5},{8,10},{9,11},{10,... | collective-permute-start | bytes 1179656 | tf_op jit(solution)/shard_map/ppermute | solution.py:411
  161.3 22.1 %collective-permute-start.31 = (bf16[1,4,384,128]{3,2,1,0:T(8,128)(2,1)S(1)}, bf16[1,4,384,128]{3,2,1,0:T(8,128)(2,1)S(1)}, u32[]{:S(2)}, u32[]{:S(2)}) collective-permute-start(bf16[1,4,384,128]{3,2,1,0:T(8,128)(2,1)S(1)} %get-tuple-element.118), channel_id=1, source_target_pairs={{0,3},{1,2},{2,1},{3,0},{4,7},{5,6},{6,5},{7,4},{8,11},{9,10},{10,... | collective-permute-start | bytes 1179656 | tf_op jit(solution)/shard_map/ppermute | solution.py:411
where the time goes:
time: 187 us; the launch traced here: 186 us
  Pallas kernels  87.9 us (47%)
  starting transfers between devices  52.9 us (28%)
  waiting for transfers between devices  42.1 us (23%)
    pallas_call x4, Pallas kernels, attend(): pl.pallas_call(functools.partial(attend_kernel, plan, rows, tile), grid=(...  65 us
    ppermute x12, starting transfers between devices, shift(): return lax.ppermute(value, RING, pairs)  34.1 us
    ppermute x22, waiting for transfers between devices, swap(): lax.ppermute(value, RING, [(i, i - i % team + (i % team ^ d)) for i in ra...  32.8 us
    ppermute x22, starting transfers between devices, swap(): lax.ppermute(value, RING, [(i, i - i % team + (i % team ^ d)) for i in ra...  18.8 us
    pallas_call x4, Pallas kernels, unpack(): pl.pallas_call(kernel, grid=(BLOCKS,), out_shape=[struct(shape, BF16)] *...  9.55 us
    ppermute x12, waiting for transfers between devices, shift(): return lax.ppermute(value, RING, pairs)  9.3 us
    pallas_call x2, Pallas kernels, pack(): pl.pallas_call(functools.partial(pack_kernel, jobs, step, start), grid=(B...  8.17 us
    pallas_call x4, Pallas kernels, relay(): pl.pallas_call(kernel, grid=(1,), out_shape=[kept(shape, BF16)] * kinds +...  4.36 us
  transfers between devices with their start and end apart: 34, of which 11 were waited for; matrix products, arithmetic and copies ran while one was open for 0% of the time, Pallas kernels for 45%

commit v1 on v0

--- a/solution.py
+++ b/solution.py
@@ -155,11 +155,14 @@
     qbuf, gbuf, kbuf, vbuf, kt, vt, dk_t, dv_t, s_buf, p_buf, ds_buf, ot = rest[4:]
     targets = {"k": kbuf, "v": vbuf, "q": qbuf, "g": gbuf}
     step = tile // BLOCKS
-    for n, at, kind, slab, e in loads:
-        for g in range(BLOCKS):
-            targets[kind][slab, pl.ds(e * tile + g * step, step)] = inputs[n][
-                0, g, pl.ds(at * step, step)
-            ]
+
+    def load(g, carry):
+        for n, at, kind, slab, e in loads:
+            to = pl.ds(pl.multiple_of(e * tile + g * step, step), step)
+            targets[kind][slab, to] = inputs[n][0, g, pl.ds(at * step, step)]
+        return carry
+
+    lax.fori_loop(0, BLOCKS, load, 0)
     width = rows * tile
     team = slabs_here * rows
     places = kbuf.shape[0]
@@ -253,20 +256,29 @@
                     backward(a, b)
             return tuple(tops), tuple(totals)
 
-        tops, totals = lax.fori_loop(0, 3, blocks, (tuple(tops), tuple(totals)))
+        carry = (tuple(tops), tuple(totals))
+        if turn in (0, 3):
+            for b in range(3):
+                carry = blocks(b, carry)
+        else:
+            carry = lax.fori_loop(0, 3, blocks, carry)
+        tops, totals = carry
         for a in here:
             if turn - a == 1:
                 between(a, totals[a])
             elif turn - a == 2:
                 after(a)
 
-    for n, sums in enumerate((dk_t, dv_t)):
-        for d in range(team):
-            local[d, n] = sums[d // rows, :, pl.ds(d % rows * tile, tile)].T
-        for m, grads in enumerate((grads_one, grads_two)):
-            for e in range(rows):
-                terms = sums[slabs_here + m, :, pl.ds(e * tile, tile)]
-                grads[e, n] = terms.astype(BF16).T
+    def give(e, carry):
+        at = pl.ds(pl.multiple_of(e * tile, tile), tile)
+        for n, sums in enumerate((dk_t, dv_t)):
+            for a in range(slabs_here):
+                local[a * rows + e, n] = sums[a, :, at].T
+            for m, grads in enumerate((grads_one, grads_two)):
+                grads[e, n] = sums[slabs_here + m, :, at].astype(BF16).T
+        return carry
+
+    lax.fori_loop(0, rows, give, 0)
 
 
 def attend(rows, tile, slabs_here, table, loads, inputs, spare):

time: 187 us -> 185 us (0.989)
  Pallas kernels: 87.9 us -> 85 us
    pallas_call x4, Pallas kernels: 65 us -> 62.1 us  [attend(): pl.pallas_call(functools.partial(attend_kernel, plan, rows, tile), grid=(...]
  transfers between devices with their start and end apart: 34 -> 34, of which waited for: 11 -> 11; matrix products, arithmetic and copies ran while one was open for 0% -> 0% of each run, Pallas kernels for 45% -> 44%
where the time goes in v1:
time: 185 us; the launch traced here: 184 us
  Pallas kernels  85 us (46%)
  starting transfers between devices  53.2 us (29%)
  waiting for transfers between devices  42.8 us (23%)
    pallas_call x4, Pallas kernels, attend(): pl.pallas_call(functools.partial(attend_kernel, plan, rows, tile), grid=(...  62.1 us
    ppermute x12, starting transfers between devices, shift(): return lax.ppermute(value, RING, pairs)  34.3 us
    ppermute x22, waiting for transfers between devices, swap(): lax.ppermute(value, RING, [(i, i - i % team + (i % team ^ d)) for i in ra...  33.5 us
    ppermute x22, starting transfers between devices, swap(): lax.ppermute(value, RING, [(i, i - i % team + (i % team ^ d)) for i in ra...  18.8 us
    pallas_call x4, Pallas kernels, unpack(): pl.pallas_call(kernel, grid=(BLOCKS,), out_shape=[struct(shape, BF16)] *...  9.55 us
    ppermute x12, waiting for transfers between devices, shift(): return lax.ppermute(value, RING, pairs)  9.31 us
    pallas_call x2, Pallas kernels, pack(): pl.pallas_call(functools.partial(pack_kernel, jobs, step, start), grid=(B...  8.17 us
    pallas_call x4, Pallas kernels, relay(): pl.pallas_call(kernel, grid=(1,), out_shape=[kept(shape, BF16)] * kinds +...  4.36 us
  transfers between devices with their start and end apart: 34, of which 11 were waited for; matrix products, arithmetic and copies ran while one was open for 0% of the time, Pallas kernels for 44%

profile of v1, /device:TPU:0, one launch (start us, length us, event | category | flops | bytes accessed | tf_op | source)
XLA Modules:
  0.0 184.0 jit_solution(16138868682516095676)
XLA Ops:
  1.3 0.7 fusion.3
  2.0 0.1 fusion.1
  2.1 2.5 %pack.2 = (bf16[1,4,400,128]{3,2,1,0:T(8,128)(2,1)S(1)}, bf16[1,4,400,128]{3,2,1,0:T(8,128)(2,1)S(1)}, bf16[1,4,400,128]{3,2,1,0:T(8,128)(2,1)S(1)}, bf16[1,4,400,128]{3,2,1,0:T(8,128)(2,1)S(1)}) custom-call(s32[4]{0:T(128)S(1)} %iota_xor_fusion.places_ref, s32[6]{0:T(128)S(1)} %convert_element_type.10.flags_ref, bf16[1,384,2048]{2,1,0:T(8,128)(2,1)} %refs_0_.3, ...), custom_call_target="tpu_custom_call" | custom-call | bytes 3276800 | tf_op jit(solution)/shard_map/pack/pallas_call | solution.py:67
  4.7 0.5 collective-permute-start
  5.2 2.6 %collective-permute-start.1 = (bf16[1,4,400,128]{3,2,1,0:T(8,128)(2,1)S(1)}, bf16[1,4,400,128]{3,2,1,0:T(8,128)(2,1)}, u32[]{:S(2)}, u32[]{:S(2)}) collective-permute-start(bf16[1,4,400,128]{3,2,1,0:T(8,128)(2,1)S(1)} %get-tuple-element.71), channel_id=1, source_target_pairs={{0,2},{1,3},{2,0},{3,1},{4,6},{5,7},{6,4},{7,5},{8,10},{9,11},{10,... | collective-permute-start | bytes 1228808 | tf_op jit(solution)/shard_map/ppermute | solution.py:423
  7.8 5.6 %pack.3 = (bf16[1,4,384,128]{3,2,1,0:T(8,128)(2,1)}, bf16[1,4,384,128]{3,2,1,0:T(8,128)(2,1)}, bf16[1,4,384,128]{3,2,1,0:T(8,128)(2,1)}, bf16[1,4,384,128]{3,2,1...) custom-call(s32[4]{0:T(128)S(1)} %iota_xor_fusion.places_ref, ...), custom_call_target="tpu_custom_call" | custom-call | bytes 9437184 | tf_op jit(solution)/shard_map/pack/pallas_call | solution.py:67
  13.5 0.2 collective-permute-start.3
  13.7 1.7 collective-permute-start.7
  15.4 0.3 collective-permute-start.6
  15.7 2.5 %collective-permute-done.1.refs_2_.refs_6_ = bf16[1,4,400,128]{3,2,1,0:T(8,128)(2,1)} collective-permute-done((bf16[1,4,400,128]{3,2,1,0:T(8,128)(2,1)S(1)}, bf16[1,4,400,128]{3,2,1,0:T(8,128)(2,1)}, u32[]{:S(2)}, u32[]{:S(2)}) %collective-permute-start.1) | collective-permute-done | bytes 409632 | tf_op jit(solution)/shard_map/ppermute | solution.py:423
  18.2 8.3 %collective-permute-done.2.refs_3_.refs_7_ = bf16[1,4,400,128]{3,2,1,0:T(8,128)(2,1)} collective-permute-done((bf16[1,4,400,128]{3,2,1,0:T(8,128)(2,1)S(1)}, bf16[1,4,400,128]{3,2,1,0:T(8,128)(2,1)}, u32[]{:S(2)}, u32[]{:S(2)}) %collective-permute-start.2) | collective-permute-done | bytes 409632 | tf_op jit(solution)/shard_map/ppermute | solution.py:423
  26.4 2.1 %relay.4 = (bf16[1,4,384,128]{3,2,1,0:T(8,128)(2,1)}, bf16[1,4,384,128]{3,2,1,0:T(8,128)(2,1)}, bf16[4,16,128]{2,1,0:T(8,128)(2,1)S(1)}) custom-call(bf16[1,4,400,128]{3,2,1,0:T(8,128)(2,1)S(1)} %get-tuple-element.69.refs_0_.refs_4_, bf16[1,4,400,128]{3,2,1,0:T(8,128)(2,1)S(1)} %collective-permute-done.refs_4_.refs_1_.refs_5_, ...), custom_call_target="tpu_custom_call" | custom-call | bytes 1572864 | tf_op jit(solution)/shard_map/relay/pallas_call | solution.py:116
  28.5 0.1 copy.29
  28.7 4.3 %collective-permute-start.13 = (bf16[1,4,384,128]{3,2,1,0:T(8,128)(2,1)}, bf16[1,4,384,128]{3,2,1,0:T(8,128)(2,1)}, u32[]{:S(2)}, u32[]{:S(2)}) collective-permute-start(bf16[1,4,384,128]{3,2,1,0:T(8,128)(2,1)} %get-tuple-element.85), channel_id=1, source_target_pairs={{0,4},{1,5},{4,8},{5,9},{6,2},{7,3},{8,12},{9,13},{10,6},{11,7},{1... | collective-permute-start | bytes 1179656 | tf_op jit(solution)/shard_map/ppermute | solution.py:435
  33.0 1.3 collective-permute-start.12
  34.4 0.1 pad_add_fusion
  34.5 0.1 copy.30
  34.6 0.2 collective-permute-done.7.refs_3_
  34.9 2.3 %collective-permute-start.10 = (bf16[1,4,384,128]{3,2,1,0:T(8,128)(2,1)}, bf16[1,4,384,128]{3,2,1,0:T(8,128)(2,1)S(1)}, u32[]{:S(2)}, u32[]{:S(2)}) collective-permute-start(bf16[1,4,384,128]{3,2,1,0:T(8,128)(2,1)} %get-tuple-element.83), channel_id=1, source_target_pairs={{0,2},{1,3},{2,0},{3,1},{4,6},{5,7},{6,4},{7,5},{8,10},{9,11},{10,... | collective-permute-start | bytes 1179656 | tf_op jit(solution)/shard_map/ppermute | solution.py:423
  37.2 6.6 %collective-permute-done.6.refs_2_ = bf16[1,4,384,128]{3,2,1,0:T(8,128)(2,1)} collective-permute-done((bf16[1,4,384,128]{3,2,1,0:T(8,128)(2,1)}, bf16[1,4,384,128]{3,2,1,0:T(8,128)(2,1)}, u32[]{:S(2)}, u32[]{:S(2)}) %collective-permute-start.6) | collective-permute-done | bytes 393248 | tf_op jit(solution)/shard_map/ppermute | solution.py:423
  43.8 0.8 collective-permute-start.11
  44.6 2.0 %relay.5 = (bf16[1,4,384,128]{3,2,1,0:T(8,128)(2,1)}, bf16[1,4,384,128]{3,2,1,0:T(8,128)(2,1)}) custom-call(bf16[3,4,384,128]{3,2,1,0:T(8,128)(2,1)S(1)} %copy-done, bf16[3,4,384,128]{3,2,1,0:T(8,128)(2,1)S(1)} %collective-permute-done.3.refs_1_, bf16[1,4,384,128]{3,2,1,0:T(8,128)(2,1)} %collective-permute-done.6.refs_2_, ...), custom_call_target="tpu_custom_call" | custom-call | bytes 1572864 | tf_op jit(solution)/shard_map/relay/pallas_call | solution.py:116
  46.5 3.5 %collective-permute-start.9 = (bf16[1,4,384,128]{3,2,1,0:T(8,128)(2,1)}, bf16[1,4,384,128]{3,2,1,0:T(8,128)(2,1)S(1)}, u32[]{:S(2)}, u32[]{:S(2)}) collective-permute-start(bf16[1,4,384,128]{3,2,1,0:T(8,128)(2,1)} %get-tuple-element.82), channel_id=1, source_target_pairs={{0,4},{1,5},{4,8},{5,9},{6,2},{7,3},{8,12},{9,13},{10,6},{11,7},{1... | collective-permute-start | bytes 1179656 | tf_op jit(solution)/shard_map/ppermute | solution.py:435
  50.0 1.3 collective-permute-start.8
  51.3 16.0 %attend.4 = (bf16[4,2,384,128]{3,2,1,0:T(8,128)(2,1)S(1)}, f32[4,2,384,128]{3,2,1,0:T(8,128)S(1)}, bf16[2,2,384,128]{3,2,1,0:T(8,128)(2,1)S(1)}, bf16[2,2,384,128]{3,2,1,0:T(8,128)(2,1)S(1)}) custom-call(s32[4,9]{1,0:T(4,128)S(1)} %pad_add_fusion.1.table_ref, bf16[1,4,400,128]{3,2,1,0:T(8,128)(2,1)S(1)} %get-tuple-element.69.refs_0_.refs_4_, ...), custom_call_target="tpu_custom_call" | custom-call | flops 5435817984 | bytes 8388608 | tf_op jit(solution)/shard_map/attend/pallas_call | solution.py:304
  67.4 0.2 relay.6
  67.6 4.7 %collective-permute-start.17 = (bf16[1,4,768,128]{3,2,1,0:T(8,128)(2,1)S(1)}, bf16[1,4,768,128]{3,2,1,0:T(8,128)(2,1)S(1)}, u32[]{:S(2)}, u32[]{:S(2)}) collective-permute-start(bf16[1,4,768,128]{3,2,1,0:T(8,128)(2,1)S(1)} %get-tuple-element.95), channel_id=1, source_target_pairs={{0,4},{1,5},{4,8},{5,9},{6,2},{7,3},{8,12},{9,13},{10,6},{11,7},{1... | collective-permute-start | bytes 2359304 | tf_op jit(solution)/shard_map/ppermute | solution.py:435
  72.3 1.5 collective-permute-start.16
  73.8 2.3 %collective-permute-start.4 = (bf16[1,4,384,128]{3,2,1,0:T(8,128)(2,1)S(1)}, bf16[1,4,384,128]{3,2,1,0:T(8,128)(2,1)S(1)}, u32[]{:S(2)}, u32[]{:S(2)}) collective-permute-start(bf16[1,4,384,128]{3,2,1,0:T(8,128)(2,1)S(1)} %copy-done.3), channel_id=1, source_target_pairs={{0,2},{1,3},{2,0},{3,1},{4,6},{5,7},{6,4},{7,5},{8,10},{9,11},{10,... | collective-permute-start | bytes 1179656 | tf_op jit(solution)/shard_map/ppermute | solution.py:423
  76.1 15.7 %attend.5 = (bf16[4,2,384,128]{3,2,1,0:T(8,128)(2,1)S(1)}, f32[4,2,384,128]{3,2,1,0:T(8,128)S(1)}, bf16[2,2,384,128]{3,2,1,0:T(8,128)(2,1)S(1)}, bf16[2,2,384,128]{3,2,1,0:T(8,128)(2,1)S(1)}) custom-call(s32[4,9]{1,0:T(4,128)S(1)} %pad_add_fusion.1.table_ref, bf16[3,4,384,128]{3,2,1,0:T(8,128)(2,1)S(1)} %copy-done, ...), custom_call_target="tpu_custom_call" | custom-call | flops 5435817984 | bytes 8388608 | tf_op jit(solution)/shard_map/attend/pallas_call | solution.py:304
  91.9 1.1 collective-permute-done.5.refs_3_
  93.0 0.2 relay.7
  93.2 4.2 %collective-permute-start.15 = (bf16[1,4,768,128]{3,2,1,0:T(8,128)(2,1)S(1)}, bf16[1,4,768,128]{3,2,1,0:T(8,128)(2,1)S(1)}, u32[]{:S(2)}, u32[]{:S(2)}) collective-permute-start(bf16[1,4,768,128]{3,2,1,0:T(8,128)(2,1)S(1)} %get-tuple-element.92), channel_id=1, source_target_pairs={{0,4},{1,5},{4,8},{5,9},{6,2},{7,3},{8,12},{9,13},{10,6},{11,7},{1... | collective-permute-start | bytes 2359304 | tf_op jit(solution)/shard_map/ppermute | solution.py:435
  97.5 1.5 collective-permute-start.14
  99.0 0.3 finish.4
  99.3 0.4 collective-permute-start.18
  99.6 1.2 collective-permute-start.19
  100.8 0.4 collective-permute-start.20
  101.2 15.2 %attend.6 = (bf16[4,2,384,128]{3,2,1,0:T(8,128)(2,1)S(1)}, f32[4,2,384,128]{3,2,1,0:T(8,128)S(1)}, bf16[2,2,384,128]{3,2,1,0:T(8,128)(2,1)S(1)}, bf16[2,2,384,128]{3,2,1,0:T(8,128)(2,1)S(1)}) custom-call(s32[4,9]{1,0:T(4,128)S(1)} %pad_add_fusion.1.table_ref, bf16[3,4,384,128]{3,2,1,0:T(8,128)(2,1)S(1)} %copy-done, ...), custom_call_target="tpu_custom_call" | custom-call | flops 5435817984 | bytes 8388608 | tf_op jit(solution)/shard_map/attend/pallas_call | solution.py:304
  116.4 4.6 %collective-permute-start.26 = (bf16[2,2,384,128]{3,2,1,0:T(8,128)(2,1)S(1)}, bf16[2,2,384,128]{3,2,1,0:T(8,128)(2,1)S(1)}, u32[]{:S(2)}, u32[]{:S(2)}) collective-permute-start(bf16[2,2,384,128]{3,2,1,0:T(8,128)(2,1)S(1)} %get-tuple-element.112), channel_id=1, source_target_pairs={{0,4},{1,5},{4,8},{5,9},{6,2},{7,3},{8,12},{9,13},{10,6},{11,7},{1... | collective-permute-start | bytes 1179656 | tf_op jit(solution)/shard_map/ppermute | solution.py:435
  121.0 1.6 collective-permute-start.27
  122.5 0.3 finish.5
  122.8 0.1 collective-permute-start.23
  123.0 1.1 collective-permute-start.24
  124.1 0.7 collective-permute-start.25
  124.8 15.2 %attend.7 = (bf16[4,2,384,128]{3,2,1,0:T(8,128)(2,1)S(1)}, f32[4,2,384,128]{3,2,1,0:T(8,128)S(1)}, bf16[2,2,384,128]{3,2,1,0:T(8,128)(2,1)S(1)}, bf16[2,2,384,128]{3,2,1,0:T(8,128)(2,1)S(1)}) custom-call(s32[4,9]{1,0:T(4,128)S(1)} %pad_add_fusion.1.table_ref, bf16[3,4,384,128]{3,2,1,0:T(8,128)(2,1)S(1)} %copy-done, ...), custom_call_target="tpu_custom_call" | custom-call | flops 5435817984 | bytes 8388608 | tf_op jit(solution)/shard_map/attend/pallas_call | solution.py:304
  140.0 4.6 %collective-permute-start.21 = (bf16[2,2,384,128]{3,2,1,0:T(8,128)(2,1)S(1)}, bf16[2,2,384,128]{3,2,1,0:T(8,128)(2,1)S(1)}, u32[]{:S(2)}, u32[]{:S(2)}) collective-permute-start(bf16[2,2,384,128]{3,2,1,0:T(8,128)(2,1)S(1)} %get-tuple-element.106), channel_id=1, source_target_pairs={{0,4},{1,5},{4,8},{5,9},{6,2},{7,3},{8,12},{9,13},{10,6},{11,7},{1... | collective-permute-start | bytes 1179656 | tf_op jit(solution)/shard_map/ppermute | solution.py:435
  144.6 1.3 collective-permute-start.22
  145.9 0.2 finish.6
  146.0 1.1 collective-permute-start.28
  147.1 1.1 collective-permute-start.33
  148.3 5.1 %collective-permute-done.21.refs_0_ = bf16[2,2,384,128]{3,2,1,0:T(8,128)(2,1)S(1)} collective-permute-done((bf16[2,2,384,128]{3,2,1,0:T(8,128)(2,1)S(1)}, bf16[2,2,384,128]{3,2,1,0:T(8,128)(2,1)S(1)}, u32[]{:S(2)}, u32[]{:S(2)}) %collective-permute-start.21) | collective-permute-done | bytes 393248 | tf_op jit(solution)/shard_map/ppermute | solution.py:435
  153.4 4.1 %collective-permute-done.22.refs_1_ = bf16[2,2,384,128]{3,2,1,0:T(8,128)(2,1)S(1)} collective-permute-done((bf16[2,2,384,128]{3,2,1,0:T(8,128)(2,1)S(1)}, bf16[2,2,384,128]{3,2,1,0:T(8,128)(2,1)S(1)}, u32[]{:S(2)}, u32[]{:S(2)}) %collective-permute-start.22) | collective-permute-done | bytes 393248 | tf_op jit(solution)/shard_map/ppermute | solution.py:435
  157.5 0.5 collective-permute-done.28.refs_6_.refs_2_
  158.1 0.2 finish.7
  158.3 1.1 collective-permute-start.30
  159.4 0.8 collective-permute-start.31
  160.2 2.4 %unpack.4 = (bf16[1,384,2048]{2,1,0:T(8,128)(2,1)}, bf16[1,384,2048]{2,1,0:T(8,128)(2,1)}, bf16[1,384,2048]{2,1,0:T(8,128)(2,1)}, bf16[1,384,2048]{2,1,0:T(8,128)(2,1)}) custom-call(s32[4]{0:T(128)S(1)} %iota_xor_fusion.places_ref, bf16[1,4,384,128]{3,2,1,0:T(8,128)(2,1)S(1)} %get-tuple-element.98.refs_7_.refs_0_, ...), custom_call_target="tpu_custom_call" | custom-call | bytes 3145728 | tf_op jit(solution)/shard_map/unpack/pallas_call | solution.py:390
  162.6 2.4 %unpack.5 = (bf16[1,384,2048]{2,1,0:T(8,128)(2,1)}, bf16[1,384,2048]{2,1,0:T(8,128)(2,1)}, bf16[1,384,2048]{2,1,0:T(8,128)(2,1)}, bf16[1,384,2048]{2,1,0:T(8,128)(2,1)}) custom-call(s32[4]{0:T(128)S(1)} %iota_xor_fusion.places_ref, ...), custom_call_target="tpu_custom_call", output_to_operand_aliasing={{0}: (5, {}), {1}: (6, {}), {2}: (7, {}), {3}: (8, {})} | custom-call | bytes 3145728 | tf_op jit(solution)/shard_map/unpack/pallas_call | solution.py:390
  165.0 0.1 collective-permute-done.33.refs_3_
  165.1 2.4 %unpack.6 = (bf16[1,384,2048]{2,1,0:T(8,128)(2,1)}, bf16[1,384,2048]{2,1,0:T(8,128)(2,1)}, bf16[1,384,2048]{2,1,0:T(8,128)(2,1)}, bf16[1,384,2048]{2,1,0:T(8,128)(2,1)}) custom-call(s32[4]{0:T(128)S(1)} %iota_xor_fusion.places_ref, ...), custom_call_target="tpu_custom_call", output_to_operand_aliasing={{0}: (5, {}), {1}: (6, {}), {2}: (7, {}), {3}: (8, {})} | custom-call | bytes 3145728 | tf_op jit(solution)/shard_map/unpack/pallas_call | solution.py:390
  167.5 7.5 %collective-permute-done.30.refs_2_ = bf16[1,4,384,128]{3,2,1,0:T(8,128)(2,1)S(1)} collective-permute-done((bf16[1,4,384,128]{3,2,1,0:T(8,128)(2,1)S(1)}, bf16[1,4,384,128]{3,2,1,0:T(8,128)(2,1)S(1)}, u32[]{:S(2)}, u32[]{:S(2)}) %collective-permute-start.30) | collective-permute-done | bytes 393248 | tf_op jit(solution)/shard_map/ppermute | solution.py:423
  174.9 6.7 %collective-permute-done.31.refs_3_ = bf16[1,4,384,128]{3,2,1,0:T(8,128)(2,1)S(1)} collective-permute-done((bf16[1,4,384,128]{3,2,1,0:T(8,128)(2,1)S(1)}, bf16[1,4,384,128]{3,2,1,0:T(8,128)(2,1)S(1)}, u32[]{:S(2)}, u32[]{:S(2)}) %collective-permute-start.31) | collective-permute-done | bytes 393248 | tf_op jit(solution)/shard_map/ppermute | solution.py:423
  181.6 2.4 %unpack.7 = (bf16[1,384,2048]{2,1,0:T(8,128)(2,1)}, bf16[1,384,2048]{2,1,0:T(8,128)(2,1)}, bf16[1,384,2048]{2,1,0:T(8,128)(2,1)}, bf16[1,384,2048]{2,1,0:T(8,128)(2,1)}) custom-call(s32[4]{0:T(128)S(1)} %iota_xor_fusion.places_ref, ...), custom_call_target="tpu_custom_call", output_to_operand_aliasing={{0}: (5, {}), {1}: (6, {}), {2}: (7, {}), {3}: (8, {})} | custom-call | bytes 3145728 | tf_op jit(solution)/shard_map/unpack/pallas_call | solution.py:390
  (47 shorter events, 0.5 us)
Async XLA Ops:
  4.7 3.2 %collective-permute-start = (bf16[1,4,400,128]{3,2,1,0:T(8,128)(2,1)S(1)}, bf16[1,4,400,128]{3,2,1,0:T(8,128)(2,1)S(1)}, u32[]{:S(2)}, u32[]{:S(2)}) collective-permute-start(bf16[1,4,400,128]{3,2,1,0:T(8,128)(2,1)S(1)} %get-tuple-element.70), channel_id=1, source_target_pairs={{0,1},{1,0},{2,3},{3,2},{4,5},{5,4},{6,7},{7,6},{8,9},{9,8},{10,11... | collective-permute-start | bytes 1228808 | tf_op jit(solution)/shard_map/ppermute | solution.py:423
  5.2 13.0 %collective-permute-start.1 = (bf16[1,4,400,128]{3,2,1,0:T(8,128)(2,1)S(1)}, bf16[1,4,400,128]{3,2,1,0:T(8,128)(2,1)}, u32[]{:S(2)}, u32[]{:S(2)}) collective-permute-start(bf16[1,4,400,128]{3,2,1,0:T(8,128)(2,1)S(1)} %get-tuple-element.71), channel_id=1, source_target_pairs={{0,2},{1,3},{2,0},{3,1},{4,6},{5,7},{6,4},{7,5},{8,10},{9,11},{10,... | collective-permute-start | bytes 1228808 | tf_op jit(solution)/shard_map/ppermute | solution.py:423
  7.7 18.7 %collective-permute-start.2 = (bf16[1,4,400,128]{3,2,1,0:T(8,128)(2,1)S(1)}, bf16[1,4,400,128]{3,2,1,0:T(8,128)(2,1)}, u32[]{:S(2)}, u32[]{:S(2)}) collective-permute-start(bf16[1,4,400,128]{3,2,1,0:T(8,128)(2,1)S(1)} %get-tuple-element.72), channel_id=1, source_target_pairs={{0,3},{1,2},{2,1},{3,0},{4,7},{5,6},{6,5},{7,4},{8,11},{9,10},{10,... | collective-permute-start | bytes 1228808 | tf_op jit(solution)/shard_map/ppermute | solution.py:423
  13.5 31.1 %collective-permute-start.3 = (bf16[3,4,384,128]{3,2,1,0:T(8,128)(2,1)}, bf16[3,4,384,128]{3,2,1,0:T(8,128)(2,1)S(1)}, u32[]{:S(2)}, u32[]{:S(2)}) collective-permute-start(bf16[3,4,384,128]{3,2,1,0:T(8,128)(2,1)} %get-tuple-element.76), channel_id=1, source_target_pairs={{0,1},{1,0},{2,3},{3,2},{4,5},{5,4},{6,7},{7,6},{8,9},{9,8},{10,11... | collective-permute-start | bytes 3538952 | tf_op jit(solution)/shard_map/ppermute | solution.py:423
  13.7 21.2 %collective-permute-start.7 = (bf16[1,4,384,128]{3,2,1,0:T(8,128)(2,1)}, bf16[1,4,384,128]{3,2,1,0:T(8,128)(2,1)}, u32[]{:S(2)}, u32[]{:S(2)}) collective-permute-start(bf16[1,4,384,128]{3,2,1,0:T(8,128)(2,1)} %get-tuple-element.79), channel_id=1, source_target_pairs={{0,3},{1,2},{2,1},{3,0},{4,7},{5,6},{6,5},{7,4},{8,11},{9,10},{10,... | collective-permute-start | bytes 1179656 | tf_op jit(solution)/shard_map/ppermute | solution.py:423
  15.4 28.4 %collective-permute-start.6 = (bf16[1,4,384,128]{3,2,1,0:T(8,128)(2,1)}, bf16[1,4,384,128]{3,2,1,0:T(8,128)(2,1)}, u32[]{:S(2)}, u32[]{:S(2)}) collective-permute-start(bf16[1,4,384,128]{3,2,1,0:T(8,128)(2,1)} %get-tuple-element.73.refs_8_), channel_id=1, source_target_pairs={{0,2},{1,3},{2,0},{3,1},{4,6},{5,7},{6,4},{7,5},{8,10},{9,11},{10,... | collective-permute-start | bytes 1179656 | tf_op jit(solution)/shard_map/ppermute | solution.py:423
  26.4 8.1 %copy-start.1 = (s32[2,3]{1,0:T(2,128)S(1)}, s32[2,3]{1,0:T(2,128)}, u32[]{:S(2)}) copy-start(s32[2,3]{1,0:T(2,128)} %constant.47.clone) | copy-start | bytes 76
  26.4 18.1 %copy-start = (bf16[3,4,384,128]{3,2,1,0:T(8,128)(2,1)S(1)}, bf16[3,4,384,128]{3,2,1,0:T(8,128)(2,1)}, u32[]{:S(2)}) copy-start(bf16[3,4,384,128]{3,2,1,0:T(8,128)(2,1)} %get-tuple-element.75.refs_0_) | copy-start | bytes 3538948
  28.7 21.4 %collective-permute-start.13 = (bf16[1,4,384,128]{3,2,1,0:T(8,128)(2,1)}, bf16[1,4,384,128]{3,2,1,0:T(8,128)(2,1)}, u32[]{:S(2)}, u32[]{:S(2)}) collective-permute-start(bf16[1,4,384,128]{3,2,1,0:T(8,128)(2,1)} %get-tuple-element.85), channel_id=1, source_target_pairs={{0,4},{1,5},{4,8},{5,9},{6,2},{7,3},{8,12},{9,13},{10,6},{11,7},{1... | collective-permute-start | bytes 1179656 | tf_op jit(solution)/shard_map/ppermute | solution.py:435
  33.0 18.3 %collective-permute-start.12 = (bf16[1,4,384,128]{3,2,1,0:T(8,128)(2,1)}, bf16[1,4,384,128]{3,2,1,0:T(8,128)(2,1)}, u32[]{:S(2)}, u32[]{:S(2)}) collective-permute-start(bf16[1,4,384,128]{3,2,1,0:T(8,128)(2,1)} %get-tuple-element.80.refs_4_), channel_id=1, source_target_pairs={{2,6},{3,7},{4,0},{5,1},{6,10},{7,11},{8,4},{9,5},{10,14},{11,15},... | collective-permute-start | bytes 1179656 | tf_op jit(solution)/shard_map/ppermute | solution.py:435
  34.9 32.5 %collective-permute-start.10 = (bf16[1,4,384,128]{3,2,1,0:T(8,128)(2,1)}, bf16[1,4,384,128]{3,2,1,0:T(8,128)(2,1)S(1)}, u32[]{:S(2)}, u32[]{:S(2)}) collective-permute-start(bf16[1,4,384,128]{3,2,1,0:T(8,128)(2,1)} %get-tuple-element.83), channel_id=1, source_target_pairs={{0,2},{1,3},{2,0},{3,1},{4,6},{5,7},{6,4},{7,5},{8,10},{9,11},{10,... | collective-permute-start | bytes 1179656 | tf_op jit(solution)/shard_map/ppermute | solution.py:423
  43.8 23.6 %collective-permute-start.11 = (bf16[1,4,384,128]{3,2,1,0:T(8,128)(2,1)}, bf16[1,4,384,128]{3,2,1,0:T(8,128)(2,1)S(1)}, u32[]{:S(2)}, u32[]{:S(2)}) collective-permute-start(bf16[1,4,384,128]{3,2,1,0:T(8,128)(2,1)} %get-tuple-element.84), channel_id=1, source_target_pairs={{0,3},{1,2},{2,1},{3,0},{4,7},{5,6},{6,5},{7,4},{8,11},{9,10},{10,... | collective-permute-start | bytes 1179656 | tf_op jit(solution)/shard_map/ppermute | solution.py:423
  46.5 29.6 %collective-permute-start.9 = (bf16[1,4,384,128]{3,2,1,0:T(8,128)(2,1)}, bf16[1,4,384,128]{3,2,1,0:T(8,128)(2,1)S(1)}, u32[]{:S(2)}, u32[]{:S(2)}) collective-permute-start(bf16[1,4,384,128]{3,2,1,0:T(8,128)(2,1)} %get-tuple-element.82), channel_id=1, source_target_pairs={{0,4},{1,5},{4,8},{5,9},{6,2},{7,3},{8,12},{9,13},{10,6},{11,7},{1... | collective-permute-start | bytes 1179656 | tf_op jit(solution)/shard_map/ppermute | solution.py:435
  50.0 26.1 %collective-permute-start.8 = (bf16[1,4,384,128]{3,2,1,0:T(8,128)(2,1)}, bf16[1,4,384,128]{3,2,1,0:T(8,128)(2,1)S(1)}, u32[]{:S(2)}, u32[]{:S(2)}) collective-permute-start(bf16[1,4,384,128]{3,2,1,0:T(8,128)(2,1)} %get-tuple-element.81.refs_6_), channel_id=1, source_target_pairs={{2,6},{3,7},{4,0},{5,1},{6,10},{7,11},{8,4},{9,5},{10,14},{11,15},... | collective-permute-start | bytes 1179656 | tf_op jit(solution)/shard_map/ppermute | solution.py:435
  67.4 6.4 %copy-start.3 = (bf16[1,4,384,128]{3,2,1,0:T(8,128)(2,1)S(1)}, bf16[1,4,384,128]{3,2,1,0:T(8,128)(2,1)}, u32[]{:S(2)}) copy-start(bf16[1,4,384,128]{3,2,1,0:T(8,128)(2,1)} %get-tuple-element.77) | copy-start | bytes 1179652
  67.4 8.7 %copy-start.2 = (bf16[1,4,384,128]{3,2,1,0:T(8,128)(2,1)S(1)}, bf16[1,4,384,128]{3,2,1,0:T(8,128)(2,1)}, u32[]{:S(2)}) copy-start(bf16[1,4,384,128]{3,2,1,0:T(8,128)(2,1)} %get-tuple-element.78) | copy-start | bytes 1179652
  67.6 31.4 %collective-permute-start.17 = (bf16[1,4,768,128]{3,2,1,0:T(8,128)(2,1)S(1)}, bf16[1,4,768,128]{3,2,1,0:T(8,128)(2,1)S(1)}, u32[]{:S(2)}, u32[]{:S(2)}) collective-permute-start(bf16[1,4,768,128]{3,2,1,0:T(8,128)(2,1)S(1)} %get-tuple-element.95), channel_id=1, source_target_pairs={{0,4},{1,5},{4,8},{5,9},{6,2},{7,3},{8,12},{9,13},{10,6},{11,7},{1... | collective-permute-start | bytes 2359304 | tf_op jit(solution)/shard_map/ppermute | solution.py:435
  72.3 26.7 %collective-permute-start.16 = (bf16[1,4,768,128]{3,2,1,0:T(8,128)(2,1)S(1)}, bf16[1,4,768,128]{3,2,1,0:T(8,128)(2,1)S(1)}, u32[]{:S(2)}, u32[]{:S(2)}) collective-permute-start(bf16[1,4,768,128]{3,2,1,0:T(8,128)(2,1)S(1)} %get-tuple-element.88.refs_6_), channel_id=1, source_target_pairs={{2,6},{3,7},{4,0},{5,1},{6,10},{7,11},{8,4},{9,5},{10,14},{11,15},... | collective-permute-start | bytes 2359304 | tf_op jit(solution)/shard_map/ppermute | solution.py:435
  73.8 18.1 %collective-permute-start.4 = (bf16[1,4,384,128]{3,2,1,0:T(8,128)(2,1)S(1)}, bf16[1,4,384,128]{3,2,1,0:T(8,128)(2,1)S(1)}, u32[]{:S(2)}, u32[]{:S(2)}) collective-permute-start(bf16[1,4,384,128]{3,2,1,0:T(8,128)(2,1)S(1)} %copy-done.3), channel_id=1, source_target_pairs={{0,2},{1,3},{2,0},{3,1},{4,6},{5,7},{6,4},{7,5},{8,10},{9,11},{10,... | collective-permute-start | bytes 1179656 | tf_op jit(solution)/shard_map/ppermute | solution.py:423
  76.1 16.9 %collective-permute-start.5 = (bf16[1,4,384,128]{3,2,1,0:T(8,128)(2,1)S(1)}, bf16[1,4,384,128]{3,2,1,0:T(8,128)(2,1)S(1)}, u32[]{:S(2)}, u32[]{:S(2)}) collective-permute-start(bf16[1,4,384,128]{3,2,1,0:T(8,128)(2,1)S(1)} %copy-done.2), channel_id=1, source_target_pairs={{0,3},{1,2},{2,1},{3,0},{4,7},{5,6},{6,5},{7,4},{8,11},{9,10},{10,... | collective-permute-start | bytes 1179656 | tf_op jit(solution)/shard_map/ppermute | solution.py:423
  93.2 23.2 %collective-permute-start.15 = (bf16[1,4,768,128]{3,2,1,0:T(8,128)(2,1)S(1)}, bf16[1,4,768,128]{3,2,1,0:T(8,128)(2,1)S(1)}, u32[]{:S(2)}, u32[]{:S(2)}) collective-permute-start(bf16[1,4,768,128]{3,2,1,0:T(8,128)(2,1)S(1)} %get-tuple-element.92), channel_id=1, source_target_pairs={{0,4},{1,5},{4,8},{5,9},{6,2},{7,3},{8,12},{9,13},{10,6},{11,7},{1... | collective-permute-start | bytes 2359304 | tf_op jit(solution)/shard_map/ppermute | solution.py:435
  97.5 23.5 %collective-permute-start.14 = (bf16[1,4,768,128]{3,2,1,0:T(8,128)(2,1)S(1)}, bf16[1,4,768,128]{3,2,1,0:T(8,128)(2,1)S(1)}, u32[]{:S(2)}, u32[]{:S(2)}) collective-permute-start(bf16[1,4,768,128]{3,2,1,0:T(8,128)(2,1)S(1)} %get-tuple-element.91.refs_6_), channel_id=1, source_target_pairs={{2,6},{3,7},{4,0},{5,1},{6,10},{7,11},{8,4},{9,5},{10,14},{11,15},... | collective-permute-start | bytes 2359304 | tf_op jit(solution)/shard_map/ppermute | solution.py:435
  99.3 23.6 %collective-permute-start.18 = (bf16[1,4,384,128]{3,2,1,0:T(8,128)(2,1)S(1)}, bf16[1,4,384,128]{3,2,1,0:T(8,128)(2,1)S(1)}, u32[]{:S(2)}, u32[]{:S(2)}) collective-permute-start(bf16[1,4,384,128]{3,2,1,0:T(8,128)(2,1)S(1)} %get-tuple-element.101), channel_id=1, source_target_pairs={{0,1},{1,0},{2,3},{3,2},{4,5},{5,4},{6,7},{7,6},{8,9},{9,8},{10,11... | collective-permute-start | bytes 1179656 | tf_op jit(solution)/shard_map/ppermute | solution.py:423
  99.6 23.3 %collective-permute-start.19 = (bf16[1,4,384,128]{3,2,1,0:T(8,128)(2,1)S(1)}, bf16[1,4,384,128]{3,2,1,0:T(8,128)(2,1)S(1)}, u32[]{:S(2)}, u32[]{:S(2)}) collective-permute-start(bf16[1,4,384,128]{3,2,1,0:T(8,128)(2,1)S(1)} %get-tuple-element.102), channel_id=1, source_target_pairs={{0,2},{1,3},{2,0},{3,1},{4,6},{5,7},{6,4},{7,5},{8,10},{9,11},{10,... | collective-permute-start | bytes 1179656 | tf_op jit(solution)/shard_map/ppermute | solution.py:423
  100.8 23.3 %collective-permute-start.20 = (bf16[1,4,384,128]{3,2,1,0:T(8,128)(2,1)S(1)}, bf16[1,4,384,128]{3,2,1,0:T(8,128)(2,1)S(1)}, u32[]{:S(2)}, u32[]{:S(2)}) collective-permute-start(bf16[1,4,384,128]{3,2,1,0:T(8,128)(2,1)S(1)} %get-tuple-element.103), channel_id=1, source_target_pairs={{0,3},{1,2},{2,1},{3,0},{4,7},{5,6},{6,5},{7,4},{8,11},{9,10},{10,... | collective-permute-start | bytes 1179656 | tf_op jit(solution)/shard_map/ppermute | solution.py:423
  116.4 23.6 %collective-permute-start.26 = (bf16[2,2,384,128]{3,2,1,0:T(8,128)(2,1)S(1)}, bf16[2,2,384,128]{3,2,1,0:T(8,128)(2,1)S(1)}, u32[]{:S(2)}, u32[]{:S(2)}) collective-permute-start(bf16[2,2,384,128]{3,2,1,0:T(8,128)(2,1)S(1)} %get-tuple-element.112), channel_id=1, source_target_pairs={{0,4},{1,5},{4,8},{5,9},{6,2},{7,3},{8,12},{9,13},{10,6},{11,7},{1... | collective-permute-start | bytes 1179656 | tf_op jit(solution)/shard_map/ppermute | solution.py:435
  121.0 23.6 %collective-permute-start.27 = (bf16[2,2,384,128]{3,2,1,0:T(8,128)(2,1)S(1)}, bf16[2,2,384,128]{3,2,1,0:T(8,128)(2,1)S(1)}, u32[]{:S(2)}, u32[]{:S(2)}) collective-permute-start(bf16[2,2,384,128]{3,2,1,0:T(8,128)(2,1)S(1)} %get-tuple-element.113), channel_id=1, source_target_pairs={{2,6},{3,7},{4,0},{5,1},{6,10},{7,11},{8,4},{9,5},{10,14},{11,15},... | collective-permute-start | bytes 1179656 | tf_op jit(solution)/shard_map/ppermute | solution.py:435
  122.8 23.2 %collective-permute-start.23 = (bf16[1,4,384,128]{3,2,1,0:T(8,128)(2,1)S(1)}, bf16[1,4,384,128]{3,2,1,0:T(8,128)(2,1)S(1)}, u32[]{:S(2)}, u32[]{:S(2)}) collective-permute-start(bf16[1,4,384,128]{3,2,1,0:T(8,128)(2,1)S(1)} %get-tuple-element.108), channel_id=1, source_target_pairs={{0,1},{1,0},{2,3},{3,2},{4,5},{5,4},{6,7},{7,6},{8,9},{9,8},{10,11... | collective-permute-start | bytes 1179656 | tf_op jit(solution)/shard_map/ppermute | solution.py:423
  123.0 24.2 %collective-permute-start.24 = (bf16[1,4,384,128]{3,2,1,0:T(8,128)(2,1)S(1)}, bf16[1,4,384,128]{3,2,1,0:T(8,128)(2,1)S(1)}, u32[]{:S(2)}, u32[]{:S(2)}) collective-permute-start(bf16[1,4,384,128]{3,2,1,0:T(8,128)(2,1)S(1)} %get-tuple-element.109), channel_id=1, source_target_pairs={{0,2},{1,3},{2,0},{3,1},{4,6},{5,7},{6,4},{7,5},{8,10},{9,11},{10,... | collective-permute-start | bytes 1179656 | tf_op jit(solution)/shard_map/ppermute | solution.py:423
  124.1 23.0 %collective-permute-start.25 = (bf16[1,4,384,128]{3,2,1,0:T(8,128)(2,1)S(1)}, bf16[1,4,384,128]{3,2,1,0:T(8,128)(2,1)S(1)}, u32[]{:S(2)}, u32[]{:S(2)}) collective-permute-start(bf16[1,4,384,128]{3,2,1,0:T(8,128)(2,1)S(1)} %get-tuple-element.110), channel_id=1, source_target_pairs={{0,3},{1,2},{2,1},{3,0},{4,7},{5,6},{6,5},{7,4},{8,11},{9,10},{10,... | collective-permute-start | bytes 1179656 | tf_op jit(solution)/shard_map/ppermute | solution.py:423
  140.0 13.4 %collective-permute-start.21 = (bf16[2,2,384,128]{3,2,1,0:T(8,128)(2,1)S(1)}, bf16[2,2,384,128]{3,2,1,0:T(8,128)(2,1)S(1)}, u32[]{:S(2)}, u32[]{:S(2)}) collective-permute-start(bf16[2,2,384,128]{3,2,1,0:T(8,128)(2,1)S(1)} %get-tuple-element.106), channel_id=1, source_target_pairs={{0,4},{1,5},{4,8},{5,9},{6,2},{7,3},{8,12},{9,13},{10,6},{11,7},{1... | collective-permute-start | bytes 1179656 | tf_op jit(solution)/shard_map/ppermute | solution.py:435
  144.6 13.0 %collective-permute-start.22 = (bf16[2,2,384,128]{3,2,1,0:T(8,128)(2,1)S(1)}, bf16[2,2,384,128]{3,2,1,0:T(8,128)(2,1)S(1)}, u32[]{:S(2)}, u32[]{:S(2)}) collective-permute-start(bf16[2,2,384,128]{3,2,1,0:T(8,128)(2,1)S(1)} %get-tuple-element.107), channel_id=1, source_target_pairs={{2,6},{3,7},{4,0},{5,1},{6,10},{7,11},{8,4},{9,5},{10,14},{11,15},... | collective-permute-start | bytes 1179656 | tf_op jit(solution)/shard_map/ppermute | solution.py:435
  146.0 12.0 %collective-permute-start.28 = (bf16[1,4,384,128]{3,2,1,0:T(8,128)(2,1)S(1)}, bf16[1,4,384,128]{3,2,1,0:T(8,128)(2,1)S(1)}, u32[]{:S(2)}, u32[]{:S(2)}) collective-permute-start(bf16[1,4,384,128]{3,2,1,0:T(8,128)(2,1)S(1)} %get-tuple-element.114), channel_id=1, source_target_pairs={{0,2},{1,3},{2,0},{3,1},{4,6},{5,7},{6,4},{7,5},{8,10},{9,11},{10,... | collective-permute-start | bytes 1179656 | tf_op jit(solution)/shard_map/ppermute | solution.py:423
  147.1 17.8 %collective-permute-start.32 = (bf16[1,4,384,128]{3,2,1,0:T(8,128)(2,1)S(1)}, bf16[1,4,384,128]{3,2,1,0:T(8,128)(2,1)S(1)}, u32[]{:S(2)}, u32[]{:S(2)}) collective-permute-start(bf16[1,4,384,128]{3,2,1,0:T(8,128)(2,1)S(1)} %get-tuple-element.120), channel_id=1, source_target_pairs={{0,1},{1,0},{2,3},{3,2},{4,5},{5,4},{6,7},{7,6},{8,9},{9,8},{10,11... | collective-permute-start | bytes 1179656 | tf_op jit(solution)/shard_map/ppermute | solution.py:423
  147.1 17.9 %collective-permute-start.33 = (bf16[1,4,384,128]{3,2,1,0:T(8,128)(2,1)S(1)}, bf16[1,4,384,128]{3,2,1,0:T(8,128)(2,1)S(1)}, u32[]{:S(2)}, u32[]{:S(2)}) collective-permute-start(bf16[1,4,384,128]{3,2,1,0:T(8,128)(2,1)S(1)} %get-tuple-element.121), channel_id=1, source_target_pairs={{0,3},{1,2},{2,1},{3,0},{4,7},{5,6},{6,5},{7,4},{8,11},{9,10},{10,... | collective-permute-start | bytes 1179656 | tf_op jit(solution)/shard_map/ppermute | solution.py:423
  158.2 9.2 %collective-permute-start.29 = (bf16[1,4,384,128]{3,2,1,0:T(8,128)(2,1)S(1)}, bf16[1,4,384,128]{3,2,1,0:T(8,128)(2,1)S(1)}, u32[]{:S(2)}, u32[]{:S(2)}) collective-permute-start(bf16[1,4,384,128]{3,2,1,0:T(8,128)(2,1)S(1)} %get-tuple-element.116), channel_id=1, source_target_pairs={{0,1},{1,0},{2,3},{3,2},{4,5},{5,4},{6,7},{7,6},{8,9},{9,8},{10,11... | collective-permute-start | bytes 1179656 | tf_op jit(solution)/shard_map/ppermute | solution.py:423
  158.3 16.6 %collective-permute-start.30 = (bf16[1,4,384,128]{3,2,1,0:T(8,128)(2,1)S(1)}, bf16[1,4,384,128]{3,2,1,0:T(8,128)(2,1)S(1)}, u32[]{:S(2)}, u32[]{:S(2)}) collective-permute-start(bf16[1,4,384,128]{3,2,1,0:T(8,128)(2,1)S(1)} %get-tuple-element.117), channel_id=1, source_target_pairs={{0,2},{1,3},{2,0},{3,1},{4,6},{5,7},{6,4},{7,5},{8,10},{9,11},{10,... | collective-permute-start | bytes 1179656 | tf_op jit(solution)/shard_map/ppermute | solution.py:423
  159.4 22.2 %collective-permute-start.31 = (bf16[1,4,384,128]{3,2,1,0:T(8,128)(2,1)S(1)}, bf16[1,4,384,128]{3,2,1,0:T(8,128)(2,1)S(1)}, u32[]{:S(2)}, u32[]{:S(2)}) collective-permute-start(bf16[1,4,384,128]{3,2,1,0:T(8,128)(2,1)S(1)} %get-tuple-element.118), channel_id=1, source_target_pairs={{0,3},{1,2},{2,1},{3,0},{4,7},{5,6},{6,5},{7,4},{8,11},{9,10},{10,... | collective-permute-start | bytes 1179656 | tf_op jit(solution)/shard_map/ppermute | solution.py:423

commit v2 on v1

--- a/solution.py
+++ b/solution.py
@@ -329,16 +329,19 @@
     )(table, *[value for value, _ in inputs], *spare)
 
 
-def finish(rows, extras, done, local, grads, spare):
-    team, _, tile, _ = done.shape
+def finish(rows, extras, dones, local, grads, spare):
+    team, _, tile, _ = local.shape
     step = tile // BLOCKS
-
-    def kernel(done, local, *refs):
-        terms, outs = refs[: len(grads)], refs[-team:]
+    ahead = 2 * len(dones)
+
+    def kernel(*refs):
+        ready, local = refs[: len(dones)], refs[len(dones)]
+        terms, outs = refs[len(dones) + 1 : len(dones) + 1 + len(grads)], refs[-team:]
         for d in range(team):
             out = outs[d].at[0]
             for n in range(2):
-                out[n] = done[d, n]
+                for m, done in enumerate(ready):
+                    out[2 * m + n] = done[d, n]
                 for g in range(BLOCKS):
                     at = pl.ds(g * step, step)
                     total = local[d, n, at]
@@ -350,7 +353,7 @@
                             total = total + term[0, g, row].astype(F32)
                         else:
                             total = total + term[d % rows, n, at].astype(F32)
-                    out[2 + n, at] = total.astype(BF16)
+                    out[ahead + n, at] = total.astype(BF16)
 
     def whole(shape):
         return pl.BlockSpec(shape, lambda i: (0,) * len(shape))
@@ -360,46 +363,48 @@
             return whole(value.shape)
         return pl.BlockSpec((1, BLOCKS, 2 * rows * step, HD), lambda i: (0, 0, 1, 0))
 
-    piece = (1, 4, tile, HD)
+    piece = (1, ahead + 2, tile, HD)
     return pl.pallas_call(
         kernel,
         grid=(1,),
         out_shape=[struct(piece, BF16)] * team,
-        in_specs=[whole(done.shape), whole(local.shape)]
+        in_specs=[whole(done.shape) for done in dones]
+        + [whole(local.shape)]
         + [grad_spec(*grad) for grad in grads]
         + [ANY] * len(spare),
         out_specs=[whole(piece)] * team,
-        cost_estimate=moved(team * 24 * tile * HD),
+        cost_estimate=moved(team * (16 + 4 * ahead) * tile * HD),
         compiler_params=LIGHT,
         name="finish",
-    )(done, local, *[value for value, _ in grads], *spare)
-
-
-def unpack(c, places, pieces, outs, shape):
+    )(*dones, local, *[value for value, _ in grads], *spare)
+
+
+def unpack(c, places, pairs, outs, shape):
     tile = shape[1]
     step = tile // BLOCKS
-    team = len(pieces)
+    team = places.shape[0]
     held = [] if outs is None else list(outs)
+    pieces = [*pairs[0], *pairs[1]]
 
     def kernel(places_ref, *refs):
         for d in range(team):
             lanes = pl.ds(pl.multiple_of(places_ref[d] * HD, HD), HD)
             for n in range(4):
-                refs[n - 4][0, :, lanes] = refs[d][0, n]
+                refs[n - 4][0, :, lanes] = refs[n // 2 * team + d][0, n % 2]
 
     return pl.pallas_call(
         kernel,
         grid=(BLOCKS,),
         out_shape=[struct(shape, BF16)] * 4,
         in_specs=[SMEM]
-        + [pl.BlockSpec((1, 4, step, HD), lambda i: (0, 0, i, 0))] * team
+        + [pl.BlockSpec((1, 2, step, HD), lambda i, at=at: (0, at, i, 0)) for _, at in pieces]
         + [ANY] * len(held),
         out_specs=[pl.BlockSpec((1, step, team * HD), lambda i: (0, i, c))] * 4,
-        input_output_aliases={1 + team + n: n for n in range(len(held))},
+        input_output_aliases={1 + len(pieces) + n: n for n in range(len(held))},
         cost_estimate=moved(16 * tile * team * HD),
         compiler_params=LIGHT,
         name="unpack",
-    )(places, *pieces, *held)
+    )(places, *[value for value, _ in pieces], *held)
 
 
 def body(queries, keys, values, grad_out, window_tiles, window_count):
@@ -468,6 +473,7 @@
     ready = {}
     worked = {}
     home = {}
+    found = {}
 
     def pass_on(c, spare):
         pieces = [arrived[c, d] for d in far]
@@ -481,12 +487,17 @@
         return outs[-1]
 
     def finished(c, spare):
-        done, local, grads_one, grads_two = worked[c]
+        _, local, grads_one, grads_two = worked[c]
         if c + 2 < per:
             grads = [(halos[c + 2][1], True), (halos[c + 2][0], True)]
         else:
             grads = [(shift(grads_one, 1), False), (shift(grads_two, 0), False)]
-        pieces = finish(rows, extras, done, local, grads, spare)
+        heads_in = [0] if c == 0 else []
+        heads_in += [c + 1] if c + 1 < per else []
+        dones = [worked[k][0] for k in heads_in]
+        pieces = finish(rows, extras, dones, local, grads, spare)
+        for m, k in enumerate(heads_in):
+            found[k] = (c, m)
         home[c] = [swap(piece, d) for d, piece in enumerate(pieces)]
         return pieces[0]
 
@@ -533,7 +544,7 @@
         if c == 0:
             spare = hbm(spare)
         if c >= 2:
-            spare.append(finished(c - 2, [worked[c - 1][0]]))
+            spare.append(finished(c - 2, []))
         if c >= 3:
             spare += home[c - 3][1:]
         worked[c] = attend(rows, tile, span, table, tuple(loads), inputs, spare)
@@ -542,10 +553,13 @@
     for c in every[-2:]:
         early = [k for k in (c - 2, c - 1) if k in home and (k == c - 2 or c == per - 1)]
         gone = [home[k][d] for k in early for d in (range(1, team) if k == c - 2 else far[:1])]
-        finished(c, [worked[per - 1][0]] + gone)
+        finished(c, gone)
     outs = None
     for c in every:
-        outs = unpack(c, members, home[c], outs, queries.shape)
+        held, at = found[c]
+        last = home[c][0].shape[1] // 2 - 1
+        pairs = ([(piece, at) for piece in home[held]], [(piece, last) for piece in home[c]])
+        outs = unpack(c, members, pairs, outs, queries.shape)
     attended, grad_queries, grad_keys, grad_values = outs
     return (attended, grad_queries, grad_keys, grad_values)
 

time: 185 us -> 176 us (0.951)
  waiting for transfers between devices: 42.8 us -> 32.6 us
    ppermute x22, waiting for transfers between devices: 33.5 us -> 26.4 us  [swap(): lax.ppermute(value, RING, [(i, i - i % team + (i % team ^ d)) for i in ra...]
    ppermute x12, waiting for transfers between devices: 9.31 us -> 6.2 us  [shift(): return lax.ppermute(value, RING, pairs)]
    ppermute x22, starting transfers between devices: 18.8 us -> 20.7 us  [swap(): lax.ppermute(value, RING, [(i, i - i % team + (i % team ^ d)) for i in ra...]
  transfers between devices with their start and end apart: 34 -> 34, of which waited for: 11 -> 10; matrix products, arithmetic and copies ran while one was open for 0% -> 0% of each run, Pallas kernels for 44% -> 46%
where the time goes in v2:
time: 176 us
  Pallas kernels  85.2 us (48%)
  starting transfers between devices  54.7 us (31%)
  waiting for transfers between devices  32.6 us (19%)
    pallas_call x4, Pallas kernels, attend(): pl.pallas_call(functools.partial(attend_kernel, plan, rows, tile), grid=(...  62.1 us
    ppermute x12, starting transfers between devices, shift(): return lax.ppermute(value, RING, pairs)  34.1 us
    ppermute x22, waiting for transfers between devices, swap(): lax.ppermute(value, RING, [(i, i - i % team + (i % team ^ d)) for i in ra...  26.4 us
    ppermute x22, starting transfers between devices, swap(): lax.ppermute(value, RING, [(i, i - i % team + (i % team ^ d)) for i in ra...  20.7 us
    pallas_call x4, Pallas kernels, unpack(): pl.pallas_call(kernel, grid=(BLOCKS,), out_shape=[struct(shape, BF16)] *...  9.72 us
    pallas_call x2, Pallas kernels, pack(): pl.pallas_call(functools.partial(pack_kernel, jobs, step, start), grid=(B...  8.17 us
    ppermute x12, waiting for transfers between devices, shift(): return lax.ppermute(value, RING, pairs)  6.2 us
    pallas_call x4, Pallas kernels, relay(): pl.pallas_call(kernel, grid=(1,), out_shape=[kept(shape, BF16)] * kinds +...  4.36 us
  transfers between devices with their start and end apart: 34, of which 10 were waited for; matrix products, arithmetic and copies ran while one was open for 0% of the time, Pallas kernels for 46%

profile of v2, /device:TPU:0, one launch (start us, length us, event | category | flops | bytes accessed | tf_op | source)
XLA Modules:
  0.0 175.6 jit_solution(4508996755167538836)
XLA Ops:
  1.3 0.7 fusion.3
  2.0 0.1 fusion.1
  2.1 2.5 %pack.2 = (bf16[1,4,400,128]{3,2,1,0:T(8,128)(2,1)S(1)}, bf16[1,4,400,128]{3,2,1,0:T(8,128)(2,1)S(1)}, bf16[1,4,400,128]{3,2,1,0:T(8,128)(2,1)S(1)}, bf16[1,4,400,128]{3,2,1,0:T(8,128)(2,1)S(1)}) custom-call(s32[4]{0:T(128)S(1)} %iota_xor_fusion.places_ref, s32[6]{0:T(128)S(1)} %convert_element_type.10.flags_ref, bf16[1,384,2048]{2,1,0:T(8,128)(2,1)} %refs_0_.3, ...), custom_call_target="tpu_custom_call" | custom-call | bytes 3276800 | tf_op jit(solution)/shard_map/pack/pallas_call | solution.py:67
  4.7 0.5 collective-permute-start
  5.2 2.6 %collective-permute-start.1 = (bf16[1,4,400,128]{3,2,1,0:T(8,128)(2,1)S(1)}, bf16[1,4,400,128]{3,2,1,0:T(8,128)(2,1)}, u32[]{:S(2)}, u32[]{:S(2)}) collective-permute-start(bf16[1,4,400,128]{3,2,1,0:T(8,128)(2,1)S(1)} %get-tuple-element.71), channel_id=1, source_target_pairs={{0,2},{1,3},{2,0},{3,1},{4,6},{5,7},{6,4},{7,5},{8,10},{9,11},{10,... | collective-permute-start | bytes 1228808 | tf_op jit(solution)/shard_map/ppermute | solution.py:428
  7.8 5.6 %pack.3 = (bf16[1,4,384,128]{3,2,1,0:T(8,128)(2,1)}, bf16[1,4,384,128]{3,2,1,0:T(8,128)(2,1)}, bf16[1,4,384,128]{3,2,1,0:T(8,128)(2,1)}, bf16[1,4,384,128]{3,2,1...) custom-call(s32[4]{0:T(128)S(1)} %iota_xor_fusion.places_ref, ...), custom_call_target="tpu_custom_call" | custom-call | bytes 9437184 | tf_op jit(solution)/shard_map/pack/pallas_call | solution.py:67
  13.5 0.2 collective-permute-start.3
  13.7 1.7 collective-permute-start.7
  15.4 0.3 collective-permute-start.6
  15.7 2.5 %collective-permute-done.1.refs_2_.refs_6_ = bf16[1,4,400,128]{3,2,1,0:T(8,128)(2,1)} collective-permute-done((bf16[1,4,400,128]{3,2,1,0:T(8,128)(2,1)S(1)}, bf16[1,4,400,128]{3,2,1,0:T(8,128)(2,1)}, u32[]{:S(2)}, u32[]{:S(2)}) %collective-permute-start.1) | collective-permute-done | bytes 409632 | tf_op jit(solution)/shard_map/ppermute | solution.py:428
  18.2 8.3 %collective-permute-done.2.refs_3_.refs_7_ = bf16[1,4,400,128]{3,2,1,0:T(8,128)(2,1)} collective-permute-done((bf16[1,4,400,128]{3,2,1,0:T(8,128)(2,1)S(1)}, bf16[1,4,400,128]{3,2,1,0:T(8,128)(2,1)}, u32[]{:S(2)}, u32[]{:S(2)}) %collective-permute-start.2) | collective-permute-done | bytes 409632 | tf_op jit(solution)/shard_map/ppermute | solution.py:428
  26.4 2.1 %relay.4 = (bf16[1,4,384,128]{3,2,1,0:T(8,128)(2,1)}, bf16[1,4,384,128]{3,2,1,0:T(8,128)(2,1)}, bf16[4,16,128]{2,1,0:T(8,128)(2,1)S(1)}) custom-call(bf16[1,4,400,128]{3,2,1,0:T(8,128)(2,1)S(1)} %get-tuple-element.69.refs_0_.refs_4_, bf16[1,4,400,128]{3,2,1,0:T(8,128)(2,1)S(1)} %collective-permute-done.refs_4_.refs_1_.refs_5_, ...), custom_call_target="tpu_custom_call" | custom-call | bytes 1572864 | tf_op jit(solution)/shard_map/relay/pallas_call | solution.py:116
  28.5 0.1 copy.29
  28.7 4.3 %collective-permute-start.13 = (bf16[1,4,384,128]{3,2,1,0:T(8,128)(2,1)}, bf16[1,4,384,128]{3,2,1,0:T(8,128)(2,1)}, u32[]{:S(2)}, u32[]{:S(2)}) collective-permute-start(bf16[1,4,384,128]{3,2,1,0:T(8,128)(2,1)} %get-tuple-element.85), channel_id=1, source_target_pairs={{0,4},{1,5},{4,8},{5,9},{6,2},{7,3},{8,12},{9,13},{10,6},{11,7},{1... | collective-permute-start | bytes 1179656 | tf_op jit(solution)/shard_map/ppermute | solution.py:440
  33.0 1.3 collective-permute-start.12
  34.3 0.1 fusion.4
  34.4 0.1 pad_add_fusion
  34.5 0.1 copy.30
  34.6 0.1 pad_add_fusion.1.table_ref
  34.6 0.2 collective-permute-done.7.refs_3_
  34.9 2.3 %collective-permute-start.10 = (bf16[1,4,384,128]{3,2,1,0:T(8,128)(2,1)}, bf16[1,4,384,128]{3,2,1,0:T(8,128)(2,1)S(1)}, u32[]{:S(2)}, u32[]{:S(2)}) collective-permute-start(bf16[1,4,384,128]{3,2,1,0:T(8,128)(2,1)} %get-tuple-element.83), channel_id=1, source_target_pairs={{0,2},{1,3},{2,0},{3,1},{4,6},{5,7},{6,4},{7,5},{8,10},{9,11},{10,... | collective-permute-start | bytes 1179656 | tf_op jit(solution)/shard_map/ppermute | solution.py:428
  37.2 6.6 %collective-permute-done.6.refs_2_ = bf16[1,4,384,128]{3,2,1,0:T(8,128)(2,1)} collective-permute-done((bf16[1,4,384,128]{3,2,1,0:T(8,128)(2,1)}, bf16[1,4,384,128]{3,2,1,0:T(8,128)(2,1)}, u32[]{:S(2)}, u32[]{:S(2)}) %collective-permute-start.6) | collective-permute-done | bytes 393248 | tf_op jit(solution)/shard_map/ppermute | solution.py:428
  43.8 0.8 collective-permute-start.11
  44.6 2.0 %relay.5 = (bf16[1,4,384,128]{3,2,1,0:T(8,128)(2,1)}, bf16[1,4,384,128]{3,2,1,0:T(8,128)(2,1)}) custom-call(bf16[3,4,384,128]{3,2,1,0:T(8,128)(2,1)S(1)} %copy-done, bf16[3,4,384,128]{3,2,1,0:T(8,128)(2,1)S(1)} %collective-permute-done.3.refs_1_, bf16[1,4,384,128]{3,2,1,0:T(8,128)(2,1)} %collective-permute-done.6.refs_2_, ...), custom_call_target="tpu_custom_call" | custom-call | bytes 1572864 | tf_op jit(solution)/shard_map/relay/pallas_call | solution.py:116
  46.5 3.5 %collective-permute-start.9 = (bf16[1,4,384,128]{3,2,1,0:T(8,128)(2,1)}, bf16[1,4,384,128]{3,2,1,0:T(8,128)(2,1)S(1)}, u32[]{:S(2)}, u32[]{:S(2)}) collective-permute-start(bf16[1,4,384,128]{3,2,1,0:T(8,128)(2,1)} %get-tuple-element.82), channel_id=1, source_target_pairs={{0,4},{1,5},{4,8},{5,9},{6,2},{7,3},{8,12},{9,13},{10,6},{11,7},{1... | collective-permute-start | bytes 1179656 | tf_op jit(solution)/shard_map/ppermute | solution.py:440
  50.0 1.3 collective-permute-start.8
  51.3 16.0 %attend.4 = (bf16[4,2,384,128]{3,2,1,0:T(8,128)(2,1)S(1)}, f32[4,2,384,128]{3,2,1,0:T(8,128)S(1)}, bf16[2,2,384,128]{3,2,1,0:T(8,128)(2,1)S(1)}, bf16[2,2,384,128]{3,2,1,0:T(8,128)(2,1)S(1)}) custom-call(s32[4,9]{1,0:T(4,128)S(1)} %pad_add_fusion.1.table_ref, bf16[1,4,400,128]{3,2,1,0:T(8,128)(2,1)S(1)} %get-tuple-element.69.refs_0_.refs_4_, ...), custom_call_target="tpu_custom_call" | custom-call | flops 5435817984 | bytes 8388608 | tf_op jit(solution)/shard_map/attend/pallas_call | solution.py:304
  67.4 0.2 relay.6
  67.6 4.7 %collective-permute-start.17 = (bf16[1,4,768,128]{3,2,1,0:T(8,128)(2,1)S(1)}, bf16[1,4,768,128]{3,2,1,0:T(8,128)(2,1)S(1)}, u32[]{:S(2)}, u32[]{:S(2)}) collective-permute-start(bf16[1,4,768,128]{3,2,1,0:T(8,128)(2,1)S(1)} %get-tuple-element.93), channel_id=1, source_target_pairs={{0,4},{1,5},{4,8},{5,9},{6,2},{7,3},{8,12},{9,13},{10,6},{11,7},{1... | collective-permute-start | bytes 2359304 | tf_op jit(solution)/shard_map/ppermute | solution.py:440
  72.3 1.5 collective-permute-start.16
  73.8 2.3 %collective-permute-start.4 = (bf16[1,4,384,128]{3,2,1,0:T(8,128)(2,1)S(1)}, bf16[1,4,384,128]{3,2,1,0:T(8,128)(2,1)S(1)}, u32[]{:S(2)}, u32[]{:S(2)}) collective-permute-start(bf16[1,4,384,128]{3,2,1,0:T(8,128)(2,1)S(1)} %copy-done.3), channel_id=1, source_target_pairs={{0,2},{1,3},{2,0},{3,1},{4,6},{5,7},{6,4},{7,5},{8,10},{9,11},{10,... | collective-permute-start | bytes 1179656 | tf_op jit(solution)/shard_map/ppermute | solution.py:428
  76.1 15.7 %attend.5 = (bf16[4,2,384,128]{3,2,1,0:T(8,128)(2,1)S(1)}, f32[4,2,384,128]{3,2,1,0:T(8,128)S(1)}, bf16[2,2,384,128]{3,2,1,0:T(8,128)(2,1)S(1)}, bf16[2,2,384,128]{3,2,1,0:T(8,128)(2,1)S(1)}) custom-call(s32[4,9]{1,0:T(4,128)S(1)} %pad_add_fusion.1.table_ref, bf16[3,4,384,128]{3,2,1,0:T(8,128)(2,1)S(1)} %copy-done, ...), custom_call_target="tpu_custom_call" | custom-call | flops 5435817984 | bytes 8388608 | tf_op jit(solution)/shard_map/attend/pallas_call | solution.py:304
  91.9 1.1 collective-permute-done.5.refs_3_
  93.0 0.2 relay.7
  93.2 4.2 %collective-permute-start.15 = (bf16[1,4,768,128]{3,2,1,0:T(8,128)(2,1)S(1)}, bf16[1,4,768,128]{3,2,1,0:T(8,128)(2,1)S(1)}, u32[]{:S(2)}, u32[]{:S(2)}) collective-permute-start(bf16[1,4,768,128]{3,2,1,0:T(8,128)(2,1)S(1)} %get-tuple-element.92), channel_id=1, source_target_pairs={{0,4},{1,5},{4,8},{5,9},{6,2},{7,3},{8,12},{9,13},{10,6},{11,7},{1... | collective-permute-start | bytes 2359304 | tf_op jit(solution)/shard_map/ppermute | solution.py:440
  97.5 1.5 collective-permute-start.14
  99.0 0.3 finish.4
  99.3 0.4 collective-permute-start.18
  99.7 1.2 collective-permute-start.19
  100.9 0.4 collective-permute-start.20
  101.2 15.2 %attend.6 = (bf16[4,2,384,128]{3,2,1,0:T(8,128)(2,1)S(1)}, f32[4,2,384,128]{3,2,1,0:T(8,128)S(1)}, bf16[2,2,384,128]{3,2,1,0:T(8,128)(2,1)S(1)}, bf16[2,2,384,128]{3,2,1,0:T(8,128)(2,1)S(1)}) custom-call(s32[4,9]{1,0:T(4,128)S(1)} %pad_add_fusion.1.table_ref, bf16[3,4,384,128]{3,2,1,0:T(8,128)(2,1)S(1)} %copy-done, ...), custom_call_target="tpu_custom_call" | custom-call | flops 5435817984 | bytes 8388608 | tf_op jit(solution)/shard_map/attend/pallas_call | solution.py:304
  116.4 4.6 %collective-permute-start.21 = (bf16[2,2,384,128]{3,2,1,0:T(8,128)(2,1)S(1)}, bf16[2,2,384,128]{3,2,1,0:T(8,128)(2,1)S(1)}, u32[]{:S(2)}, u32[]{:S(2)}) collective-permute-start(bf16[2,2,384,128]{3,2,1,0:T(8,128)(2,1)S(1)} %get-tuple-element.106), channel_id=1, source_target_pairs={{0,4},{1,5},{4,8},{5,9},{6,2},{7,3},{8,12},{9,13},{10,6},{11,7},{1... | collective-permute-start | bytes 1179656 | tf_op jit(solution)/shard_map/ppermute | solution.py:440
  121.0 1.6 collective-permute-start.22
  122.6 0.3 finish.5
  122.9 0.1 collective-permute-start.28
  123.0 1.1 collective-permute-start.29
  124.1 3.1 %collective-permute-done.20.refs_9_.refs_6_.refs_3_.refs_7_ = bf16[1,6,384,128]{3,2,1,0:T(8,128)(2,1)S(1)} collective-permute-done((bf16[1,6,384,128]{3,2,1,0:T(8,128)(2,1)S(1)}, bf16[1,6,384,128]{3,2,1,0:T(8,128)(2,1)S(1)}, u32[]{:S(2)}, u32[]{:S(2)}) %collective-permute-start.20) | collective-permute-done | bytes 589856 | tf_op jit(solution)/shard_map/ppermute | solution.py:428
  127.2 2.2 %collective-permute-start.30 = (bf16[1,4,384,128]{3,2,1,0:T(8,128)(2,1)S(1)}, bf16[1,4,384,128]{3,2,1,0:T(8,128)(2,1)S(1)}, u32[]{:S(2)}, u32[]{:S(2)}) collective-permute-start(bf16[1,4,384,128]{3,2,1,0:T(8,128)(2,1)S(1)} %get-tuple-element.117), channel_id=1, source_target_pairs={{0,3},{1,2},{2,1},{3,0},{4,7},{5,6},{6,5},{7,4},{8,11},{9,10},{10,... | collective-permute-start | bytes 1179656 | tf_op jit(solution)/shard_map/ppermute | solution.py:428
  129.4 15.2 %attend.7 = (bf16[4,2,384,128]{3,2,1,0:T(8,128)(2,1)S(1)}, f32[4,2,384,128]{3,2,1,0:T(8,128)S(1)}, bf16[2,2,384,128]{3,2,1,0:T(8,128)(2,1)S(1)}, bf16[2,2,384,128]{3,2,1,0:T(8,128)(2,1)S(1)}) custom-call(s32[4,9]{1,0:T(4,128)S(1)} %pad_add_fusion.1.table_ref, bf16[3,4,384,128]{3,2,1,0:T(8,128)(2,1)S(1)} %copy-done, ...), custom_call_target="tpu_custom_call" | custom-call | flops 5435817984 | bytes 8388608 | tf_op jit(solution)/shard_map/attend/pallas_call | solution.py:304
  144.6 0.2 finish.6
  144.8 0.9 collective-permute-start.24
  145.7 4.3 %collective-permute-start.26 = (bf16[2,2,384,128]{3,2,1,0:T(8,128)(2,1)S(1)}, bf16[2,2,384,128]{3,2,1,0:T(8,128)(2,1)S(1)}, u32[]{:S(2)}, u32[]{:S(2)}) collective-permute-start(bf16[2,2,384,128]{3,2,1,0:T(8,128)(2,1)S(1)} %get-tuple-element.113), channel_id=1, source_target_pairs={{0,4},{1,5},{4,8},{5,9},{6,2},{7,3},{8,12},{9,13},{10,6},{11,7},{1... | collective-permute-start | bytes 1179656 | tf_op jit(solution)/shard_map/ppermute | solution.py:440
  150.0 1.3 collective-permute-start.27
  151.4 1.6 collective-permute-start.25
  153.0 2.7 %collective-permute-done.24.refs_6_.refs_2_ = bf16[1,4,384,128]{3,2,1,0:T(8,128)(2,1)S(1)} collective-permute-done((bf16[1,4,384,128]{3,2,1,0:T(8,128)(2,1)S(1)}, bf16[1,4,384,128]{3,2,1,0:T(8,128)(2,1)S(1)}, u32[]{:S(2)}, u32[]{:S(2)}) %collective-permute-start.24) | collective-permute-done | bytes 393248 | tf_op jit(solution)/shard_map/ppermute | solution.py:428
  155.7 2.0 %collective-permute-done.26.refs_1_ = bf16[2,2,384,128]{3,2,1,0:T(8,128)(2,1)S(1)} collective-permute-done((bf16[2,2,384,128]{3,2,1,0:T(8,128)(2,1)S(1)}, bf16[2,2,384,128]{3,2,1,0:T(8,128)(2,1)S(1)}, u32[]{:S(2)}, u32[]{:S(2)}) %collective-permute-start.26) | collective-permute-done | bytes 393248 | tf_op jit(solution)/shard_map/ppermute | solution.py:440
  157.7 4.1 %collective-permute-done.27.refs_2_ = bf16[2,2,384,128]{3,2,1,0:T(8,128)(2,1)S(1)} collective-permute-done((bf16[2,2,384,128]{3,2,1,0:T(8,128)(2,1)S(1)}, bf16[2,2,384,128]{3,2,1,0:T(8,128)(2,1)S(1)}, u32[]{:S(2)}, u32[]{:S(2)}) %collective-permute-start.27) | collective-permute-done | bytes 393248 | tf_op jit(solution)/shard_map/ppermute | solution.py:440
  161.8 0.1 finish.7
  162.1 1.8 %collective-permute-start.33 = (bf16[1,2,384,128]{3,2,1,0:T(8,128)(2,1)S(1)}, bf16[1,2,384,128]{3,2,1,0:T(8,128)(2,1)S(1)}, u32[]{:S(2)}, u32[]{:S(2)}) collective-permute-start(bf16[1,2,384,128]{3,2,1,0:T(8,128)(2,1)S(1)} %get-tuple-element.121), channel_id=1, source_target_pairs={{0,3},{1,2},{2,1},{3,0},{4,7},{5,6},{6,5},{7,4},{8,11},{9,10},{10,... | collective-permute-start | bytes 589832 | tf_op jit(solution)/shard_map/ppermute | solution.py:428
  163.9 2.4 %unpack.4 = (bf16[1,384,2048]{2,1,0:T(8,128)(2,1)}, bf16[1,384,2048]{2,1,0:T(8,128)(2,1)}, bf16[1,384,2048]{2,1,0:T(8,128)(2,1)}, bf16[1,384,2048]{2,1,0:T(8,128)(2,1)}) custom-call(s32[4]{0:T(128)S(1)} %iota_xor_fusion.places_ref, bf16[1,6,384,128]{3,2,1,0:T(8,128)(2,1)S(1)} %get-tuple-element.97.refs_7_.refs_0_.refs_4_, ...), custom_call_target="tpu_custom_call" | custom-call | bytes 3145728 | tf_op jit(solution)/shard_map/unpack/pallas_call | solution.py:395
  166.3 2.4 %unpack.5 = (bf16[1,384,2048]{2,1,0:T(8,128)(2,1)}, bf16[1,384,2048]{2,1,0:T(8,128)(2,1)}, bf16[1,384,2048]{2,1,0:T(8,128)(2,1)}, bf16[1,384,2048]{2,1,0:T(8,128)(2,1)}) custom-call(s32[4]{0:T(128)S(1)} %iota_xor_fusion.places_ref, ...), custom_call_target="tpu_custom_call", output_to_operand_aliasing={{0}: (9, {}), {1}: (10, {}), {2}: (11, {}), {3}: (12, {})} | custom-call | bytes 3145728 | tf_op jit(solution)/shard_map/unpack/pallas_call | solution.py:395
  168.8 2.5 %unpack.6 = (bf16[1,384,2048]{2,1,0:T(8,128)(2,1)}, bf16[1,384,2048]{2,1,0:T(8,128)(2,1)}, bf16[1,384,2048]{2,1,0:T(8,128)(2,1)}, bf16[1,384,2048]{2,1,0:T(8,128)(2,1)}) custom-call(s32[4]{0:T(128)S(1)} %iota_xor_fusion.places_ref, ...), custom_call_target="tpu_custom_call", output_to_operand_aliasing={{0}: (9, {}), {1}: (10, {}), {2}: (11, {}), {3}: (12, {})} | custom-call | bytes 3145728 | tf_op jit(solution)/shard_map/unpack/pallas_call | solution.py:395
  171.2 1.9 %collective-permute-done.33.refs_7_ = bf16[1,2,384,128]{3,2,1,0:T(8,128)(2,1)S(1)} collective-permute-done((bf16[1,2,384,128]{3,2,1,0:T(8,128)(2,1)S(1)}, bf16[1,2,384,128]{3,2,1,0:T(8,128)(2,1)S(1)}, u32[]{:S(2)}, u32[]{:S(2)}) %collective-permute-start.33) | collective-permute-done | bytes 196640 | tf_op jit(solution)/shard_map/ppermute | solution.py:428
  173.1 2.4 %unpack.7 = (bf16[1,384,2048]{2,1,0:T(8,128)(2,1)}, bf16[1,384,2048]{2,1,0:T(8,128)(2,1)}, bf16[1,384,2048]{2,1,0:T(8,128)(2,1)}, bf16[1,384,2048]{2,1,0:T(8,128)(2,1)}) custom-call(s32[4]{0:T(128)S(1)} %iota_xor_fusion.places_ref, ...), custom_call_target="tpu_custom_call", output_to_operand_aliasing={{0}: (9, {}), {1}: (10, {}), {2}: (11, {}), {3}: (12, {})} | custom-call | bytes 3145728 | tf_op jit(solution)/shard_map/unpack/pallas_call | solution.py:395
  (47 shorter events, 0.5 us)
Async XLA Ops:
  4.7 3.2 %collective-permute-start = (bf16[1,4,400,128]{3,2,1,0:T(8,128)(2,1)S(1)}, bf16[1,4,400,128]{3,2,1,0:T(8,128)(2,1)S(1)}, u32[]{:S(2)}, u32[]{:S(2)}) collective-permute-start(bf16[1,4,400,128]{3,2,1,0:T(8,128)(2,1)S(1)} %get-tuple-element.70), channel_id=1, source_target_pairs={{0,1},{1,0},{2,3},{3,2},{4,5},{5,4},{6,7},{7,6},{8,9},{9,8},{10,11... | collective-permute-start | bytes 1228808 | tf_op jit(solution)/shard_map/ppermute | solution.py:428
  5.2 13.0 %collective-permute-start.1 = (bf16[1,4,400,128]{3,2,1,0:T(8,128)(2,1)S(1)}, bf16[1,4,400,128]{3,2,1,0:T(8,128)(2,1)}, u32[]{:S(2)}, u32[]{:S(2)}) collective-permute-start(bf16[1,4,400,128]{3,2,1,0:T(8,128)(2,1)S(1)} %get-tuple-element.71), channel_id=1, source_target_pairs={{0,2},{1,3},{2,0},{3,1},{4,6},{5,7},{6,4},{7,5},{8,10},{9,11},{10,... | collective-permute-start | bytes 1228808 | tf_op jit(solution)/shard_map/ppermute | solution.py:428
  7.7 18.7 %collective-permute-start.2 = (bf16[1,4,400,128]{3,2,1,0:T(8,128)(2,1)S(1)}, bf16[1,4,400,128]{3,2,1,0:T(8,128)(2,1)}, u32[]{:S(2)}, u32[]{:S(2)}) collective-permute-start(bf16[1,4,400,128]{3,2,1,0:T(8,128)(2,1)S(1)} %get-tuple-element.72), channel_id=1, source_target_pairs={{0,3},{1,2},{2,1},{3,0},{4,7},{5,6},{6,5},{7,4},{8,11},{9,10},{10,... | collective-permute-start | bytes 1228808 | tf_op jit(solution)/shard_map/ppermute | solution.py:428
  13.5 31.1 %collective-permute-start.3 = (bf16[3,4,384,128]{3,2,1,0:T(8,128)(2,1)}, bf16[3,4,384,128]{3,2,1,0:T(8,128)(2,1)S(1)}, u32[]{:S(2)}, u32[]{:S(2)}) collective-permute-start(bf16[3,4,384,128]{3,2,1,0:T(8,128)(2,1)} %get-tuple-element.76), channel_id=1, source_target_pairs={{0,1},{1,0},{2,3},{3,2},{4,5},{5,4},{6,7},{7,6},{8,9},{9,8},{10,11... | collective-permute-start | bytes 3538952 | tf_op jit(solution)/shard_map/ppermute | solution.py:428
  13.7 21.2 %collective-permute-start.7 = (bf16[1,4,384,128]{3,2,1,0:T(8,128)(2,1)}, bf16[1,4,384,128]{3,2,1,0:T(8,128)(2,1)}, u32[]{:S(2)}, u32[]{:S(2)}) collective-permute-start(bf16[1,4,384,128]{3,2,1,0:T(8,128)(2,1)} %get-tuple-element.79), channel_id=1, source_target_pairs={{0,3},{1,2},{2,1},{3,0},{4,7},{5,6},{6,5},{7,4},{8,11},{9,10},{10,... | collective-permute-start | bytes 1179656 | tf_op jit(solution)/shard_map/ppermute | solution.py:428
  15.4 28.4 %collective-permute-start.6 = (bf16[1,4,384,128]{3,2,1,0:T(8,128)(2,1)}, bf16[1,4,384,128]{3,2,1,0:T(8,128)(2,1)}, u32[]{:S(2)}, u32[]{:S(2)}) collective-permute-start(bf16[1,4,384,128]{3,2,1,0:T(8,128)(2,1)} %get-tuple-element.73.refs_8_), channel_id=1, source_target_pairs={{0,2},{1,3},{2,0},{3,1},{4,6},{5,7},{6,4},{7,5},{8,10},{9,11},{10,... | collective-permute-start | bytes 1179656 | tf_op jit(solution)/shard_map/ppermute | solution.py:428
  26.4 8.1 %copy-start.1 = (s32[2,3]{1,0:T(2,128)S(1)}, s32[2,3]{1,0:T(2,128)}, u32[]{:S(2)}) copy-start(s32[2,3]{1,0:T(2,128)} %constant.47.clone) | copy-start | bytes 76
  26.4 18.1 %copy-start = (bf16[3,4,384,128]{3,2,1,0:T(8,128)(2,1)S(1)}, bf16[3,4,384,128]{3,2,1,0:T(8,128)(2,1)}, u32[]{:S(2)}) copy-start(bf16[3,4,384,128]{3,2,1,0:T(8,128)(2,1)} %get-tuple-element.75.refs_0_) | copy-start | bytes 3538948
  28.7 21.4 %collective-permute-start.13 = (bf16[1,4,384,128]{3,2,1,0:T(8,128)(2,1)}, bf16[1,4,384,128]{3,2,1,0:T(8,128)(2,1)}, u32[]{:S(2)}, u32[]{:S(2)}) collective-permute-start(bf16[1,4,384,128]{3,2,1,0:T(8,128)(2,1)} %get-tuple-element.85), channel_id=1, source_target_pairs={{0,4},{1,5},{4,8},{5,9},{6,2},{7,3},{8,12},{9,13},{10,6},{11,7},{1... | collective-permute-start | bytes 1179656 | tf_op jit(solution)/shard_map/ppermute | solution.py:440
  33.0 18.3 %collective-permute-start.12 = (bf16[1,4,384,128]{3,2,1,0:T(8,128)(2,1)}, bf16[1,4,384,128]{3,2,1,0:T(8,128)(2,1)}, u32[]{:S(2)}, u32[]{:S(2)}) collective-permute-start(bf16[1,4,384,128]{3,2,1,0:T(8,128)(2,1)} %get-tuple-element.80.refs_4_), channel_id=1, source_target_pairs={{2,6},{3,7},{4,0},{5,1},{6,10},{7,11},{8,4},{9,5},{10,14},{11,15},... | collective-permute-start | bytes 1179656 | tf_op jit(solution)/shard_map/ppermute | solution.py:440
  34.9 32.5 %collective-permute-start.10 = (bf16[1,4,384,128]{3,2,1,0:T(8,128)(2,1)}, bf16[1,4,384,128]{3,2,1,0:T(8,128)(2,1)S(1)}, u32[]{:S(2)}, u32[]{:S(2)}) collective-permute-start(bf16[1,4,384,128]{3,2,1,0:T(8,128)(2,1)} %get-tuple-element.83), channel_id=1, source_target_pairs={{0,2},{1,3},{2,0},{3,1},{4,6},{5,7},{6,4},{7,5},{8,10},{9,11},{10,... | collective-permute-start | bytes 1179656 | tf_op jit(solution)/shard_map/ppermute | solution.py:428
  43.8 23.6 %collective-permute-start.11 = (bf16[1,4,384,128]{3,2,1,0:T(8,128)(2,1)}, bf16[1,4,384,128]{3,2,1,0:T(8,128)(2,1)S(1)}, u32[]{:S(2)}, u32[]{:S(2)}) collective-permute-start(bf16[1,4,384,128]{3,2,1,0:T(8,128)(2,1)} %get-tuple-element.84), channel_id=1, source_target_pairs={{0,3},{1,2},{2,1},{3,0},{4,7},{5,6},{6,5},{7,4},{8,11},{9,10},{10,... | collective-permute-start | bytes 1179656 | tf_op jit(solution)/shard_map/ppermute | solution.py:428
  46.5 29.6 %collective-permute-start.9 = (bf16[1,4,384,128]{3,2,1,0:T(8,128)(2,1)}, bf16[1,4,384,128]{3,2,1,0:T(8,128)(2,1)S(1)}, u32[]{:S(2)}, u32[]{:S(2)}) collective-permute-start(bf16[1,4,384,128]{3,2,1,0:T(8,128)(2,1)} %get-tuple-element.82), channel_id=1, source_target_pairs={{0,4},{1,5},{4,8},{5,9},{6,2},{7,3},{8,12},{9,13},{10,6},{11,7},{1... | collective-permute-start | bytes 1179656 | tf_op jit(solution)/shard_map/ppermute | solution.py:440
  50.0 26.1 %collective-permute-start.8 = (bf16[1,4,384,128]{3,2,1,0:T(8,128)(2,1)}, bf16[1,4,384,128]{3,2,1,0:T(8,128)(2,1)S(1)}, u32[]{:S(2)}, u32[]{:S(2)}) collective-permute-start(bf16[1,4,384,128]{3,2,1,0:T(8,128)(2,1)} %get-tuple-element.81.refs_6_), channel_id=1, source_target_pairs={{2,6},{3,7},{4,0},{5,1},{6,10},{7,11},{8,4},{9,5},{10,14},{11,15},... | collective-permute-start | bytes 1179656 | tf_op jit(solution)/shard_map/ppermute | solution.py:440
  67.4 6.4 %copy-start.3 = (bf16[1,4,384,128]{3,2,1,0:T(8,128)(2,1)S(1)}, bf16[1,4,384,128]{3,2,1,0:T(8,128)(2,1)}, u32[]{:S(2)}) copy-start(bf16[1,4,384,128]{3,2,1,0:T(8,128)(2,1)} %get-tuple-element.77) | copy-start | bytes 1179652
  67.4 8.7 %copy-start.2 = (bf16[1,4,384,128]{3,2,1,0:T(8,128)(2,1)S(1)}, bf16[1,4,384,128]{3,2,1,0:T(8,128)(2,1)}, u32[]{:S(2)}) copy-start(bf16[1,4,384,128]{3,2,1,0:T(8,128)(2,1)} %get-tuple-element.78) | copy-start | bytes 1179652
  67.6 31.4 %collective-permute-start.17 = (bf16[1,4,768,128]{3,2,1,0:T(8,128)(2,1)S(1)}, bf16[1,4,768,128]{3,2,1,0:T(8,128)(2,1)S(1)}, u32[]{:S(2)}, u32[]{:S(2)}) collective-permute-start(bf16[1,4,768,128]{3,2,1,0:T(8,128)(2,1)S(1)} %get-tuple-element.93), channel_id=1, source_target_pairs={{0,4},{1,5},{4,8},{5,9},{6,2},{7,3},{8,12},{9,13},{10,6},{11,7},{1... | collective-permute-start | bytes 2359304 | tf_op jit(solution)/shard_map/ppermute | solution.py:440
  72.3 26.7 %collective-permute-start.16 = (bf16[1,4,768,128]{3,2,1,0:T(8,128)(2,1)S(1)}, bf16[1,4,768,128]{3,2,1,0:T(8,128)(2,1)S(1)}, u32[]{:S(2)}, u32[]{:S(2)}) collective-permute-start(bf16[1,4,768,128]{3,2,1,0:T(8,128)(2,1)S(1)} %get-tuple-element.88.refs_6_), channel_id=1, source_target_pairs={{2,6},{3,7},{4,0},{5,1},{6,10},{7,11},{8,4},{9,5},{10,14},{11,15},... | collective-permute-start | bytes 2359304 | tf_op jit(solution)/shard_map/ppermute | solution.py:440
  73.8 18.1 %collective-permute-start.4 = (bf16[1,4,384,128]{3,2,1,0:T(8,128)(2,1)S(1)}, bf16[1,4,384,128]{3,2,1,0:T(8,128)(2,1)S(1)}, u32[]{:S(2)}, u32[]{:S(2)}) collective-permute-start(bf16[1,4,384,128]{3,2,1,0:T(8,128)(2,1)S(1)} %copy-done.3), channel_id=1, source_target_pairs={{0,2},{1,3},{2,0},{3,1},{4,6},{5,7},{6,4},{7,5},{8,10},{9,11},{10,... | collective-permute-start | bytes 1179656 | tf_op jit(solution)/shard_map/ppermute | solution.py:428
  76.1 16.9 %collective-permute-start.5 = (bf16[1,4,384,128]{3,2,1,0:T(8,128)(2,1)S(1)}, bf16[1,4,384,128]{3,2,1,0:T(8,128)(2,1)S(1)}, u32[]{:S(2)}, u32[]{:S(2)}) collective-permute-start(bf16[1,4,384,128]{3,2,1,0:T(8,128)(2,1)S(1)} %copy-done.2), channel_id=1, source_target_pairs={{0,3},{1,2},{2,1},{3,0},{4,7},{5,6},{6,5},{7,4},{8,11},{9,10},{10,... | collective-permute-start | bytes 1179656 | tf_op jit(solution)/shard_map/ppermute | solution.py:428
  93.2 23.2 %collective-permute-start.15 = (bf16[1,4,768,128]{3,2,1,0:T(8,128)(2,1)S(1)}, bf16[1,4,768,128]{3,2,1,0:T(8,128)(2,1)S(1)}, u32[]{:S(2)}, u32[]{:S(2)}) collective-permute-start(bf16[1,4,768,128]{3,2,1,0:T(8,128)(2,1)S(1)} %get-tuple-element.92), channel_id=1, source_target_pairs={{0,4},{1,5},{4,8},{5,9},{6,2},{7,3},{8,12},{9,13},{10,6},{11,7},{1... | collective-permute-start | bytes 2359304 | tf_op jit(solution)/shard_map/ppermute | solution.py:440
  97.5 23.6 %collective-permute-start.14 = (bf16[1,4,768,128]{3,2,1,0:T(8,128)(2,1)S(1)}, bf16[1,4,768,128]{3,2,1,0:T(8,128)(2,1)S(1)}, u32[]{:S(2)}, u32[]{:S(2)}) collective-permute-start(bf16[1,4,768,128]{3,2,1,0:T(8,128)(2,1)S(1)} %get-tuple-element.91.refs_6_), channel_id=1, source_target_pairs={{2,6},{3,7},{4,0},{5,1},{6,10},{7,11},{8,4},{9,5},{10,14},{11,15},... | collective-permute-start | bytes 2359304 | tf_op jit(solution)/shard_map/ppermute | solution.py:440
  99.3 23.6 %collective-permute-start.18 = (bf16[1,6,384,128]{3,2,1,0:T(8,128)(2,1)S(1)}, bf16[1,6,384,128]{3,2,1,0:T(8,128)(2,1)S(1)}, u32[]{:S(2)}, u32[]{:S(2)}) collective-permute-start(bf16[1,6,384,128]{3,2,1,0:T(8,128)(2,1)S(1)} %get-tuple-element.101), channel_id=1, source_target_pairs={{0,1},{1,0},{2,3},{3,2},{4,5},{5,4},{6,7},{7,6},{8,9},{9,8},{10,11... | collective-permute-start | bytes 1769480 | tf_op jit(solution)/shard_map/ppermute | solution.py:428
  99.7 23.3 %collective-permute-start.19 = (bf16[1,6,384,128]{3,2,1,0:T(8,128)(2,1)S(1)}, bf16[1,6,384,128]{3,2,1,0:T(8,128)(2,1)S(1)}, u32[]{:S(2)}, u32[]{:S(2)}) collective-permute-start(bf16[1,6,384,128]{3,2,1,0:T(8,128)(2,1)S(1)} %get-tuple-element.102), channel_id=1, source_target_pairs={{0,2},{1,3},{2,0},{3,1},{4,6},{5,7},{6,4},{7,5},{8,10},{9,11},{10,... | collective-permute-start | bytes 1769480 | tf_op jit(solution)/shard_map/ppermute | solution.py:428
  100.9 26.3 %collective-permute-start.20 = (bf16[1,6,384,128]{3,2,1,0:T(8,128)(2,1)S(1)}, bf16[1,6,384,128]{3,2,1,0:T(8,128)(2,1)S(1)}, u32[]{:S(2)}, u32[]{:S(2)}) collective-permute-start(bf16[1,6,384,128]{3,2,1,0:T(8,128)(2,1)S(1)} %get-tuple-element.103), channel_id=1, source_target_pairs={{0,3},{1,2},{2,1},{3,0},{4,7},{5,6},{6,5},{7,4},{8,11},{9,10},{10,... | collective-permute-start | bytes 1769480 | tf_op jit(solution)/shard_map/ppermute | solution.py:428
  116.4 28.2 %collective-permute-start.21 = (bf16[2,2,384,128]{3,2,1,0:T(8,128)(2,1)S(1)}, bf16[2,2,384,128]{3,2,1,0:T(8,128)(2,1)S(1)}, u32[]{:S(2)}, u32[]{:S(2)}) collective-permute-start(bf16[2,2,384,128]{3,2,1,0:T(8,128)(2,1)S(1)} %get-tuple-element.106), channel_id=1, source_target_pairs={{0,4},{1,5},{4,8},{5,9},{6,2},{7,3},{8,12},{9,13},{10,6},{11,7},{1... | collective-permute-start | bytes 1179656 | tf_op jit(solution)/shard_map/ppermute | solution.py:440
  121.0 23.6 %collective-permute-start.22 = (bf16[2,2,384,128]{3,2,1,0:T(8,128)(2,1)S(1)}, bf16[2,2,384,128]{3,2,1,0:T(8,128)(2,1)S(1)}, u32[]{:S(2)}, u32[]{:S(2)}) collective-permute-start(bf16[2,2,384,128]{3,2,1,0:T(8,128)(2,1)S(1)} %get-tuple-element.107), channel_id=1, source_target_pairs={{2,6},{3,7},{4,0},{5,1},{6,10},{7,11},{8,4},{9,5},{10,14},{11,15},... | collective-permute-start | bytes 1179656 | tf_op jit(solution)/shard_map/ppermute | solution.py:440
  122.9 27.1 %collective-permute-start.28 = (bf16[1,4,384,128]{3,2,1,0:T(8,128)(2,1)S(1)}, bf16[1,4,384,128]{3,2,1,0:T(8,128)(2,1)S(1)}, u32[]{:S(2)}, u32[]{:S(2)}) collective-permute-start(bf16[1,4,384,128]{3,2,1,0:T(8,128)(2,1)S(1)} %get-tuple-element.115), channel_id=1, source_target_pairs={{0,1},{1,0},{2,3},{3,2},{4,5},{5,4},{6,7},{7,6},{8,9},{9,8},{10,11... | collective-permute-start | bytes 1179656 | tf_op jit(solution)/shard_map/ppermute | solution.py:428
  123.0 28.3 %collective-permute-start.29 = (bf16[1,4,384,128]{3,2,1,0:T(8,128)(2,1)S(1)}, bf16[1,4,384,128]{3,2,1,0:T(8,128)(2,1)S(1)}, u32[]{:S(2)}, u32[]{:S(2)}) collective-permute-start(bf16[1,4,384,128]{3,2,1,0:T(8,128)(2,1)S(1)} %get-tuple-element.116), channel_id=1, source_target_pairs={{0,2},{1,3},{2,0},{3,1},{4,6},{5,7},{6,4},{7,5},{8,10},{9,11},{10,... | collective-permute-start | bytes 1179656 | tf_op jit(solution)/shard_map/ppermute | solution.py:428
  127.2 24.2 %collective-permute-start.30 = (bf16[1,4,384,128]{3,2,1,0:T(8,128)(2,1)S(1)}, bf16[1,4,384,128]{3,2,1,0:T(8,128)(2,1)S(1)}, u32[]{:S(2)}, u32[]{:S(2)}) collective-permute-start(bf16[1,4,384,128]{3,2,1,0:T(8,128)(2,1)S(1)} %get-tuple-element.117), channel_id=1, source_target_pairs={{0,3},{1,2},{2,1},{3,0},{4,7},{5,6},{6,5},{7,4},{8,11},{9,10},{10,... | collective-permute-start | bytes 1179656 | tf_op jit(solution)/shard_map/ppermute | solution.py:428
  144.8 10.9 %collective-permute-start.24 = (bf16[1,4,384,128]{3,2,1,0:T(8,128)(2,1)S(1)}, bf16[1,4,384,128]{3,2,1,0:T(8,128)(2,1)S(1)}, u32[]{:S(2)}, u32[]{:S(2)}) collective-permute-start(bf16[1,4,384,128]{3,2,1,0:T(8,128)(2,1)S(1)} %get-tuple-element.110), channel_id=1, source_target_pairs={{0,2},{1,3},{2,0},{3,1},{4,6},{5,7},{6,4},{7,5},{8,10},{9,11},{10,... | collective-permute-start | bytes 1179656 | tf_op jit(solution)/shard_map/ppermute | solution.py:428
  145.7 12.0 %collective-permute-start.26 = (bf16[2,2,384,128]{3,2,1,0:T(8,128)(2,1)S(1)}, bf16[2,2,384,128]{3,2,1,0:T(8,128)(2,1)S(1)}, u32[]{:S(2)}, u32[]{:S(2)}) collective-permute-start(bf16[2,2,384,128]{3,2,1,0:T(8,128)(2,1)S(1)} %get-tuple-element.113), channel_id=1, source_target_pairs={{0,4},{1,5},{4,8},{5,9},{6,2},{7,3},{8,12},{9,13},{10,6},{11,7},{1... | collective-permute-start | bytes 1179656 | tf_op jit(solution)/shard_map/ppermute | solution.py:440
  150.0 11.8 %collective-permute-start.27 = (bf16[2,2,384,128]{3,2,1,0:T(8,128)(2,1)S(1)}, bf16[2,2,384,128]{3,2,1,0:T(8,128)(2,1)S(1)}, u32[]{:S(2)}, u32[]{:S(2)}) collective-permute-start(bf16[2,2,384,128]{3,2,1,0:T(8,128)(2,1)S(1)} %get-tuple-element.114), channel_id=1, source_target_pairs={{2,6},{3,7},{4,0},{5,1},{6,10},{7,11},{8,4},{9,5},{10,14},{11,15},... | collective-permute-start | bytes 1179656 | tf_op jit(solution)/shard_map/ppermute | solution.py:440
  151.3 17.5 %collective-permute-start.23 = (bf16[1,4,384,128]{3,2,1,0:T(8,128)(2,1)S(1)}, bf16[1,4,384,128]{3,2,1,0:T(8,128)(2,1)S(1)}, u32[]{:S(2)}, u32[]{:S(2)}) collective-permute-start(bf16[1,4,384,128]{3,2,1,0:T(8,128)(2,1)S(1)} %get-tuple-element.109), channel_id=1, source_target_pairs={{0,1},{1,0},{2,3},{3,2},{4,5},{5,4},{6,7},{7,6},{8,9},{9,8},{10,11... | collective-permute-start | bytes 1179656 | tf_op jit(solution)/shard_map/ppermute | solution.py:428
  151.4 17.4 %collective-permute-start.25 = (bf16[1,4,384,128]{3,2,1,0:T(8,128)(2,1)S(1)}, bf16[1,4,384,128]{3,2,1,0:T(8,128)(2,1)S(1)}, u32[]{:S(2)}, u32[]{:S(2)}) collective-permute-start(bf16[1,4,384,128]{3,2,1,0:T(8,128)(2,1)S(1)} %get-tuple-element.111), channel_id=1, source_target_pairs={{0,3},{1,2},{2,1},{3,0},{4,7},{5,6},{6,5},{7,4},{8,11},{9,10},{10,... | collective-permute-start | bytes 1179656 | tf_op jit(solution)/shard_map/ppermute | solution.py:428
  162.0 9.3 %collective-permute-start.31 = (bf16[1,2,384,128]{3,2,1,0:T(8,128)(2,1)S(1)}, bf16[1,2,384,128]{3,2,1,0:T(8,128)(2,1)S(1)}, u32[]{:S(2)}, u32[]{:S(2)}) collective-permute-start(bf16[1,2,384,128]{3,2,1,0:T(8,128)(2,1)S(1)} %get-tuple-element.119), channel_id=1, source_target_pairs={{0,1},{1,0},{2,3},{3,2},{4,5},{5,4},{6,7},{7,6},{8,9},{9,8},{10,11... | collective-permute-start | bytes 589832 | tf_op jit(solution)/shard_map/ppermute | solution.py:428
  162.1 9.2 %collective-permute-start.32 = (bf16[1,2,384,128]{3,2,1,0:T(8,128)(2,1)S(1)}, bf16[1,2,384,128]{3,2,1,0:T(8,128)(2,1)S(1)}, u32[]{:S(2)}, u32[]{:S(2)}) collective-permute-start(bf16[1,2,384,128]{3,2,1,0:T(8,128)(2,1)S(1)} %get-tuple-element.120), channel_id=1, source_target_pairs={{0,2},{1,3},{2,0},{3,1},{4,6},{5,7},{6,4},{7,5},{8,10},{9,11},{10,... | collective-permute-start | bytes 589832 | tf_op jit(solution)/shard_map/ppermute | solution.py:428
  162.1 11.0 %collective-permute-start.33 = (bf16[1,2,384,128]{3,2,1,0:T(8,128)(2,1)S(1)}, bf16[1,2,384,128]{3,2,1,0:T(8,128)(2,1)S(1)}, u32[]{:S(2)}, u32[]{:S(2)}) collective-permute-start(bf16[1,2,384,128]{3,2,1,0:T(8,128)(2,1)S(1)} %get-tuple-element.121), channel_id=1, source_target_pairs={{0,3},{1,2},{2,1},{3,0},{4,7},{5,6},{6,5},{7,4},{8,11},{9,10},{10,... | collective-permute-start | bytes 589832 | tf_op jit(solution)/shard_map/ppermute | solution.py:428

commit v3 on v2

--- a/solution.py
+++ b/solution.py
@@ -257,7 +257,7 @@
             return tuple(tops), tuple(totals)
 
         carry = (tuple(tops), tuple(totals))
-        if turn in (0, 3):
+        if turn in (2,):
             for b in range(3):
                 carry = blocks(b, carry)
         else:

time: 176 us -> 177 us (level)
  no operation moved by 1% of the time
where the time goes in v3:
time: 177 us; the launch traced here: 176 us
  Pallas kernels  85.9 us (49%)
  starting transfers between devices  54.7 us (31%)
  waiting for transfers between devices  32.2 us (18%)
    pallas_call x4, Pallas kernels, attend(): pl.pallas_call(functools.partial(attend_kernel, plan, rows, tile), grid=(...  62.8 us
    ppermute x12, starting transfers between devices, shift(): return lax.ppermute(value, RING, pairs)  34 us
    ppermute x22, waiting for transfers between devices, swap(): lax.ppermute(value, RING, [(i, i - i % team + (i % team ^ d)) for i in ra...  26.1 us
    ppermute x22, starting transfers between devices, swap(): lax.ppermute(value, RING, [(i, i - i % team + (i % team ^ d)) for i in ra...  20.7 us
    pallas_call x4, Pallas kernels, unpack(): pl.pallas_call(kernel, grid=(BLOCKS,), out_shape=[struct(shape, BF16)] *...  9.72 us
    pallas_call x2, Pallas kernels, pack(): pl.pallas_call(functools.partial(pack_kernel, jobs, step, start), grid=(B...  8.17 us
    ppermute x12, waiting for transfers between devices, shift(): return lax.ppermute(value, RING, pairs)  6.18 us
    pallas_call x4, Pallas kernels, relay(): pl.pallas_call(kernel, grid=(1,), out_shape=[kept(shape, BF16)] * kinds +...  4.36 us
  transfers between devices with their start and end apart: 34, of which 10 were waited for; matrix products, arithmetic and copies ran while one was open for 0% of the time, Pallas kernels for 46%

profile of v3, /device:TPU:0, one launch (start us, length us, event | category | flops | bytes accessed | tf_op | source)
XLA Modules:
  0.0 175.9 jit_solution(9132265762125600247)
XLA Ops:
  1.3 0.7 fusion.3
  2.0 0.1 fusion.1
  2.1 2.5 %pack.2 = (bf16[1,4,400,128]{3,2,1,0:T(8,128)(2,1)S(1)}, bf16[1,4,400,128]{3,2,1,0:T(8,128)(2,1)S(1)}, bf16[1,4,400,128]{3,2,1,0:T(8,128)(2,1)S(1)}, bf16[1,4,400,128]{3,2,1,0:T(8,128)(2,1)S(1)}) custom-call(s32[4]{0:T(128)S(1)} %iota_xor_fusion.places_ref, s32[6]{0:T(128)S(1)} %convert_element_type.10.flags_ref, bf16[1,384,2048]{2,1,0:T(8,128)(2,1)} %refs_0_.3, ...), custom_call_target="tpu_custom_call" | custom-call | bytes 3276800 | tf_op jit(solution)/shard_map/pack/pallas_call | solution.py:67
  4.7 0.5 collective-permute-start
  5.2 2.6 %collective-permute-start.1 = (bf16[1,4,400,128]{3,2,1,0:T(8,128)(2,1)S(1)}, bf16[1,4,400,128]{3,2,1,0:T(8,128)(2,1)}, u32[]{:S(2)}, u32[]{:S(2)}) collective-permute-start(bf16[1,4,400,128]{3,2,1,0:T(8,128)(2,1)S(1)} %get-tuple-element.71), channel_id=1, source_target_pairs={{0,2},{1,3},{2,0},{3,1},{4,6},{5,7},{6,4},{7,5},{8,10},{9,11},{10,... | collective-permute-start | bytes 1228808 | tf_op jit(solution)/shard_map/ppermute | solution.py:428
  7.8 5.6 %pack.3 = (bf16[1,4,384,128]{3,2,1,0:T(8,128)(2,1)}, bf16[1,4,384,128]{3,2,1,0:T(8,128)(2,1)}, bf16[1,4,384,128]{3,2,1,0:T(8,128)(2,1)}, bf16[1,4,384,128]{3,2,1...) custom-call(s32[4]{0:T(128)S(1)} %iota_xor_fusion.places_ref, ...), custom_call_target="tpu_custom_call" | custom-call | bytes 9437184 | tf_op jit(solution)/shard_map/pack/pallas_call | solution.py:67
  13.5 0.2 collective-permute-start.3
  13.7 1.7 collective-permute-start.7
  15.4 0.3 collective-permute-start.6
  15.7 2.5 %collective-permute-done.1.refs_2_.refs_6_ = bf16[1,4,400,128]{3,2,1,0:T(8,128)(2,1)} collective-permute-done((bf16[1,4,400,128]{3,2,1,0:T(8,128)(2,1)S(1)}, bf16[1,4,400,128]{3,2,1,0:T(8,128)(2,1)}, u32[]{:S(2)}, u32[]{:S(2)}) %collective-permute-start.1) | collective-permute-done | bytes 409632 | tf_op jit(solution)/shard_map/ppermute | solution.py:428
  18.2 8.3 %collective-permute-done.2.refs_3_.refs_7_ = bf16[1,4,400,128]{3,2,1,0:T(8,128)(2,1)} collective-permute-done((bf16[1,4,400,128]{3,2,1,0:T(8,128)(2,1)S(1)}, bf16[1,4,400,128]{3,2,1,0:T(8,128)(2,1)}, u32[]{:S(2)}, u32[]{:S(2)}) %collective-permute-start.2) | collective-permute-done | bytes 409632 | tf_op jit(solution)/shard_map/ppermute | solution.py:428
  26.4 2.1 %relay.4 = (bf16[1,4,384,128]{3,2,1,0:T(8,128)(2,1)}, bf16[1,4,384,128]{3,2,1,0:T(8,128)(2,1)}, bf16[4,16,128]{2,1,0:T(8,128)(2,1)S(1)}) custom-call(bf16[1,4,400,128]{3,2,1,0:T(8,128)(2,1)S(1)} %get-tuple-element.69.refs_0_.refs_4_, bf16[1,4,400,128]{3,2,1,0:T(8,128)(2,1)S(1)} %collective-permute-done.refs_4_.refs_1_.refs_5_, ...), custom_call_target="tpu_custom_call" | custom-call | bytes 1572864 | tf_op jit(solution)/shard_map/relay/pallas_call | solution.py:116
  28.5 0.1 copy.29
  28.7 4.3 %collective-permute-start.13 = (bf16[1,4,384,128]{3,2,1,0:T(8,128)(2,1)}, bf16[1,4,384,128]{3,2,1,0:T(8,128)(2,1)}, u32[]{:S(2)}, u32[]{:S(2)}) collective-permute-start(bf16[1,4,384,128]{3,2,1,0:T(8,128)(2,1)} %get-tuple-element.85), channel_id=1, source_target_pairs={{0,4},{1,5},{4,8},{5,9},{6,2},{7,3},{8,12},{9,13},{10,6},{11,7},{1... | collective-permute-start | bytes 1179656 | tf_op jit(solution)/shard_map/ppermute | solution.py:440
  33.0 1.3 collective-permute-start.12
  34.3 0.1 fusion.4
  34.4 0.1 pad_add_fusion
  34.5 0.1 copy.30
  34.6 0.1 pad_add_fusion.1.table_ref
  34.6 0.2 collective-permute-done.7.refs_3_
  34.9 2.3 %collective-permute-start.10 = (bf16[1,4,384,128]{3,2,1,0:T(8,128)(2,1)}, bf16[1,4,384,128]{3,2,1,0:T(8,128)(2,1)S(1)}, u32[]{:S(2)}, u32[]{:S(2)}) collective-permute-start(bf16[1,4,384,128]{3,2,1,0:T(8,128)(2,1)} %get-tuple-element.83), channel_id=1, source_target_pairs={{0,2},{1,3},{2,0},{3,1},{4,6},{5,7},{6,4},{7,5},{8,10},{9,11},{10,... | collective-permute-start | bytes 1179656 | tf_op jit(solution)/shard_map/ppermute | solution.py:428
  37.2 6.6 %collective-permute-done.6.refs_2_ = bf16[1,4,384,128]{3,2,1,0:T(8,128)(2,1)} collective-permute-done((bf16[1,4,384,128]{3,2,1,0:T(8,128)(2,1)}, bf16[1,4,384,128]{3,2,1,0:T(8,128)(2,1)}, u32[]{:S(2)}, u32[]{:S(2)}) %collective-permute-start.6) | collective-permute-done | bytes 393248 | tf_op jit(solution)/shard_map/ppermute | solution.py:428
  43.8 0.8 collective-permute-start.11
  44.6 2.0 %relay.5 = (bf16[1,4,384,128]{3,2,1,0:T(8,128)(2,1)}, bf16[1,4,384,128]{3,2,1,0:T(8,128)(2,1)}) custom-call(bf16[3,4,384,128]{3,2,1,0:T(8,128)(2,1)S(1)} %copy-done, bf16[3,4,384,128]{3,2,1,0:T(8,128)(2,1)S(1)} %collective-permute-done.3.refs_1_, bf16[1,4,384,128]{3,2,1,0:T(8,128)(2,1)} %collective-permute-done.6.refs_2_, ...), custom_call_target="tpu_custom_call" | custom-call | bytes 1572864 | tf_op jit(solution)/shard_map/relay/pallas_call | solution.py:116
  46.5 3.5 %collective-permute-start.9 = (bf16[1,4,384,128]{3,2,1,0:T(8,128)(2,1)}, bf16[1,4,384,128]{3,2,1,0:T(8,128)(2,1)S(1)}, u32[]{:S(2)}, u32[]{:S(2)}) collective-permute-start(bf16[1,4,384,128]{3,2,1,0:T(8,128)(2,1)} %get-tuple-element.82), channel_id=1, source_target_pairs={{0,4},{1,5},{4,8},{5,9},{6,2},{7,3},{8,12},{9,13},{10,6},{11,7},{1... | collective-permute-start | bytes 1179656 | tf_op jit(solution)/shard_map/ppermute | solution.py:440
  50.0 1.3 collective-permute-start.8
  51.3 16.2 %attend.4 = (bf16[4,2,384,128]{3,2,1,0:T(8,128)(2,1)S(1)}, f32[4,2,384,128]{3,2,1,0:T(8,128)S(1)}, bf16[2,2,384,128]{3,2,1,0:T(8,128)(2,1)S(1)}, bf16[2,2,384,128]{3,2,1,0:T(8,128)(2,1)S(1)}) custom-call(s32[4,9]{1,0:T(4,128)S(1)} %pad_add_fusion.1.table_ref, bf16[1,4,400,128]{3,2,1,0:T(8,128)(2,1)S(1)} %get-tuple-element.69.refs_0_.refs_4_, ...), custom_call_target="tpu_custom_call" | custom-call | flops 5435817984 | bytes 8388608 | tf_op jit(solution)/shard_map/attend/pallas_call | solution.py:304
  67.6 0.2 relay.6
  67.7 4.7 %collective-permute-start.17 = (bf16[1,4,768,128]{3,2,1,0:T(8,128)(2,1)S(1)}, bf16[1,4,768,128]{3,2,1,0:T(8,128)(2,1)S(1)}, u32[]{:S(2)}, u32[]{:S(2)}) collective-permute-start(bf16[1,4,768,128]{3,2,1,0:T(8,128)(2,1)S(1)} %get-tuple-element.93), channel_id=1, source_target_pairs={{0,4},{1,5},{4,8},{5,9},{6,2},{7,3},{8,12},{9,13},{10,6},{11,7},{1... | collective-permute-start | bytes 2359304 | tf_op jit(solution)/shard_map/ppermute | solution.py:440
  72.5 1.5 collective-permute-start.16
  73.9 2.3 %collective-permute-start.4 = (bf16[1,4,384,128]{3,2,1,0:T(8,128)(2,1)S(1)}, bf16[1,4,384,128]{3,2,1,0:T(8,128)(2,1)S(1)}, u32[]{:S(2)}, u32[]{:S(2)}) collective-permute-start(bf16[1,4,384,128]{3,2,1,0:T(8,128)(2,1)S(1)} %copy-done.3), channel_id=1, source_target_pairs={{0,2},{1,3},{2,0},{3,1},{4,6},{5,7},{6,4},{7,5},{8,10},{9,11},{10,... | collective-permute-start | bytes 1179656 | tf_op jit(solution)/shard_map/ppermute | solution.py:428
  76.3 15.9 %attend.5 = (bf16[4,2,384,128]{3,2,1,0:T(8,128)(2,1)S(1)}, f32[4,2,384,128]{3,2,1,0:T(8,128)S(1)}, bf16[2,2,384,128]{3,2,1,0:T(8,128)(2,1)S(1)}, bf16[2,2,384,128]{3,2,1,0:T(8,128)(2,1)S(1)}) custom-call(s32[4,9]{1,0:T(4,128)S(1)} %pad_add_fusion.1.table_ref, bf16[3,4,384,128]{3,2,1,0:T(8,128)(2,1)S(1)} %copy-done, ...), custom_call_target="tpu_custom_call" | custom-call | flops 5435817984 | bytes 8388608 | tf_op jit(solution)/shard_map/attend/pallas_call | solution.py:304
  92.2 1.0 collective-permute-done.5.refs_3_
  93.2 0.2 relay.7
  93.4 4.2 %collective-permute-start.15 = (bf16[1,4,768,128]{3,2,1,0:T(8,128)(2,1)S(1)}, bf16[1,4,768,128]{3,2,1,0:T(8,128)(2,1)S(1)}, u32[]{:S(2)}, u32[]{:S(2)}) collective-permute-start(bf16[1,4,768,128]{3,2,1,0:T(8,128)(2,1)S(1)} %get-tuple-element.92), channel_id=1, source_target_pairs={{0,4},{1,5},{4,8},{5,9},{6,2},{7,3},{8,12},{9,13},{10,6},{11,7},{1... | collective-permute-start | bytes 2359304 | tf_op jit(solution)/shard_map/ppermute | solution.py:440
  97.6 1.5 collective-permute-start.14
  99.2 0.3 finish.4
  99.5 0.4 collective-permute-start.18
  99.9 1.2 collective-permute-start.19
  101.0 0.4 collective-permute-start.20
  101.4 15.4 %attend.6 = (bf16[4,2,384,128]{3,2,1,0:T(8,128)(2,1)S(1)}, f32[4,2,384,128]{3,2,1,0:T(8,128)S(1)}, bf16[2,2,384,128]{3,2,1,0:T(8,128)(2,1)S(1)}, bf16[2,2,384,128]{3,2,1,0:T(8,128)(2,1)S(1)}) custom-call(s32[4,9]{1,0:T(4,128)S(1)} %pad_add_fusion.1.table_ref, bf16[3,4,384,128]{3,2,1,0:T(8,128)(2,1)S(1)} %copy-done, ...), custom_call_target="tpu_custom_call" | custom-call | flops 5435817984 | bytes 8388608 | tf_op jit(solution)/shard_map/attend/pallas_call | solution.py:304
  116.8 4.6 %collective-permute-start.21 = (bf16[2,2,384,128]{3,2,1,0:T(8,128)(2,1)S(1)}, bf16[2,2,384,128]{3,2,1,0:T(8,128)(2,1)S(1)}, u32[]{:S(2)}, u32[]{:S(2)}) collective-permute-start(bf16[2,2,384,128]{3,2,1,0:T(8,128)(2,1)S(1)} %get-tuple-element.106), channel_id=1, source_target_pairs={{0,4},{1,5},{4,8},{5,9},{6,2},{7,3},{8,12},{9,13},{10,6},{11,7},{1... | collective-permute-start | bytes 1179656 | tf_op jit(solution)/shard_map/ppermute | solution.py:440
  121.4 1.6 collective-permute-start.22
  122.9 0.3 finish.5
  123.2 0.1 collective-permute-start.28
  123.3 1.2 collective-permute-start.29
  124.5 2.9 %collective-permute-done.20.refs_9_.refs_6_.refs_3_.refs_7_ = bf16[1,6,384,128]{3,2,1,0:T(8,128)(2,1)S(1)} collective-permute-done((bf16[1,6,384,128]{3,2,1,0:T(8,128)(2,1)S(1)}, bf16[1,6,384,128]{3,2,1,0:T(8,128)(2,1)S(1)}, u32[]{:S(2)}, u32[]{:S(2)}) %collective-permute-start.20) | collective-permute-done | bytes 589856 | tf_op jit(solution)/shard_map/ppermute | solution.py:428
  127.4 2.2 %collective-permute-start.30 = (bf16[1,4,384,128]{3,2,1,0:T(8,128)(2,1)S(1)}, bf16[1,4,384,128]{3,2,1,0:T(8,128)(2,1)S(1)}, u32[]{:S(2)}, u32[]{:S(2)}) collective-permute-start(bf16[1,4,384,128]{3,2,1,0:T(8,128)(2,1)S(1)} %get-tuple-element.117), channel_id=1, source_target_pairs={{0,3},{1,2},{2,1},{3,0},{4,7},{5,6},{6,5},{7,4},{8,11},{9,10},{10,... | collective-permute-start | bytes 1179656 | tf_op jit(solution)/shard_map/ppermute | solution.py:428
  129.6 15.4 %attend.7 = (bf16[4,2,384,128]{3,2,1,0:T(8,128)(2,1)S(1)}, f32[4,2,384,128]{3,2,1,0:T(8,128)S(1)}, bf16[2,2,384,128]{3,2,1,0:T(8,128)(2,1)S(1)}, bf16[2,2,384,128]{3,2,1,0:T(8,128)(2,1)S(1)}) custom-call(s32[4,9]{1,0:T(4,128)S(1)} %pad_add_fusion.1.table_ref, bf16[3,4,384,128]{3,2,1,0:T(8,128)(2,1)S(1)} %copy-done, ...), custom_call_target="tpu_custom_call" | custom-call | flops 5435817984 | bytes 8388608 | tf_op jit(solution)/shard_map/attend/pallas_call | solution.py:304
  145.0 0.2 finish.6
  145.1 0.9 collective-permute-start.24
  146.0 4.3 %collective-permute-start.26 = (bf16[2,2,384,128]{3,2,1,0:T(8,128)(2,1)S(1)}, bf16[2,2,384,128]{3,2,1,0:T(8,128)(2,1)S(1)}, u32[]{:S(2)}, u32[]{:S(2)}) collective-permute-start(bf16[2,2,384,128]{3,2,1,0:T(8,128)(2,1)S(1)} %get-tuple-element.113), channel_id=1, source_target_pairs={{0,4},{1,5},{4,8},{5,9},{6,2},{7,3},{8,12},{9,13},{10,6},{11,7},{1... | collective-permute-start | bytes 1179656 | tf_op jit(solution)/shard_map/ppermute | solution.py:440
  150.3 1.3 collective-permute-start.27
  151.7 1.6 collective-permute-start.25
  153.3 2.7 %collective-permute-done.24.refs_6_.refs_2_ = bf16[1,4,384,128]{3,2,1,0:T(8,128)(2,1)S(1)} collective-permute-done((bf16[1,4,384,128]{3,2,1,0:T(8,128)(2,1)S(1)}, bf16[1,4,384,128]{3,2,1,0:T(8,128)(2,1)S(1)}, u32[]{:S(2)}, u32[]{:S(2)}) %collective-permute-start.24) | collective-permute-done | bytes 393248 | tf_op jit(solution)/shard_map/ppermute | solution.py:428
  156.0 2.0 %collective-permute-done.26.refs_1_ = bf16[2,2,384,128]{3,2,1,0:T(8,128)(2,1)S(1)} collective-permute-done((bf16[2,2,384,128]{3,2,1,0:T(8,128)(2,1)S(1)}, bf16[2,2,384,128]{3,2,1,0:T(8,128)(2,1)S(1)}, u32[]{:S(2)}, u32[]{:S(2)}) %collective-permute-start.26) | collective-permute-done | bytes 393248 | tf_op jit(solution)/shard_map/ppermute | solution.py:440
  158.0 4.1 %collective-permute-done.27.refs_2_ = bf16[2,2,384,128]{3,2,1,0:T(8,128)(2,1)S(1)} collective-permute-done((bf16[2,2,384,128]{3,2,1,0:T(8,128)(2,1)S(1)}, bf16[2,2,384,128]{3,2,1,0:T(8,128)(2,1)S(1)}, u32[]{:S(2)}, u32[]{:S(2)}) %collective-permute-start.27) | collective-permute-done | bytes 393248 | tf_op jit(solution)/shard_map/ppermute | solution.py:440
  162.2 0.1 finish.7
  162.5 1.8 %collective-permute-start.33 = (bf16[1,2,384,128]{3,2,1,0:T(8,128)(2,1)S(1)}, bf16[1,2,384,128]{3,2,1,0:T(8,128)(2,1)S(1)}, u32[]{:S(2)}, u32[]{:S(2)}) collective-permute-start(bf16[1,2,384,128]{3,2,1,0:T(8,128)(2,1)S(1)} %get-tuple-element.121), channel_id=1, source_target_pairs={{0,3},{1,2},{2,1},{3,0},{4,7},{5,6},{6,5},{7,4},{8,11},{9,10},{10,... | collective-permute-start | bytes 589832 | tf_op jit(solution)/shard_map/ppermute | solution.py:428
  164.2 2.4 %unpack.4 = (bf16[1,384,2048]{2,1,0:T(8,128)(2,1)}, bf16[1,384,2048]{2,1,0:T(8,128)(2,1)}, bf16[1,384,2048]{2,1,0:T(8,128)(2,1)}, bf16[1,384,2048]{2,1,0:T(8,128)(2,1)}) custom-call(s32[4]{0:T(128)S(1)} %iota_xor_fusion.places_ref, bf16[1,6,384,128]{3,2,1,0:T(8,128)(2,1)S(1)} %get-tuple-element.97.refs_7_.refs_0_.refs_4_, ...), custom_call_target="tpu_custom_call" | custom-call | bytes 3145728 | tf_op jit(solution)/shard_map/unpack/pallas_call | solution.py:395
  166.7 2.4 %unpack.5 = (bf16[1,384,2048]{2,1,0:T(8,128)(2,1)}, bf16[1,384,2048]{2,1,0:T(8,128)(2,1)}, bf16[1,384,2048]{2,1,0:T(8,128)(2,1)}, bf16[1,384,2048]{2,1,0:T(8,128)(2,1)}) custom-call(s32[4]{0:T(128)S(1)} %iota_xor_fusion.places_ref, ...), custom_call_target="tpu_custom_call", output_to_operand_aliasing={{0}: (9, {}), {1}: (10, {}), {2}: (11, {}), {3}: (12, {})} | custom-call | bytes 3145728 | tf_op jit(solution)/shard_map/unpack/pallas_call | solution.py:395
  169.1 2.5 %unpack.6 = (bf16[1,384,2048]{2,1,0:T(8,128)(2,1)}, bf16[1,384,2048]{2,1,0:T(8,128)(2,1)}, bf16[1,384,2048]{2,1,0:T(8,128)(2,1)}, bf16[1,384,2048]{2,1,0:T(8,128)(2,1)}) custom-call(s32[4]{0:T(128)S(1)} %iota_xor_fusion.places_ref, ...), custom_call_target="tpu_custom_call", output_to_operand_aliasing={{0}: (9, {}), {1}: (10, {}), {2}: (11, {}), {3}: (12, {})} | custom-call | bytes 3145728 | tf_op jit(solution)/shard_map/unpack/pallas_call | solution.py:395
  171.6 1.9 %collective-permute-done.33.refs_7_ = bf16[1,2,384,128]{3,2,1,0:T(8,128)(2,1)S(1)} collective-permute-done((bf16[1,2,384,128]{3,2,1,0:T(8,128)(2,1)S(1)}, bf16[1,2,384,128]{3,2,1,0:T(8,128)(2,1)S(1)}, u32[]{:S(2)}, u32[]{:S(2)}) %collective-permute-start.33) | collective-permute-done | bytes 196640 | tf_op jit(solution)/shard_map/ppermute | solution.py:428
  173.5 2.4 %unpack.7 = (bf16[1,384,2048]{2,1,0:T(8,128)(2,1)}, bf16[1,384,2048]{2,1,0:T(8,128)(2,1)}, bf16[1,384,2048]{2,1,0:T(8,128)(2,1)}, bf16[1,384,2048]{2,1,0:T(8,128)(2,1)}) custom-call(s32[4]{0:T(128)S(1)} %iota_xor_fusion.places_ref, ...), custom_call_target="tpu_custom_call", output_to_operand_aliasing={{0}: (9, {}), {1}: (10, {}), {2}: (11, {}), {3}: (12, {})} | custom-call | bytes 3145728 | tf_op jit(solution)/shard_map/unpack/pallas_call | solution.py:395
  (47 shorter events, 0.5 us)
Async XLA Ops:
  4.7 3.2 %collective-permute-start = (bf16[1,4,400,128]{3,2,1,0:T(8,128)(2,1)S(1)}, bf16[1,4,400,128]{3,2,1,0:T(8,128)(2,1)S(1)}, u32[]{:S(2)}, u32[]{:S(2)}) collective-permute-start(bf16[1,4,400,128]{3,2,1,0:T(8,128)(2,1)S(1)} %get-tuple-element.70), channel_id=1, source_target_pairs={{0,1},{1,0},{2,3},{3,2},{4,5},{5,4},{6,7},{7,6},{8,9},{9,8},{10,11... | collective-permute-start | bytes 1228808 | tf_op jit(solution)/shard_map/ppermute | solution.py:428
  5.2 13.0 %collective-permute-start.1 = (bf16[1,4,400,128]{3,2,1,0:T(8,128)(2,1)S(1)}, bf16[1,4,400,128]{3,2,1,0:T(8,128)(2,1)}, u32[]{:S(2)}, u32[]{:S(2)}) collective-permute-start(bf16[1,4,400,128]{3,2,1,0:T(8,128)(2,1)S(1)} %get-tuple-element.71), channel_id=1, source_target_pairs={{0,2},{1,3},{2,0},{3,1},{4,6},{5,7},{6,4},{7,5},{8,10},{9,11},{10,... | collective-permute-start | bytes 1228808 | tf_op jit(solution)/shard_map/ppermute | solution.py:428
  7.7 18.7 %collective-permute-start.2 = (bf16[1,4,400,128]{3,2,1,0:T(8,128)(2,1)S(1)}, bf16[1,4,400,128]{3,2,1,0:T(8,128)(2,1)}, u32[]{:S(2)}, u32[]{:S(2)}) collective-permute-start(bf16[1,4,400,128]{3,2,1,0:T(8,128)(2,1)S(1)} %get-tuple-element.72), channel_id=1, source_target_pairs={{0,3},{1,2},{2,1},{3,0},{4,7},{5,6},{6,5},{7,4},{8,11},{9,10},{10,... | collective-permute-start | bytes 1228808 | tf_op jit(solution)/shard_map/ppermute | solution.py:428
  13.5 31.1 %collective-permute-start.3 = (bf16[3,4,384,128]{3,2,1,0:T(8,128)(2,1)}, bf16[3,4,384,128]{3,2,1,0:T(8,128)(2,1)S(1)}, u32[]{:S(2)}, u32[]{:S(2)}) collective-permute-start(bf16[3,4,384,128]{3,2,1,0:T(8,128)(2,1)} %get-tuple-element.76), channel_id=1, source_target_pairs={{0,1},{1,0},{2,3},{3,2},{4,5},{5,4},{6,7},{7,6},{8,9},{9,8},{10,11... | collective-permute-start | bytes 3538952 | tf_op jit(solution)/shard_map/ppermute | solution.py:428
  13.7 21.2 %collective-permute-start.7 = (bf16[1,4,384,128]{3,2,1,0:T(8,128)(2,1)}, bf16[1,4,384,128]{3,2,1,0:T(8,128)(2,1)}, u32[]{:S(2)}, u32[]{:S(2)}) collective-permute-start(bf16[1,4,384,128]{3,2,1,0:T(8,128)(2,1)} %get-tuple-element.79), channel_id=1, source_target_pairs={{0,3},{1,2},{2,1},{3,0},{4,7},{5,6},{6,5},{7,4},{8,11},{9,10},{10,... | collective-permute-start | bytes 1179656 | tf_op jit(solution)/shard_map/ppermute | solution.py:428
  15.4 28.4 %collective-permute-start.6 = (bf16[1,4,384,128]{3,2,1,0:T(8,128)(2,1)}, bf16[1,4,384,128]{3,2,1,0:T(8,128)(2,1)}, u32[]{:S(2)}, u32[]{:S(2)}) collective-permute-start(bf16[1,4,384,128]{3,2,1,0:T(8,128)(2,1)} %get-tuple-element.73.refs_8_), channel_id=1, source_target_pairs={{0,2},{1,3},{2,0},{3,1},{4,6},{5,7},{6,4},{7,5},{8,10},{9,11},{10,... | collective-permute-start | bytes 1179656 | tf_op jit(solution)/shard_map/ppermute | solution.py:428
  26.4 8.1 %copy-start.1 = (s32[2,3]{1,0:T(2,128)S(1)}, s32[2,3]{1,0:T(2,128)}, u32[]{:S(2)}) copy-start(s32[2,3]{1,0:T(2,128)} %constant.47.clone) | copy-start | bytes 76
  26.4 18.1 %copy-start = (bf16[3,4,384,128]{3,2,1,0:T(8,128)(2,1)S(1)}, bf16[3,4,384,128]{3,2,1,0:T(8,128)(2,1)}, u32[]{:S(2)}) copy-start(bf16[3,4,384,128]{3,2,1,0:T(8,128)(2,1)} %get-tuple-element.75.refs_0_) | copy-start | bytes 3538948
  28.7 21.4 %collective-permute-start.13 = (bf16[1,4,384,128]{3,2,1,0:T(8,128)(2,1)}, bf16[1,4,384,128]{3,2,1,0:T(8,128)(2,1)}, u32[]{:S(2)}, u32[]{:S(2)}) collective-permute-start(bf16[1,4,384,128]{3,2,1,0:T(8,128)(2,1)} %get-tuple-element.85), channel_id=1, source_target_pairs={{0,4},{1,5},{4,8},{5,9},{6,2},{7,3},{8,12},{9,13},{10,6},{11,7},{1... | collective-permute-start | bytes 1179656 | tf_op jit(solution)/shard_map/ppermute | solution.py:440
  33.0 18.3 %collective-permute-start.12 = (bf16[1,4,384,128]{3,2,1,0:T(8,128)(2,1)}, bf16[1,4,384,128]{3,2,1,0:T(8,128)(2,1)}, u32[]{:S(2)}, u32[]{:S(2)}) collective-permute-start(bf16[1,4,384,128]{3,2,1,0:T(8,128)(2,1)} %get-tuple-element.80.refs_4_), channel_id=1, source_target_pairs={{2,6},{3,7},{4,0},{5,1},{6,10},{7,11},{8,4},{9,5},{10,14},{11,15},... | collective-permute-start | bytes 1179656 | tf_op jit(solution)/shard_map/ppermute | solution.py:440
  34.9 32.7 %collective-permute-start.10 = (bf16[1,4,384,128]{3,2,1,0:T(8,128)(2,1)}, bf16[1,4,384,128]{3,2,1,0:T(8,128)(2,1)S(1)}, u32[]{:S(2)}, u32[]{:S(2)}) collective-permute-start(bf16[1,4,384,128]{3,2,1,0:T(8,128)(2,1)} %get-tuple-element.83), channel_id=1, source_target_pairs={{0,2},{1,3},{2,0},{3,1},{4,6},{5,7},{6,4},{7,5},{8,10},{9,11},{10,... | collective-permute-start | bytes 1179656 | tf_op jit(solution)/shard_map/ppermute | solution.py:428
  43.8 23.7 %collective-permute-start.11 = (bf16[1,4,384,128]{3,2,1,0:T(8,128)(2,1)}, bf16[1,4,384,128]{3,2,1,0:T(8,128)(2,1)S(1)}, u32[]{:S(2)}, u32[]{:S(2)}) collective-permute-start(bf16[1,4,384,128]{3,2,1,0:T(8,128)(2,1)} %get-tuple-element.84), channel_id=1, source_target_pairs={{0,3},{1,2},{2,1},{3,0},{4,7},{5,6},{6,5},{7,4},{8,11},{9,10},{10,... | collective-permute-start | bytes 1179656 | tf_op jit(solution)/shard_map/ppermute | solution.py:428
  46.5 29.8 %collective-permute-start.9 = (bf16[1,4,384,128]{3,2,1,0:T(8,128)(2,1)}, bf16[1,4,384,128]{3,2,1,0:T(8,128)(2,1)S(1)}, u32[]{:S(2)}, u32[]{:S(2)}) collective-permute-start(bf16[1,4,384,128]{3,2,1,0:T(8,128)(2,1)} %get-tuple-element.82), channel_id=1, source_target_pairs={{0,4},{1,5},{4,8},{5,9},{6,2},{7,3},{8,12},{9,13},{10,6},{11,7},{1... | collective-permute-start | bytes 1179656 | tf_op jit(solution)/shard_map/ppermute | solution.py:440
  50.0 26.3 %collective-permute-start.8 = (bf16[1,4,384,128]{3,2,1,0:T(8,128)(2,1)}, bf16[1,4,384,128]{3,2,1,0:T(8,128)(2,1)S(1)}, u32[]{:S(2)}, u32[]{:S(2)}) collective-permute-start(bf16[1,4,384,128]{3,2,1,0:T(8,128)(2,1)} %get-tuple-element.81.refs_6_), channel_id=1, source_target_pairs={{2,6},{3,7},{4,0},{5,1},{6,10},{7,11},{8,4},{9,5},{10,14},{11,15},... | collective-permute-start | bytes 1179656 | tf_op jit(solution)/shard_map/ppermute | solution.py:440
  67.5 6.4 %copy-start.3 = (bf16[1,4,384,128]{3,2,1,0:T(8,128)(2,1)S(1)}, bf16[1,4,384,128]{3,2,1,0:T(8,128)(2,1)}, u32[]{:S(2)}) copy-start(bf16[1,4,384,128]{3,2,1,0:T(8,128)(2,1)} %get-tuple-element.77) | copy-start | bytes 1179652
  67.6 8.7 %copy-start.2 = (bf16[1,4,384,128]{3,2,1,0:T(8,128)(2,1)S(1)}, bf16[1,4,384,128]{3,2,1,0:T(8,128)(2,1)}, u32[]{:S(2)}) copy-start(bf16[1,4,384,128]{3,2,1,0:T(8,128)(2,1)} %get-tuple-element.78) | copy-start | bytes 1179652
  67.7 31.4 %collective-permute-start.17 = (bf16[1,4,768,128]{3,2,1,0:T(8,128)(2,1)S(1)}, bf16[1,4,768,128]{3,2,1,0:T(8,128)(2,1)S(1)}, u32[]{:S(2)}, u32[]{:S(2)}) collective-permute-start(bf16[1,4,768,128]{3,2,1,0:T(8,128)(2,1)S(1)} %get-tuple-element.93), channel_id=1, source_target_pairs={{0,4},{1,5},{4,8},{5,9},{6,2},{7,3},{8,12},{9,13},{10,6},{11,7},{1... | collective-permute-start | bytes 2359304 | tf_op jit(solution)/shard_map/ppermute | solution.py:440
  72.5 26.7 %collective-permute-start.16 = (bf16[1,4,768,128]{3,2,1,0:T(8,128)(2,1)S(1)}, bf16[1,4,768,128]{3,2,1,0:T(8,128)(2,1)S(1)}, u32[]{:S(2)}, u32[]{:S(2)}) collective-permute-start(bf16[1,4,768,128]{3,2,1,0:T(8,128)(2,1)S(1)} %get-tuple-element.88.refs_6_), channel_id=1, source_target_pairs={{2,6},{3,7},{4,0},{5,1},{6,10},{7,11},{8,4},{9,5},{10,14},{11,15},... | collective-permute-start | bytes 2359304 | tf_op jit(solution)/shard_map/ppermute | solution.py:440
  73.9 18.3 %collective-permute-start.4 = (bf16[1,4,384,128]{3,2,1,0:T(8,128)(2,1)S(1)}, bf16[1,4,384,128]{3,2,1,0:T(8,128)(2,1)S(1)}, u32[]{:S(2)}, u32[]{:S(2)}) collective-permute-start(bf16[1,4,384,128]{3,2,1,0:T(8,128)(2,1)S(1)} %copy-done.3), channel_id=1, source_target_pairs={{0,2},{1,3},{2,0},{3,1},{4,6},{5,7},{6,4},{7,5},{8,10},{9,11},{10,... | collective-permute-start | bytes 1179656 | tf_op jit(solution)/shard_map/ppermute | solution.py:428
  76.3 16.9 %collective-permute-start.5 = (bf16[1,4,384,128]{3,2,1,0:T(8,128)(2,1)S(1)}, bf16[1,4,384,128]{3,2,1,0:T(8,128)(2,1)S(1)}, u32[]{:S(2)}, u32[]{:S(2)}) collective-permute-start(bf16[1,4,384,128]{3,2,1,0:T(8,128)(2,1)S(1)} %copy-done.2), channel_id=1, source_target_pairs={{0,3},{1,2},{2,1},{3,0},{4,7},{5,6},{6,5},{7,4},{8,11},{9,10},{10,... | collective-permute-start | bytes 1179656 | tf_op jit(solution)/shard_map/ppermute | solution.py:428
  93.4 23.4 %collective-permute-start.15 = (bf16[1,4,768,128]{3,2,1,0:T(8,128)(2,1)S(1)}, bf16[1,4,768,128]{3,2,1,0:T(8,128)(2,1)S(1)}, u32[]{:S(2)}, u32[]{:S(2)}) collective-permute-start(bf16[1,4,768,128]{3,2,1,0:T(8,128)(2,1)S(1)} %get-tuple-element.92), channel_id=1, source_target_pairs={{0,4},{1,5},{4,8},{5,9},{6,2},{7,3},{8,12},{9,13},{10,6},{11,7},{1... | collective-permute-start | bytes 2359304 | tf_op jit(solution)/shard_map/ppermute | solution.py:440
  97.6 23.7 %collective-permute-start.14 = (bf16[1,4,768,128]{3,2,1,0:T(8,128)(2,1)S(1)}, bf16[1,4,768,128]{3,2,1,0:T(8,128)(2,1)S(1)}, u32[]{:S(2)}, u32[]{:S(2)}) collective-permute-start(bf16[1,4,768,128]{3,2,1,0:T(8,128)(2,1)S(1)} %get-tuple-element.91.refs_6_), channel_id=1, source_target_pairs={{2,6},{3,7},{4,0},{5,1},{6,10},{7,11},{8,4},{9,5},{10,14},{11,15},... | collective-permute-start | bytes 2359304 | tf_op jit(solution)/shard_map/ppermute | solution.py:440
  99.5 23.7 %collective-permute-start.18 = (bf16[1,6,384,128]{3,2,1,0:T(8,128)(2,1)S(1)}, bf16[1,6,384,128]{3,2,1,0:T(8,128)(2,1)S(1)}, u32[]{:S(2)}, u32[]{:S(2)}) collective-permute-start(bf16[1,6,384,128]{3,2,1,0:T(8,128)(2,1)S(1)} %get-tuple-element.101), channel_id=1, source_target_pairs={{0,1},{1,0},{2,3},{3,2},{4,5},{5,4},{6,7},{7,6},{8,9},{9,8},{10,11... | collective-permute-start | bytes 1769480 | tf_op jit(solution)/shard_map/ppermute | solution.py:428
  99.9 23.5 %collective-permute-start.19 = (bf16[1,6,384,128]{3,2,1,0:T(8,128)(2,1)S(1)}, bf16[1,6,384,128]{3,2,1,0:T(8,128)(2,1)S(1)}, u32[]{:S(2)}, u32[]{:S(2)}) collective-permute-start(bf16[1,6,384,128]{3,2,1,0:T(8,128)(2,1)S(1)} %get-tuple-element.102), channel_id=1, source_target_pairs={{0,2},{1,3},{2,0},{3,1},{4,6},{5,7},{6,4},{7,5},{8,10},{9,11},{10,... | collective-permute-start | bytes 1769480 | tf_op jit(solution)/shard_map/ppermute | solution.py:428
  101.0 26.3 %collective-permute-start.20 = (bf16[1,6,384,128]{3,2,1,0:T(8,128)(2,1)S(1)}, bf16[1,6,384,128]{3,2,1,0:T(8,128)(2,1)S(1)}, u32[]{:S(2)}, u32[]{:S(2)}) collective-permute-start(bf16[1,6,384,128]{3,2,1,0:T(8,128)(2,1)S(1)} %get-tuple-element.103), channel_id=1, source_target_pairs={{0,3},{1,2},{2,1},{3,0},{4,7},{5,6},{6,5},{7,4},{8,11},{9,10},{10,... | collective-permute-start | bytes 1769480 | tf_op jit(solution)/shard_map/ppermute | solution.py:428
  116.8 28.2 %collective-permute-start.21 = (bf16[2,2,384,128]{3,2,1,0:T(8,128)(2,1)S(1)}, bf16[2,2,384,128]{3,2,1,0:T(8,128)(2,1)S(1)}, u32[]{:S(2)}, u32[]{:S(2)}) collective-permute-start(bf16[2,2,384,128]{3,2,1,0:T(8,128)(2,1)S(1)} %get-tuple-element.106), channel_id=1, source_target_pairs={{0,4},{1,5},{4,8},{5,9},{6,2},{7,3},{8,12},{9,13},{10,6},{11,7},{1... | collective-permute-start | bytes 1179656 | tf_op jit(solution)/shard_map/ppermute | solution.py:440
  121.4 23.6 %collective-permute-start.22 = (bf16[2,2,384,128]{3,2,1,0:T(8,128)(2,1)S(1)}, bf16[2,2,384,128]{3,2,1,0:T(8,128)(2,1)S(1)}, u32[]{:S(2)}, u32[]{:S(2)}) collective-permute-start(bf16[2,2,384,128]{3,2,1,0:T(8,128)(2,1)S(1)} %get-tuple-element.107), channel_id=1, source_target_pairs={{2,6},{3,7},{4,0},{5,1},{6,10},{7,11},{8,4},{9,5},{10,14},{11,15},... | collective-permute-start | bytes 1179656 | tf_op jit(solution)/shard_map/ppermute | solution.py:440
  123.2 27.1 %collective-permute-start.28 = (bf16[1,4,384,128]{3,2,1,0:T(8,128)(2,1)S(1)}, bf16[1,4,384,128]{3,2,1,0:T(8,128)(2,1)S(1)}, u32[]{:S(2)}, u32[]{:S(2)}) collective-permute-start(bf16[1,4,384,128]{3,2,1,0:T(8,128)(2,1)S(1)} %get-tuple-element.115), channel_id=1, source_target_pairs={{0,1},{1,0},{2,3},{3,2},{4,5},{5,4},{6,7},{7,6},{8,9},{9,8},{10,11... | collective-permute-start | bytes 1179656 | tf_op jit(solution)/shard_map/ppermute | solution.py:428
  123.3 28.3 %collective-permute-start.29 = (bf16[1,4,384,128]{3,2,1,0:T(8,128)(2,1)S(1)}, bf16[1,4,384,128]{3,2,1,0:T(8,128)(2,1)S(1)}, u32[]{:S(2)}, u32[]{:S(2)}) collective-permute-start(bf16[1,4,384,128]{3,2,1,0:T(8,128)(2,1)S(1)} %get-tuple-element.116), channel_id=1, source_target_pairs={{0,2},{1,3},{2,0},{3,1},{4,6},{5,7},{6,4},{7,5},{8,10},{9,11},{10,... | collective-permute-start | bytes 1179656 | tf_op jit(solution)/shard_map/ppermute | solution.py:428
  127.4 24.3 %collective-permute-start.30 = (bf16[1,4,384,128]{3,2,1,0:T(8,128)(2,1)S(1)}, bf16[1,4,384,128]{3,2,1,0:T(8,128)(2,1)S(1)}, u32[]{:S(2)}, u32[]{:S(2)}) collective-permute-start(bf16[1,4,384,128]{3,2,1,0:T(8,128)(2,1)S(1)} %get-tuple-element.117), channel_id=1, source_target_pairs={{0,3},{1,2},{2,1},{3,0},{4,7},{5,6},{6,5},{7,4},{8,11},{9,10},{10,... | collective-permute-start | bytes 1179656 | tf_op jit(solution)/shard_map/ppermute | solution.py:428
  145.1 10.9 %collective-permute-start.24 = (bf16[1,4,384,128]{3,2,1,0:T(8,128)(2,1)S(1)}, bf16[1,4,384,128]{3,2,1,0:T(8,128)(2,1)S(1)}, u32[]{:S(2)}, u32[]{:S(2)}) collective-permute-start(bf16[1,4,384,128]{3,2,1,0:T(8,128)(2,1)S(1)} %get-tuple-element.110), channel_id=1, source_target_pairs={{0,2},{1,3},{2,0},{3,1},{4,6},{5,7},{6,4},{7,5},{8,10},{9,11},{10,... | collective-permute-start | bytes 1179656 | tf_op jit(solution)/shard_map/ppermute | solution.py:428
  146.0 12.0 %collective-permute-start.26 = (bf16[2,2,384,128]{3,2,1,0:T(8,128)(2,1)S(1)}, bf16[2,2,384,128]{3,2,1,0:T(8,128)(2,1)S(1)}, u32[]{:S(2)}, u32[]{:S(2)}) collective-permute-start(bf16[2,2,384,128]{3,2,1,0:T(8,128)(2,1)S(1)} %get-tuple-element.113), channel_id=1, source_target_pairs={{0,4},{1,5},{4,8},{5,9},{6,2},{7,3},{8,12},{9,13},{10,6},{11,7},{1... | collective-permute-start | bytes 1179656 | tf_op jit(solution)/shard_map/ppermute | solution.py:440
  150.3 11.8 %collective-permute-start.27 = (bf16[2,2,384,128]{3,2,1,0:T(8,128)(2,1)S(1)}, bf16[2,2,384,128]{3,2,1,0:T(8,128)(2,1)S(1)}, u32[]{:S(2)}, u32[]{:S(2)}) collective-permute-start(bf16[2,2,384,128]{3,2,1,0:T(8,128)(2,1)S(1)} %get-tuple-element.114), channel_id=1, source_target_pairs={{2,6},{3,7},{4,0},{5,1},{6,10},{7,11},{8,4},{9,5},{10,14},{11,15},... | collective-permute-start | bytes 1179656 | tf_op jit(solution)/shard_map/ppermute | solution.py:440
  151.6 17.5 %collective-permute-start.23 = (bf16[1,4,384,128]{3,2,1,0:T(8,128)(2,1)S(1)}, bf16[1,4,384,128]{3,2,1,0:T(8,128)(2,1)S(1)}, u32[]{:S(2)}, u32[]{:S(2)}) collective-permute-start(bf16[1,4,384,128]{3,2,1,0:T(8,128)(2,1)S(1)} %get-tuple-element.109), channel_id=1, source_target_pairs={{0,1},{1,0},{2,3},{3,2},{4,5},{5,4},{6,7},{7,6},{8,9},{9,8},{10,11... | collective-permute-start | bytes 1179656 | tf_op jit(solution)/shard_map/ppermute | solution.py:428
  151.7 17.4 %collective-permute-start.25 = (bf16[1,4,384,128]{3,2,1,0:T(8,128)(2,1)S(1)}, bf16[1,4,384,128]{3,2,1,0:T(8,128)(2,1)S(1)}, u32[]{:S(2)}, u32[]{:S(2)}) collective-permute-start(bf16[1,4,384,128]{3,2,1,0:T(8,128)(2,1)S(1)} %get-tuple-element.111), channel_id=1, source_target_pairs={{0,3},{1,2},{2,1},{3,0},{4,7},{5,6},{6,5},{7,4},{8,11},{9,10},{10,... | collective-permute-start | bytes 1179656 | tf_op jit(solution)/shard_map/ppermute | solution.py:428
  162.3 9.3 %collective-permute-start.31 = (bf16[1,2,384,128]{3,2,1,0:T(8,128)(2,1)S(1)}, bf16[1,2,384,128]{3,2,1,0:T(8,128)(2,1)S(1)}, u32[]{:S(2)}, u32[]{:S(2)}) collective-permute-start(bf16[1,2,384,128]{3,2,1,0:T(8,128)(2,1)S(1)} %get-tuple-element.119), channel_id=1, source_target_pairs={{0,1},{1,0},{2,3},{3,2},{4,5},{5,4},{6,7},{7,6},{8,9},{9,8},{10,11... | collective-permute-start | bytes 589832 | tf_op jit(solution)/shard_map/ppermute | solution.py:428
  162.4 9.2 %collective-permute-start.32 = (bf16[1,2,384,128]{3,2,1,0:T(8,128)(2,1)S(1)}, bf16[1,2,384,128]{3,2,1,0:T(8,128)(2,1)S(1)}, u32[]{:S(2)}, u32[]{:S(2)}) collective-permute-start(bf16[1,2,384,128]{3,2,1,0:T(8,128)(2,1)S(1)} %get-tuple-element.120), channel_id=1, source_target_pairs={{0,2},{1,3},{2,0},{3,1},{4,6},{5,7},{6,4},{7,5},{8,10},{9,11},{10,... | collective-permute-start | bytes 589832 | tf_op jit(solution)/shard_map/ppermute | solution.py:428
  162.5 11.0 %collective-permute-start.33 = (bf16[1,2,384,128]{3,2,1,0:T(8,128)(2,1)S(1)}, bf16[1,2,384,128]{3,2,1,0:T(8,128)(2,1)S(1)}, u32[]{:S(2)}, u32[]{:S(2)}) collective-permute-start(bf16[1,2,384,128]{3,2,1,0:T(8,128)(2,1)S(1)} %get-tuple-element.121), channel_id=1, source_target_pairs={{0,3},{1,2},{2,1},{3,0},{4,7},{5,6},{6,5},{7,4},{8,11},{9,10},{10,... | collective-permute-start | bytes 589832 | tf_op jit(solution)/shard_map/ppermute | solution.py:428
